TPU v7x, 32 devices: a whole 2x2x4 slice. The times are simulated.
32 devices in a mesh: groups: 2 (over y), wide: 8 (over z, x), narrow: 2 (over core).
Axes of the slice: x: 2, y: 2, z: 4, core: 2. Of those that a mesh axis runs over, the one named last changes fastest.
Arguments:
- traces: bfloat16 [256, 4096, 256], P(None, ('groups', 'wide'), 'narrow'), parts along dimension 1, may hold values from -6 to 6
- row_counts: int32 [16, 16], P(('groups', 'wide')), parts along dimension 0, may hold values from 1 to 8, as said below
- tile_cols: int32 [16, 80], P(('groups', 'wide')), parts along dimension 0, may hold values from 0 to 15, as said below
- tiles: bfloat16 [16, 80, 2, 128, 128], P(('groups', 'wide'), 'narrow'), parts along dimension 0, may hold values from -0.15625 to 0.15625
Outputs:
- redatumed_traces: bfloat16 [256, 4096, 256], P(None, ('groups', 'wide'), 'narrow'), parts along dimension 1
There are 2 independent parts, one for each index of `groups`. A program takes and returns all parts, laid end to end along the dimension named above; each array names one. Nothing has to cross between parts.
Inputs may be any that keep to these rules, and one draw needn't show every extreme that they name: `row_counts`: for each frequency the 16 counts sum to at most 80, and to exactly 80 for at least one frequency; every frequency has a row with 8. A frequency's kept tiles fill its first slots, the rows one after another in order. `tile_cols`: the live slots of one tile row name different tile columns; slots past a frequency's total are not read.
All inputs are finite; a program needn't handle non-finite values.
Results may differ from a plain program's by a relative error of at most 0.012.
Values may be sent and summed in bfloat16 or wider, within the bound.
No kernel may reach another device: no remote copies, remote signals or barrier semaphores. Data moves between devices by JAX's collectives and lax.ppermute only.
A program may use at most 128 MiB of HBM per device.

v0:
```python
import math

import jax
import jax.numpy as jnp
from jax import lax
from jax.sharding import PartitionSpec as P


def transform_tables(samples, frequencies):
    sample_ids = jnp.arange(samples, dtype=jnp.int32)
    freq_ids = 1 + jnp.arange(frequencies, dtype=jnp.int32)
    turn_index = freq_ids[:, None] * sample_ids[None, :] % samples
    phases = turn_index.astype(jnp.float32) * (2.0 * math.pi / samples)
    norm_scale = samples ** (-0.5)
    cosine = jnp.cos(phases)
    sine_part = jnp.sin(phases)
    forward = (jnp.stack([cosine, -sine_part], axis=1) * norm_scale).astype(jnp.bfloat16)
    inverse = (
        (jnp.stack([cosine, -sine_part], axis=2) * (2.0 * norm_scale))
        .transpose(1, 0, 2)
        .astype(jnp.bfloat16)
    )
    return (forward, inverse)


def row_weights(row_ends, slot_ids, row_total):
    slot_rows = jnp.sum((row_ends[None, :] <= slot_ids[:, None]).astype(jnp.int32), axis=1)
    alive = slot_ids < row_ends[-1]
    slot_rows = jnp.minimum(slot_rows, row_total - 1)
    match = (slot_rows[:, None] == jnp.arange(row_total, dtype=jnp.int32)[None, :]) & alive[:, None]
    return match.astype(jnp.float32)


def accumulate(spectrum, counts, columns, kernel, first_id):
    slot_count = kernel.shape[0]
    tile_size = kernel.shape[-1]
    width_cols = spectrum.shape[-1]
    row_total = counts.shape[0]
    blocks = spectrum.reshape(2, row_total, tile_size, width_cols)
    row_ends = jnp.cumsum(counts)
    slot_block = 8
    initial = jnp.zeros((2, row_total, tile_size, width_cols), jnp.float32)

    def add_block(block_index, running):
        first_slot = block_index * slot_block
        kernel_block = lax.dynamic_slice_in_dim(kernel, first_slot, slot_block, 0)
        column_ids = lax.dynamic_slice_in_dim(columns, first_slot, slot_block, 0)
        slot_ids = first_id + first_slot + jnp.arange(slot_block, dtype=jnp.int32)
        weights = row_weights(row_ends, slot_ids, row_total)
        picked = jnp.take(blocks, column_ids, axis=1)
        products = jnp.einsum(
            "kcij,dkjv->cdkiv", kernel_block, picked, preferred_element_type=jnp.float32
        )
        real_part = products[0, 0] - products[1, 1]
        imag_part = products[0, 1] + products[1, 0]
        slot_terms = jnp.stack([real_part, imag_part], axis=0)
        return running + jnp.einsum("kr,ckiv->criv", weights, slot_terms)

    block_turns = slot_count // slot_block
    running = lax.fori_loop(0, block_turns, add_block, initial)
    return running.reshape(2, -1, width_cols)


def shards(traces, row_counts, tile_cols, tiles):
    samples = traces.shape[0]
    frequencies = lax.axis_size("wide") * row_counts.shape[0]
    forward, inverse = transform_tables(samples, frequencies)
    spectra = jnp.einsum(
        "fct,trv->fcrv", forward, traces, preferred_element_type=jnp.float32
    ).astype(jnp.bfloat16)
    halves = tiles.shape[1]
    counts = row_counts[0]
    position = lax.axis_index("narrow")
    own_start = position * halves
    own_cols = lax.dynamic_slice_in_dim(tile_cols[0], own_start, halves, 0)
    own_tiles = tiles[0]
    spectrum = lax.all_to_all(spectra, "wide", split_axis=0, concat_axis=2, tiled=True)[0]
    gathered = lax.all_gather(spectrum, "narrow", axis=2, tiled=True)
    partial_term = accumulate(gathered, counts, own_cols, own_tiles, own_start)
    summed = lax.psum_scatter(
        partial_term.astype(jnp.bfloat16), "narrow", scatter_dimension=2, tiled=True
    )
    synthesis = lax.all_to_all(summed[None], "wide", split_axis=2, concat_axis=0, tiled=True)
    redatumed = jnp.einsum("tfc,fcrv->trv", inverse, synthesis, preferred_element_type=jnp.float32)
    return redatumed.astype(jnp.bfloat16)


def solution(mesh):
    in_specs = (
        P(None, ("groups", "wide"), "narrow"),
        P(("groups", "wide"), None),
        P(("groups", "wide"), None),
        P(("groups", "wide"), "narrow", None, None, None),
    )
    out_specs = P(None, ("groups", "wide"), "narrow")
    return jax.shard_map(shards, mesh=mesh, in_specs=in_specs, out_specs=out_specs, check_vma=False)
```

profile of v0, /device:TPU:0, one launch (start us, length us, event | category | flops | bytes accessed | tf_op | source)
XLA Modules:
  0.0 223.3 jit_solution(7081785622035317087)
XLA Ops:
  6.7 14.6 %fusion.19 = bf16[8,2,256,128]{3,0,2,1:T(8,128)(2,1)S(1)} fusion(bf16[256,256,128]{2,1,0:T(8,128)(2,1)} %param.6, f32[8,1,256]{2,0,1:T(8,128)S(1)} %get-tuple-element.173, f32[8,1,256]{2,0,1:T(8,128)S(1)} %get-tuple-element.172), kind=kOutput, calls=%fused_computation.35 | convolution fusion | flops 268972032 | bytes 17842176 | tf_op jit(solution)/shard_map/fct,trv->fcrv/dot_general | solution.py:68
  21.5 32.8 %all_to_all.33 = bf16[8,2,256,128]{3,2,1,0:T(8,128)(2,1)S(1)} all-to-all(bf16[8,2,256,128]{3,2,1,0:T(8,128)(2,1)S(1)} %copy.40), channel_id=1, replica_groups=mesh['groups'=2,'wide'=8,'narrow'=2] {'wide'}, dimensions={0} | all-to-all | bytes 2097152 | tf_op jit(solution)/shard_map/all_to_all | solution.py:77
  54.3 1.1 copy.41
  56.0 8.9 %all-gather.2.cloned.1.call-done = bf16[2,2048,256]{2,1,0:T(8,128)(2,1)} async-done(((bf16[2,2048,128]{2,1,0:T(8,128)(2,1)}), bf16[2,2048,256]{2,1,0:T(8,128)(2,1)}) %all-gather.2.cloned.1.call-update) | async-done | bytes 2097168 | tf_op jit(solution)/shard_map/all_gather | solution.py:78
  64.9 58.5 %while.14 = (s32[]{:T(128)}, f32[2,16,128,256]{3,1,2,0:T(8,128)}, s32[40]{0:T(128)S(1)}, bf16[2,16,128,256]{3,2,1,0:T(8,128)(2,1)}, bf16[40,2,128,128]{3,2,1,0:T...) while((s32[]{:T(128)}, f32[2,16,128,256]{3,1,2,0:T(8,128)}, ...), condition=%wide.region_3.4_spmd.clone, body=%wide.region_1.3_spmd.clone.sunk | while | flops 289408704 | bytes 26743412 | solution.py:60
  66.5 2.2 gather_fusion
  68.7 2.0 convolution_bitcast_fusion.2
  72.0 2.9 %bitcast_add_fusion.2 = f32[2,16,128,256]{3,1,2,0:T(8,128)} fusion(f32[2,16,128,256]{3,1,2,0:T(8,128)} %get-tuple-element.233, bf16[2,8,128,256]{3,1,2,0:T(8,128)(2,1)S(1)} %copy.75, pred[]{:T(512)S(6)} %compare.23, s32[8]{0:T(128)S(1)} %broadcast_minimum_fusion.2, pred[8]{0:T(512)(128)(4,1)S(1)} %broadcast_compare_fusion.2), kind=kOutput, calls=%fused_computation.1.clone.1 | convolution fusion | flops 18874624 | bytes 9437225 | tf_op jit(solution)/shard_map/while/body/eval_jaxpr/kr,ckiv->criv/dot_general | solution.py:57
  76.4 2.2 gather_fusion
  78.6 2.0 convolution_bitcast_fusion.2
  81.0 0.9 copy.75
  81.9 5.1 %bitcast_add_fusion.2 = f32[2,16,128,256]{3,1,2,0:T(8,128)} fusion(f32[2,16,128,256]{3,1,2,0:T(8,128)} %get-tuple-element.233, bf16[2,8,128,256]{3,1,2,0:T(8,128)(2,1)S(1)} %copy.75, pred[]{:T(512)S(6)} %compare.23, s32[8]{0:T(128)S(1)} %broadcast_minimum_fusion.2, pred[8]{0:T(512)(128)(4,1)S(1)} %broadcast_compare_fusion.2), kind=kOutput, calls=%fused_computation.1.clone.1 | convolution fusion | flops 18874624 | bytes 9437225 | tf_op jit(solution)/shard_map/while/body/eval_jaxpr/kr,ckiv->criv/dot_general | solution.py:57
  88.6 2.2 gather_fusion
  90.8 2.0 convolution_bitcast_fusion.2
  94.1 5.1 %bitcast_add_fusion.2 = f32[2,16,128,256]{3,1,2,0:T(8,128)} fusion(f32[2,16,128,256]{3,1,2,0:T(8,128)} %get-tuple-element.233, bf16[2,8,128,256]{3,1,2,0:T(8,128)(2,1)S(1)} %copy.75, pred[]{:T(512)S(6)} %compare.23, s32[8]{0:T(128)S(1)} %broadcast_minimum_fusion.2, pred[8]{0:T(512)(128)(4,1)S(1)} %broadcast_compare_fusion.2), kind=kOutput, calls=%fused_computation.1.clone.1 | convolution fusion | flops 18874624 | bytes 9437225 | tf_op jit(solution)/shard_map/while/body/eval_jaxpr/kr,ckiv->criv/dot_general | solution.py:57
  100.7 2.2 gather_fusion
  102.9 2.0 convolution_bitcast_fusion.2
  106.2 5.1 %bitcast_add_fusion.2 = f32[2,16,128,256]{3,1,2,0:T(8,128)} fusion(f32[2,16,128,256]{3,1,2,0:T(8,128)} %get-tuple-element.233, bf16[2,8,128,256]{3,1,2,0:T(8,128)(2,1)S(1)} %copy.75, pred[]{:T(512)S(6)} %compare.23, s32[8]{0:T(128)S(1)} %broadcast_minimum_fusion.2, pred[8]{0:T(512)(128)(4,1)S(1)} %broadcast_compare_fusion.2), kind=kOutput, calls=%fused_computation.1.clone.1 | convolution fusion | flops 18874624 | bytes 9437225 | tf_op jit(solution)/shard_map/while/body/eval_jaxpr/kr,ckiv->criv/dot_general | solution.py:57
  112.8 2.2 gather_fusion
  115.1 2.0 convolution_bitcast_fusion.2
  118.3 5.1 %bitcast_add_fusion.2 = f32[2,16,128,256]{3,1,2,0:T(8,128)} fusion(f32[2,16,128,256]{3,1,2,0:T(8,128)} %get-tuple-element.233, bf16[2,8,128,256]{3,1,2,0:T(8,128)(2,1)S(1)} %copy.75, pred[]{:T(512)S(6)} %compare.23, s32[8]{0:T(128)S(1)} %broadcast_minimum_fusion.2, pred[8]{0:T(512)(128)(4,1)S(1)} %broadcast_compare_fusion.2), kind=kOutput, calls=%fused_computation.1.clone.1 | convolution fusion | flops 18874624 | bytes 9437225 | tf_op jit(solution)/shard_map/while/body/eval_jaxpr/kr,ckiv->criv/dot_general | solution.py:57
  123.4 4.4 %copy.73 = bf16[2,16,128,256]{3,2,1,0:T(8,128)(2,1)S(1)} copy(f32[2,16,128,256]{3,1,2,0:T(8,128)} %get-tuple-element.129) | data formatting | bytes 6291456 | tf_op jit(solution)/shard_map/while | solution.py:60
  127.8 3.9 %copy.57 = bf16[2,2048,256]{1,0,2:T(2,128)(2,1)} copy(bf16[2,2048,256]{2,1,0:T(8,128)(2,1)S(1)} %bitcast.100) | data formatting | bytes 4194304
  131.8 3.8 %copy.61 = bf16[32,8,2,2048]{3,1,2,0:T(8,128)(2,1)} copy(bf16[32,8,2,2048]{3,2,1,0:T(2,128)(2,1)} %bitcast.102) | data formatting | bytes 4194304
  135.6 10.9 %reduce-scatter.4.cloned.1.call-done = bf16[128,4096]{1,0:T(8,128)(2,1)} async-done(((bf16[256,4096]{1,0:T(8,128)(2,1)}), bf16[128,4096]{1,0:T(8,128)(2,1)}) %reduce-scatter.4.cloned.1.call-update) | async-done | bytes 1048592
  146.6 1.8 reshape.320
  148.4 1.0 copy.58
  149.5 9.5 %copy.44 = bf16[1,2,2048,128]{3,1,0,2:T(2,128)(2,1)} copy(bf16[1,2,2048,128]{3,2,1,0:T(8,128)(2,1)S(1)} %bitcast.106) | data formatting | bytes 2097152 | tf_op jit(solution)/shard_map/broadcast_in_dim | solution.py:83
  158.9 5.8 %all-to-all-start.1 = ((bf16[1,2,2048,128]{3,1,0,2:T(2,128)(2,1)}), bf16[1,2,2048,128]{3,1,0,2:T(2,128)(2,1)S(1)}, u32[]{:S(2)}, u32[]{:S(2)}) async-start(bf16[1,2,2048,128]{3,1,0,2:T(2,128)(2,1)} %copy.44), calls=%async_computation.1 | async-start | bytes 2097152 | tf_op jit(solution)/shard_map/all_to_all | solution.py:83
  164.8 26.1 %all-to-all-done.1 = bf16[1,2,2048,128]{3,1,0,2:T(2,128)(2,1)S(1)} async-done(((bf16[1,2,2048,128]{3,1,0,2:T(2,128)(2,1)}), bf16[1,2,2048,128]{3,1,0,2:T(2,128)(2,1)S(1)}, u32[]{:S(2)}, u32[]{:S(2)}) %all-to-all-start.1) | async-done | bytes 1048608 | tf_op jit(solution)/shard_map/all_to_all | solution.py:83
  190.9 8.1 %bitcast_convert_fusion = bf16[256,256,128]{2,0,1:T(8,128)(2,1)} fusion(bf16[1,2,8,256,128]{4,1,3,2,0:T(2,128)(2,1)S(1)} %bitcast.103, f32[8,256,1]{1,0,2:T(8,128)S(1)} %get-tuple-element.171, f32[8,256,1]{1,0,2:T(8,128)S(1)} %get-tuple-element.170), kind=kOutput, calls=%fused_computation.30 | convolution fusion | flops 276836352 | bytes 17842176 | tf_op jit(solution)/shard_map/tfc,fcrv->trv/dot_general | solution.py:84
  199.0 17.4 %copy.47 = bf16[256,256,128]{2,1,0:T(8,128)(2,1)} copy(bf16[256,256,128]{2,0,1:T(8,128)(2,1)} %bitcast_convert_fusion) | data formatting | bytes 33554432 | tf_op jit(solution)/shard_map/convert_element_type | solution.py:85
  (73 shorter events, 13.9 us)
Async XLA Ops:
  6.5 49.4 %copy-start = (s32[1,80]{1,0:T(1,128)S(1)}, s32[1,80]{1,0:T(1,128)}, u32[]{:S(2)}) copy-start(s32[1,80]{1,0:T(1,128)} %param.8) | copy-start | bytes 964
  6.5 58.4 %all-gather.2.cloned.1.call-start = ((), (), s32[]{:S(2)}) async-start(), calls=%async_computation.3 | async-start | bytes 3145728 | tf_op jit(solution)/shard_map/all_gather | solution.py:78
  21.3 34.4 %copy-start.2 = (s32[1,16]{1,0:T(1,128)S(1)}, s32[1,16]{1,0:T(1,128)}, u32[]{:S(2)}) copy-start(s32[1,16]{1,0:T(1,128)} %param.7) | copy-start | bytes 196
  55.4 91.2 %reduce-scatter.4.cloned.1.call-start = ((), (), s32[]{:S(2)}) async-start(), calls=%async_computation.4 | async-start | bytes 3145728
  158.9 32.0 %all-to-all-start.1 = ((bf16[1,2,2048,128]{3,1,0,2:T(2,128)(2,1)}), bf16[1,2,2048,128]{3,1,0,2:T(2,128)(2,1)S(1)}, u32[]{:S(2)}, u32[]{:S(2)}) async-start(bf16[1,2,2048,128]{3,1,0,2:T(2,128)(2,1)} %copy.44), calls=%async_computation.1 | async-start | bytes 2097152 | tf_op jit(solution)/shard_map/all_to_all | solution.py:83
  199.0 17.4 %copy-start.1 = (s32[1,80]{1,0:T(1,128)S(1)}, s32[1,80]{1,0:T(1,128)}, u32[]{:S(2)}) copy-start(s32[1,80]{1,0:T(1,128)} %param.8) | copy-start | bytes 964
Sparse Core Ops, SparseCore 0:
  55.5 9.3 all-gather.1
  135.7 10.7 reduce-scatter.3
where the time goes:
time: 224 us; the launch traced here: 223 us
  local copies, waits for them, and re-layouts  62.1 us (28%)
  matrix products  56.1 us (25%)
  waiting for transfers between devices  46 us (21%)
  blocking collectives  32.8 us (15%)
  between operations  13.5 us (6%)
  other arithmetic  6.5 us (3%)
  starting transfers between devices  6 us (3%)
    all_to_all x1, blocking collectives, shards(): lax.all_to_all(spectra, 'wide', split_axis=0, concat_axis=2, tiled=True)[0]  32.8 us
    all_to_all x1, waiting for transfers between devices, shards(): lax.all_to_all(summed[None], 'wide', split_axis=2, concat_axis=0, tiled=T...  26.1 us
    dot_general x5, matrix products, add_block(): return running + jnp.einsum('kr,ckiv->criv', weights, slot_terms)  23.2 us
    convert_element_type x1, local copies, waits for them, and re-layouts, shards(): return redatumed.astype(jnp.bfloat16)  17.4 us
    dot_general x1, matrix products, shards(): jnp.einsum('fct,trv->fcrv', forward, traces, preferred_element_type=jnp.f...  14.6 us
    gather x5, local copies, waits for them, and re-layouts, add_block(): picked = jnp.take(blocks, column_ids, axis=1)  11 us
    unnamed x3, waiting for transfers between devices  11 us
    unnamed x10, local copies, waits for them, and re-layouts  10.6 us
  transfers between devices with their start and end apart: 3, of which 3 were waited for; matrix products, arithmetic and copies ran while one was open for 0% of the time, Pallas kernels for 0%

commit v1 on v0

v1 whole, which is shorter than its diff:
```python
import functools
import math

import jax
import jax.numpy as jnp
import numpy as np
from jax import lax
from jax.experimental import pallas as pl
from jax.experimental.pallas import tpu as pltpu
from jax.sharding import PartitionSpec as P

BF16 = jnp.bfloat16
F32 = jnp.float32
SUB = 16


def transform_tables(samples, frequencies):
    turns = (1 + np.arange(frequencies))[:, None] * np.arange(samples)[None, :] % samples
    phases = turns * (2.0 * math.pi / samples)
    both = np.stack([np.cos(phases), -np.sin(phases)], axis=1) * samples**-0.5
    small = both.astype(jnp.bfloat16)
    twice = (2.0 * both).astype(jnp.bfloat16)
    forward = np.zeros((frequencies, 2, SUB, samples, SUB), jnp.bfloat16)
    inverse = np.zeros((samples, SUB, frequencies, 2, SUB), jnp.bfloat16)
    for r in range(SUB):
        forward[:, :, r, :, r] = small
        inverse[:, r, :, :, r] = twice.transpose(2, 0, 1)
    return (
        forward.reshape(frequencies, 2 * SUB, samples * SUB),
        inverse.reshape(samples * SUB, frequencies * 2 * SUB),
    )


def params(**kwargs):
    return pltpu.CompilerParams(vmem_limit_bytes=56 * 2**20, **kwargs)


def forward_kernel(group, blocks, me_ref, table_ref, traces_ref, *out_refs):
    samples, _, width = traces_ref.shape
    me = me_ref[0]
    columns = jnp.concatenate(
        [
            traces_ref[:, SUB * b : SUB * (b + 1), :].reshape(samples * SUB, width)
            for b in range(blocks)
        ],
        axis=1,
    )
    for first in range(0, len(out_refs), group):
        table = jnp.concatenate([table_ref[me ^ s] for s in range(first, first + group)], axis=0)
        found = jnp.dot(table, columns, preferred_element_type=F32).astype(BF16)
        for s in range(group):
            for c in range(2):
                for b in range(blocks):
                    row = (2 * s + c) * SUB
                    out_refs[first + s][c, SUB * b : SUB * (b + 1), :] = found[
                        row : row + SUB, width * b : width * (b + 1)
                    ]


def forward(me, table, traces, first, count):
    samples, _, width = traces.shape
    parties = table.shape[0]
    step = min(2 * SUB, count)
    return pl.pallas_call(
        functools.partial(forward_kernel, min(8, parties), step // SUB),
        grid_spec=pltpu.PrefetchScalarGridSpec(
            num_scalar_prefetch=1,
            grid=(count // step,),
            in_specs=[
                pl.BlockSpec(table.shape, lambda i, _: (0, 0, 0), pipeline_mode=pl.Buffered(1)),
                pl.BlockSpec((samples, step, width), lambda i, _: (0, first // step + i, 0)),
            ],
            out_specs=[pl.BlockSpec((2, step, width), lambda i, _: (0, i, 0))] * parties,
        ),
        out_shape=[jax.ShapeDtypeStruct((2, count, width), BF16)] * parties,
        compiler_params=params(),
        cost_estimate=pl.CostEstimate(
            flops=2 * parties * 32 * samples * SUB * width * count // SUB,
            bytes_accessed=2 * samples * count * width,
            transcendentals=0,
        ),
        name="forward",
    )(me, table, traces)


def tiles_kernel(parties, taken, given, slot_ref, own_ref, other_ref, *refs):
    in_refs = refs[: parties * len(taken)]
    out_refs = refs[parties * len(taken) : parties * (len(taken) + len(given))]
    top_ref, low_ref, sum_ref = refs[-3:]
    step = pl.program_id(0)
    block, _, size, _ = own_ref.shape
    width = in_refs[0].shape[-1]
    rows = sum(count for _, count in taken)
    me = slot_ref[2, 0]

    @pl.when(step == 0)
    def _():
        for q, (first, count) in enumerate(taken):
            for s in range(parties):
                ref = in_refs[q * parties + s]
                place = pl.ds(pl.multiple_of((me ^ s) * rows + first, SUB), count)
                top_ref[place, :width] = ref[0]
                top_ref[place, width:] = ref[1]
                low_ref[place, :width] = -ref[1]
                low_ref[place, width:] = ref[0]
        sum_ref[...] = jnp.zeros_like(sum_ref)

    for k in range(block):
        for which, ref in ((0, own_ref), (1, other_ref)):
            slot = step * block + k
            target = slot_ref[which, slot]
            column = slot_ref[3 + which, slot]
            place = pl.ds(pl.multiple_of(column * size, size), size)
            pair = jnp.concatenate([ref[k, 0], ref[k, 1]], axis=1)
            weights = jnp.concatenate([top_ref[place, :], low_ref[place, :]], axis=0)
            spot = pl.ds(pl.multiple_of(target * size, size), size)
            sum_ref[spot, :] += jnp.dot(pair, weights, preferred_element_type=F32)

    @pl.when(step == pl.num_programs(0) - 1)
    def _():
        for q, (first, count) in enumerate(given):
            for s in range(parties):
                place = pl.ds(pl.multiple_of((me ^ s) * rows + first, SUB), count)
                ref = out_refs[q * parties + s]
                ref[0] = sum_ref[place, :width].astype(BF16)
                ref[1] = sum_ref[place, width:].astype(BF16)


def apply_tiles(slots, own, other, spectra, taken, given):
    parties = len(spectra) // len(taken)
    halves, _, size, _ = own.shape
    width = spectra[0].shape[-1]
    total = parties * sum(count for _, count in taken)
    block = math.gcd(8, halves)
    whole = lambda i, _: (0, 0, 0)
    return pl.pallas_call(
        functools.partial(tiles_kernel, parties, taken, given),
        grid_spec=pltpu.PrefetchScalarGridSpec(
            num_scalar_prefetch=1,
            grid=(halves // block,),
            in_specs=[pl.BlockSpec((block, 2, size, size), lambda i, _: (i, 0, 0, 0))] * 2
            + [pl.BlockSpec(a.shape, whole, pipeline_mode=pl.Buffered(1)) for a in spectra],
            out_specs=[
                pl.BlockSpec((2, count, width), whole)
                for _, count in given
                for _ in range(parties)
            ],
            scratch_shapes=[
                pltpu.VMEM((total, 2 * width), BF16),
                pltpu.VMEM((total, 2 * width), BF16),
                pltpu.VMEM((total + size, 2 * width), F32),
            ],
        ),
        out_shape=[
            jax.ShapeDtypeStruct((2, count, width), BF16)
            for _, count in given
            for _ in range(parties)
        ],
        compiler_params=params(),
        cost_estimate=pl.CostEstimate(
            flops=2 * 2 * halves * size * 4 * size * width,
            bytes_accessed=4 * own.size,
            transcendentals=0,
        ),
        name="tiles",
    )(slots, own, other, *spectra)


def inverse_kernel(parties, blocks, me_ref, table_ref, *refs):
    in_refs = refs[:parties]
    out_ref, held_ref = refs[-2:]
    samples, _, width = out_ref.shape
    me = me_ref[0]

    @pl.when(pl.program_id(1) == 0)
    def _():
        for s in range(parties):
            for c in range(2):
                for b in range(blocks):
                    held_ref[me ^ s, SUB * c : SUB * (c + 1), width * b : width * (b + 1)] = (
                        in_refs[s][c, SUB * b : SUB * (b + 1), :]
                    )

    found = jnp.dot(
        table_ref[...],
        held_ref[...].reshape(parties * 2 * SUB, blocks * width),
        preferred_element_type=F32,
    ).astype(BF16)
    for b in range(blocks):
        out_ref[:, SUB * b : SUB * (b + 1), :] = found[:, width * b : width * (b + 1)].reshape(
            samples, SUB, width
        )


def inverse(me, table, redatumed, first, rows, filled):
    parties = len(redatumed)
    _, count, width = redatumed[0].shape
    samples = table.shape[0] // SUB
    step = min(2 * SUB, count)
    parts = 4
    extra = [] if filled is None else [filled]

    def kernel(me_ref, table_ref, *refs):
        refs = refs if filled is None else refs[:parties] + refs[parties + 1 :]
        inverse_kernel(parties, step // SUB, me_ref, table_ref, *refs)

    return pl.pallas_call(
        kernel,
        grid_spec=pltpu.PrefetchScalarGridSpec(
            num_scalar_prefetch=1,
            grid=(count // step, parts),
            in_specs=[pl.BlockSpec((samples // parts * SUB, table.shape[1]), lambda i, j, _: (j, 0))]
            + [pl.BlockSpec((2, step, width), lambda i, j, _: (0, i, 0))] * parties
            + [pl.BlockSpec(memory_space=pl.ANY)] * len(extra),
            out_specs=pl.BlockSpec(
                (samples // parts, step, width), lambda i, j, _: (j, first // step + i, 0)
            ),
            scratch_shapes=[pltpu.VMEM((parties, 2 * SUB, step // SUB * width), BF16)],
        ),
        out_shape=jax.ShapeDtypeStruct((samples, rows, width), BF16),
        input_output_aliases={} if filled is None else {2 + parties: 0},
        compiler_params=params(),
        cost_estimate=pl.CostEstimate(
            flops=2 * parties * 32 * samples * SUB * width * count // SUB,
            bytes_accessed=2 * samples * count * width,
            transcendentals=0,
        ),
        name="inverse",
    )(me, table, *redatumed, *extra)


def exchange(blocks):
    parties = len(blocks)
    got = [blocks[0]]
    for s in range(1, parties):
        pairs = [(k, k ^ s) for k in range(parties)]
        got.append(lax.ppermute(blocks[s], "wide", pairs))
    return got


def cuts(rows, sizes):
    if rows % (sum(sizes) * 2 * SUB):
        return ((0, rows),)
    unit = rows // sum(sizes)
    return tuple((unit * sum(sizes[:i]), unit * n) for i, n in enumerate(sizes))


def shards(traces, row_counts, tile_cols, tiles):
    samples, rows, _ = traces.shape
    parties = lax.axis_size("wide")
    halves = tiles.shape[1]
    forward_table, inverse_table = transform_tables(samples, parties)
    me = lax.axis_index("wide").astype(jnp.int32)
    side = lax.axis_index("narrow").astype(jnp.int32)
    taken = cuts(rows, (1, 3))
    given = cuts(rows, (3, 1))

    other = lax.ppermute(tiles[0], "narrow", [(0, 1), (1, 0)])
    ends = jnp.cumsum(row_counts[0])
    slot_ids = jnp.arange(2 * halves, dtype=jnp.int32)
    slot_rows = jnp.sum((ends[None, :] <= slot_ids[:, None]).astype(jnp.int32), axis=1)
    columns = jnp.clip(tile_cols[0], 0, row_counts.shape[1] - 1)
    turn = lambda a: jnp.where(side == 0, a.reshape(2, halves), a.reshape(2, halves)[::-1])
    slots = jnp.concatenate(
        [turn(slot_rows), jnp.full((1, halves), me, jnp.int32), turn(columns)], axis=0
    )

    place = me.reshape(1)
    spectra = []
    for first, count in taken:
        spectra += exchange(forward(place, forward_table, traces, first, count))
    redatumed = apply_tiles(slots, tiles[0], other, spectra, taken, given)
    result = None
    for q, (first, _) in enumerate(given):
        blocks = exchange(redatumed[q * parties : (q + 1) * parties])
        result = inverse(place, inverse_table, blocks, first, rows, result)
    return result


def solution(mesh):
    in_specs = (
        P(None, ("groups", "wide"), "narrow"),
        P(("groups", "wide"), None),
        P(("groups", "wide"), None),
        P(("groups", "wide"), "narrow", None, None, None),
    )
    out_specs = P(None, ("groups", "wide"), "narrow")
    return jax.shard_map(shards, mesh=mesh, in_specs=in_specs, out_specs=out_specs, check_vma=False)
```

time: 224 us -> 119 us (0.53)
  local copies, waits for them, and re-layouts: 62.1 us -> 2.52 us
  matrix products: 56.1 us -> 0 us
  Pallas kernels: 0 us -> 49.8 us
  starting transfers between devices: 6 us -> 44.4 us
  blocking collectives: 32.8 us -> 0 us
  waiting for transfers between devices: 46 us -> 20 us
  between operations: 13.5 us -> 0.37 us
  other arithmetic: 6.5 us -> 0.92 us
    dot_general x12 -> x0, matrix products: 56.1 us -> none  [the longest x5 23.2 us: add_block(): return running + jnp.einsum('kr,ckiv->criv', weights, slot_terms)]
    pallas_call x0 -> x5, Pallas kernels: none -> 49.8 us  [the longest x2 27.9 us: inverse(): pl.pallas_call(kernel, grid_spec=pltpu.PrefetchScalarGridSpec(num_scalar_...]
    ppermute x0 -> x29, starting transfers between devices: none -> 44.4 us  [the longest x28 43.9 us: exchange(): got.append(lax.ppermute(blocks[s], 'wide', pairs))]
    all_to_all x1 -> x0, blocking collectives: 32.8 us -> none  [shards(): lax.all_to_all(spectra, 'wide', split_axis=0, concat_axis=2, tiled=True)[0]]
    all_to_all x1 -> x0, waiting for transfers between devices: 26.1 us -> none  [shards(): lax.all_to_all(summed[None], 'wide', split_axis=2, concat_axis=0, tiled=T...]
    ppermute x0 -> x29, waiting for transfers between devices: none -> 20 us  [the longest x28 20 us: exchange(): got.append(lax.ppermute(blocks[s], 'wide', pairs))]
    convert_element_type x2 -> x0, local copies, waits for them, and re-layouts: 17.6 us -> none  [the longest x1 17.4 us: shards(): return redatumed.astype(jnp.bfloat16)]
    gather x5 -> x0, local copies, waits for them, and re-layouts: 11 us -> none  [add_block(): picked = jnp.take(blocks, column_ids, axis=1)]
  transfers between devices with their start and end apart: 3 -> 29, of which waited for: 3 -> 7; matrix products, arithmetic and copies ran while one was open for 0% -> 1% of each run, Pallas kernels for 0% -> 29%
where the time goes in v1:
time: 119 us; the launch traced here: 118 us
  Pallas kernels  49.8 us (42%)
  starting transfers between devices  44.4 us (37%)
  waiting for transfers between devices  20 us (17%)
  local copies, waits for them, and re-layouts  2.52 us (2%)
    ppermute x28, starting transfers between devices, exchange(): got.append(lax.ppermute(blocks[s], 'wide', pairs))  43.9 us
    pallas_call x2, Pallas kernels, inverse(): pl.pallas_call(kernel, grid_spec=pltpu.PrefetchScalarGridSpec(num_scalar_...  27.9 us
    ppermute x28, waiting for transfers between devices, exchange(): got.append(lax.ppermute(blocks[s], 'wide', pairs))  20 us
    pallas_call x2, Pallas kernels, forward(): pl.pallas_call(functools.partial(forward_kernel, min(8, parties), step //...  14 us
    pallas_call x1, Pallas kernels, apply_tiles(): pl.pallas_call(functools.partial(tiles_kernel, parties, taken, given), gr...  8.01 us
  transfers between devices with their start and end apart: 29, of which 7 were waited for; matrix products, arithmetic and copies ran while one was open for 1% of the time, Pallas kernels for 29%

profile of v1, /device:TPU:0, one launch (start us, length us, event | category | flops | bytes accessed | tf_op | source)
XLA Modules:
  0.0 118.0 jit_solution(13124252914043214989)
XLA Ops:
  0.5 4.4 %forward.2 = (bf16[2,64,128]{2,1,0:T(8,128)(2,1)}, bf16[2,64,128]{2,1,0:T(8,128)(2,1)}, bf16[2,64,128]{2,1,0:T(8,128)(2,1)}, bf16[2,64,128]{2,1,0:T(8,128)(2,1)}...) custom-call(s32[1]{0:T(128)} %bitcast.me_ref, ...), custom_call_target="tpu_custom_call" | custom-call | flops 1073741824 | bytes 4194304 | tf_op jit(solution)/shard_map/forward/pallas_call | solution.py:64
  4.9 2.5 %collective-permute-start.1 = (bf16[2,64,128]{2,1,0:T(8,128)(2,1)}, bf16[2,64,128]{2,1,0:T(8,128)(2,1)S(1)}, u32[]{:S(2)}, u32[]{:S(2)}) collective-permute-start(bf16[2,64,128]{2,1,0:T(8,128)(2,1)} %get-tuple-element.38), channel_id=1, source_target_pairs={{0,2},{2,0},{4,6},{6,4},{8,10},{10,8},{12,14},{14,12},{1,3},{3,1},... | collective-permute-start | bytes 98312 | tf_op jit(solution)/shard_map/ppermute | solution.py:237
  7.4 1.6 %collective-permute-start.2 = (bf16[2,64,128]{2,1,0:T(8,128)(2,1)}, bf16[2,64,128]{2,1,0:T(8,128)(2,1)S(1)}, u32[]{:S(2)}, u32[]{:S(2)}) collective-permute-start(bf16[2,64,128]{2,1,0:T(8,128)(2,1)} %get-tuple-element.39), channel_id=1, source_target_pairs={{0,4},{2,6},{4,0},{6,2},{8,12},{10,14},{12,8},{14,10},{1,5},{3,7},... | collective-permute-start | bytes 98312 | tf_op jit(solution)/shard_map/ppermute | solution.py:237
  9.0 3.0 %collective-permute-start.4 = (bf16[2,64,128]{2,1,0:T(8,128)(2,1)}, bf16[2,64,128]{2,1,0:T(8,128)(2,1)S(1)}, u32[]{:S(2)}, u32[]{:S(2)}) collective-permute-start(bf16[2,64,128]{2,1,0:T(8,128)(2,1)} %get-tuple-element.41), channel_id=1, source_target_pairs={{0,8},{2,10},{4,12},{6,14},{8,0},{10,2},{12,4},{14,6},{1,9},{3,11}... | collective-permute-start | bytes 98312 | tf_op jit(solution)/shard_map/ppermute | solution.py:237
  12.3 9.6 %forward.3 = (bf16[2,192,128]{2,1,0:T(8,128)(2,1)}, bf16[2,192,128]{2,1,0:T(8,128)(2,1)}, bf16[2,192,128]{2,1,0:T(8,128)(2,1)}, bf16[2,192,128]{2,1,0:T(8,128)(2...) custom-call(s32[1]{0:T(128)} %bitcast.me_ref, ...), custom_call_target="tpu_custom_call" | custom-call | flops 3221225472 | bytes 12582912 | tf_op jit(solution)/shard_map/forward/pallas_call | solution.py:64
  22.0 1.3 %collective-permute-start.5 = (bf16[2,64,128]{2,1,0:T(8,128)(2,1)S(1)}, bf16[2,64,128]{2,1,0:T(8,128)(2,1)S(1)}, u32[]{:S(2)}, u32[]{:S(2)}) collective-permute-start(bf16[2,64,128]{2,1,0:T(8,128)(2,1)S(1)} %copy-done.32), channel_id=1, source_target_pairs={{0,10},{2,8},{4,14},{6,12},{8,2},{10,0},{12,6},{14,4},{1,11},{3,9}... | collective-permute-start | bytes 98312 | tf_op jit(solution)/shard_map/ppermute | solution.py:237
  23.3 3.7 %collective-permute-start.6 = (bf16[2,64,128]{2,1,0:T(8,128)(2,1)S(1)}, bf16[2,64,128]{2,1,0:T(8,128)(2,1)S(1)}, u32[]{:S(2)}, u32[]{:S(2)}) collective-permute-start(bf16[2,64,128]{2,1,0:T(8,128)(2,1)S(1)} %copy-done.31), channel_id=1, source_target_pairs={{0,12},{2,14},{4,8},{6,10},{8,4},{10,6},{12,0},{14,2},{1,13},{3,15... | collective-permute-start | bytes 98312 | tf_op jit(solution)/shard_map/ppermute | solution.py:237
  27.3 1.7 %collective-permute-start.8 = (bf16[2,192,128]{2,1,0:T(8,128)(2,1)}, bf16[2,192,128]{2,1,0:T(8,128)(2,1)S(1)}, u32[]{:S(2)}, u32[]{:S(2)}) collective-permute-start(bf16[2,192,128]{2,1,0:T(8,128)(2,1)} %get-tuple-element.46), channel_id=1, source_target_pairs={{0,2},{2,0},{4,6},{6,4},{8,10},{10,8},{12,14},{14,12},{1,3},{3,1},... | collective-permute-start | bytes 294920 | tf_op jit(solution)/shard_map/ppermute | solution.py:237
  29.4 1.6 %collective-permute-start.10 = (bf16[2,192,128]{2,1,0:T(8,128)(2,1)}, bf16[2,192,128]{2,1,0:T(8,128)(2,1)S(1)}, u32[]{:S(2)}, u32[]{:S(2)}) collective-permute-start(bf16[2,192,128]{2,1,0:T(8,128)(2,1)} %get-tuple-element.48), channel_id=1, source_target_pairs={{0,6},{2,4},{4,2},{6,0},{8,14},{10,12},{12,10},{14,8},{1,7},{3,5},... | collective-permute-start | bytes 294920 | tf_op jit(solution)/shard_map/ppermute | solution.py:237
  31.1 2.9 %collective-permute-done.7.refs_7_ = bf16[2,64,128]{2,1,0:T(8,128)(2,1)S(1)} collective-permute-done((bf16[2,64,128]{2,1,0:T(8,128)(2,1)S(1)}, bf16[2,64,128]{2,1,0:T(8,128)(2,1)S(1)}, u32[]{:S(2)}, u32[]{:S(2)}) %collective-permute-start.7) | collective-permute-done | bytes 32800 | tf_op jit(solution)/shard_map/ppermute | solution.py:237
  34.0 3.1 %collective-permute-start.12 = (bf16[2,192,128]{2,1,0:T(8,128)(2,1)}, bf16[2,192,128]{2,1,0:T(8,128)(2,1)S(1)}, u32[]{:S(2)}, u32[]{:S(2)}) collective-permute-start(bf16[2,192,128]{2,1,0:T(8,128)(2,1)} %get-tuple-element.50), channel_id=1, source_target_pairs={{0,10},{2,8},{4,14},{6,12},{8,2},{10,0},{12,6},{14,4},{1,11},{3,9}... | collective-permute-start | bytes 294920 | tf_op jit(solution)/shard_map/ppermute | solution.py:237
  37.1 1.4 %collective-permute-start.13 = (bf16[2,192,128]{2,1,0:T(8,128)(2,1)}, bf16[2,192,128]{2,1,0:T(8,128)(2,1)S(1)}, u32[]{:S(2)}, u32[]{:S(2)}) collective-permute-start(bf16[2,192,128]{2,1,0:T(8,128)(2,1)} %get-tuple-element.51), channel_id=1, source_target_pairs={{0,12},{2,14},{4,8},{6,10},{8,4},{10,6},{12,0},{14,2},{1,13},{3,15... | collective-permute-start | bytes 294920 | tf_op jit(solution)/shard_map/ppermute | solution.py:237
  38.6 3.1 %collective-permute-start.14 = (bf16[2,192,128]{2,1,0:T(8,128)(2,1)}, bf16[2,192,128]{2,1,0:T(8,128)(2,1)S(1)}, u32[]{:S(2)}, u32[]{:S(2)}) collective-permute-start(bf16[2,192,128]{2,1,0:T(8,128)(2,1)} %get-tuple-element.52), channel_id=1, source_target_pairs={{0,14},{2,12},{4,10},{6,8},{8,6},{10,4},{12,2},{14,0},{1,15},{3,13... | collective-permute-start | bytes 294920 | tf_op jit(solution)/shard_map/ppermute | solution.py:237
  42.3 4.9 %collective-permute-done.11.refs_12_ = bf16[2,192,128]{2,1,0:T(8,128)(2,1)S(1)} collective-permute-done((bf16[2,192,128]{2,1,0:T(8,128)(2,1)}, bf16[2,192,128]{2,1,0:T(8,128)(2,1)S(1)}, u32[]{:S(2)}, u32[]{:S(2)}) %collective-permute-start.11) | collective-permute-done | bytes 98336 | tf_op jit(solution)/shard_map/ppermute | solution.py:237
  47.2 2.6 %collective-permute-done.12.refs_13_ = bf16[2,192,128]{2,1,0:T(8,128)(2,1)S(1)} collective-permute-done((bf16[2,192,128]{2,1,0:T(8,128)(2,1)}, bf16[2,192,128]{2,1,0:T(8,128)(2,1)S(1)}, u32[]{:S(2)}, u32[]{:S(2)}) %collective-permute-start.12) | collective-permute-done | bytes 98336 | tf_op jit(solution)/shard_map/ppermute | solution.py:237
  50.6 0.9 copy-done
  51.4 8.0 %tiles.1 = (bf16[2,192,128]{2,1,0:T(8,128)(2,1)}, bf16[2,192,128]{2,1,0:T(8,128)(2,1)}, bf16[2,192,128]{2,1,0:T(8,128)(2,1)}, bf16[2,192,128]{2,1,0:T(8,128)(2,1...) custom-call(s32[5,40]{1,0:T(8,128)} %pad_add_fusion.slot_ref, ...), custom_call_target="tpu_custom_call" | custom-call | flops 1342177280 | bytes 5242880 | tf_op jit(solution)/shard_map/tiles/pallas_call | solution.py:136
  59.5 1.0 collective-permute-start.22
  60.5 3.0 %collective-permute-start.23 = (bf16[2,192,128]{2,1,0:T(8,128)(2,1)}, bf16[2,192,128]{2,1,0:T(8,128)(2,1)S(1)}, u32[]{:S(2)}, u32[]{:S(2)}) collective-permute-start(bf16[2,192,128]{2,1,0:T(8,128)(2,1)} %get-tuple-element.63), channel_id=1, source_target_pairs={{0,4},{2,6},{4,0},{6,2},{8,12},{10,14},{12,8},{14,10},{1,5},{3,7},... | collective-permute-start | bytes 294920 | tf_op jit(solution)/shard_map/ppermute | solution.py:237
  63.5 0.9 collective-permute-start.15
  64.4 2.6 %collective-permute-start.24 = (bf16[2,192,128]{2,1,0:T(8,128)(2,1)}, bf16[2,192,128]{2,1,0:T(8,128)(2,1)S(1)}, u32[]{:S(2)}, u32[]{:S(2)}) collective-permute-start(bf16[2,192,128]{2,1,0:T(8,128)(2,1)} %get-tuple-element.64), channel_id=1, source_target_pairs={{0,6},{2,4},{4,2},{6,0},{8,14},{10,12},{12,10},{14,8},{1,7},{3,5},... | collective-permute-start | bytes 294920 | tf_op jit(solution)/shard_map/ppermute | solution.py:237
  67.6 1.1 collective-permute-start.25
  69.1 1.9 %collective-permute-start.26 = (bf16[2,192,128]{2,1,0:T(8,128)(2,1)}, bf16[2,192,128]{2,1,0:T(8,128)(2,1)S(1)}, u32[]{:S(2)}, u32[]{:S(2)}) collective-permute-start(bf16[2,192,128]{2,1,0:T(8,128)(2,1)} %get-tuple-element.66), channel_id=1, source_target_pairs={{0,10},{2,8},{4,14},{6,12},{8,2},{10,0},{12,6},{14,4},{1,11},{3,9}... | collective-permute-start | bytes 294920 | tf_op jit(solution)/shard_map/ppermute | solution.py:237
  71.0 1.8 %collective-permute-start.27 = (bf16[2,192,128]{2,1,0:T(8,128)(2,1)}, bf16[2,192,128]{2,1,0:T(8,128)(2,1)S(1)}, u32[]{:S(2)}, u32[]{:S(2)}) collective-permute-start(bf16[2,192,128]{2,1,0:T(8,128)(2,1)} %get-tuple-element.67), channel_id=1, source_target_pairs={{0,12},{2,14},{4,8},{6,10},{8,4},{10,6},{12,0},{14,2},{1,13},{3,15... | collective-permute-start | bytes 294920 | tf_op jit(solution)/shard_map/ppermute | solution.py:237
  72.8 2.5 %collective-permute-start.28 = (bf16[2,192,128]{2,1,0:T(8,128)(2,1)}, bf16[2,192,128]{2,1,0:T(8,128)(2,1)S(1)}, u32[]{:S(2)}, u32[]{:S(2)}) collective-permute-start(bf16[2,192,128]{2,1,0:T(8,128)(2,1)} %get-tuple-element.68), channel_id=1, source_target_pairs={{0,14},{2,12},{4,10},{6,8},{8,6},{10,4},{12,2},{14,0},{1,15},{3,13... | collective-permute-start | bytes 294920 | tf_op jit(solution)/shard_map/ppermute | solution.py:237
  75.3 6.4 %collective-permute-done.25.refs_4_ = bf16[2,192,128]{2,1,0:T(8,128)(2,1)S(1)} collective-permute-done((bf16[2,192,128]{2,1,0:T(8,128)(2,1)}, bf16[2,192,128]{2,1,0:T(8,128)(2,1)S(1)}, u32[]{:S(2)}, u32[]{:S(2)}) %collective-permute-start.25) | collective-permute-done | bytes 98336 | tf_op jit(solution)/shard_map/ppermute | solution.py:237
  81.7 2.1 %collective-permute-done.26.refs_5_ = bf16[2,192,128]{2,1,0:T(8,128)(2,1)S(1)} collective-permute-done((bf16[2,192,128]{2,1,0:T(8,128)(2,1)}, bf16[2,192,128]{2,1,0:T(8,128)(2,1)S(1)}, u32[]{:S(2)}, u32[]{:S(2)}) %collective-permute-start.26) | collective-permute-done | bytes 98336 | tf_op jit(solution)/shard_map/ppermute | solution.py:237
  83.8 0.8 collective-permute-start.19
  84.6 1.8 %collective-permute-start.20 = (bf16[2,64,128]{2,1,0:T(8,128)(2,1)}, bf16[2,64,128]{2,1,0:T(8,128)(2,1)S(1)}, u32[]{:S(2)}, u32[]{:S(2)}) collective-permute-start(bf16[2,64,128]{2,1,0:T(8,128)(2,1)} %get-tuple-element.59), channel_id=1, source_target_pairs={{0,12},{2,14},{4,8},{6,10},{8,4},{10,6},{12,0},{14,2},{1,13},{3,15... | collective-permute-start | bytes 98312 | tf_op jit(solution)/shard_map/ppermute | solution.py:237
  86.4 3.0 %collective-permute-start.21 = (bf16[2,64,128]{2,1,0:T(8,128)(2,1)}, bf16[2,64,128]{2,1,0:T(8,128)(2,1)S(1)}, u32[]{:S(2)}, u32[]{:S(2)}) collective-permute-start(bf16[2,64,128]{2,1,0:T(8,128)(2,1)} %get-tuple-element.60), channel_id=1, source_target_pairs={{0,14},{2,12},{4,10},{6,8},{8,6},{10,4},{12,2},{14,0},{1,15},{3,13... | collective-permute-start | bytes 98312 | tf_op jit(solution)/shard_map/ppermute | solution.py:237
  89.4 20.3 %inverse.2.refs_8_ = bf16[256,256,128]{2,1,0:T(8,128)(2,1)} custom-call(s32[1]{0:T(128)} %bitcast.me_ref, bf16[4096,256]{1,0:T(8,128)(2,1)} %constant.20.clone.table_ref, bf16[2,192,128]{2,1,0:T(8,128)(2,1)} %get-tuple-element.61.refs_0_, bf16[2,192,128]{2,1,0:T(8,128)(2,1)} %copy-done.1, bf16[2,192,128]{2,1,0:T(8,128)(2,1)} %copy-done.2, ...), custom_call_target="tpu_custom_call" | custom-call | flops 3221225472 | bytes 12582912 | tf_op jit(solution)/shard_map/inverse/pallas_call | solution.py:207
  110.5 7.5 %inverse.3 = bf16[256,256,128]{2,1,0:T(8,128)(2,1)} custom-call(s32[1]{0:T(128)} %bitcast.me_ref, bf16[4096,256]{1,0:T(8,128)(2,1)} %constant.20.clone.table_ref, bf16[2,64,128]{2,1,0:T(8,128)(2,1)} %get-tuple-element.53.refs_0_, bf16[2,64,128]{2,1,0:T(8,128)(2,1)} %copy-done.22, bf16[2,64,128]{2,1,0:T(8,128)(2,1)} %copy-done.23, ...), custom_call_target="tpu_custom_call", output_to_operand_aliasing={{}: (10, {})} | custom-call | flops 1073741824 | bytes 4194304 | tf_op jit(solution)/shard_map/inverse/pallas_call | solution.py:207
  (111 shorter events, 4.7 us)
Async XLA Ops:
  0.0 49.9 %collective-permute-start = (bf16[40,2,128,128]{3,2,1,0:T(8,128)(2,1)}, bf16[40,2,128,128]{3,2,1,0:T(8,128)(2,1)S(1)}, u32[]{:S(2)}, u32[]{:S(2)}) collective-permute-start(bf16[40,2,128,128]{3,2,1,0:T(8,128)(2,1)} %bitcast.4), channel_id=1, source_target_pairs={{0,1},{1,0},{2,3},{3,2},{4,5},{5,4},{6,7},{7,6},{8,9},{9,8},{10,11... | collective-permute-start | bytes 7864328 | tf_op jit(solution)/shard_map/ppermute | solution.py:258
  4.9 17.1 %collective-permute-start.1 = (bf16[2,64,128]{2,1,0:T(8,128)(2,1)}, bf16[2,64,128]{2,1,0:T(8,128)(2,1)S(1)}, u32[]{:S(2)}, u32[]{:S(2)}) collective-permute-start(bf16[2,64,128]{2,1,0:T(8,128)(2,1)} %get-tuple-element.38), channel_id=1, source_target_pairs={{0,2},{2,0},{4,6},{6,4},{8,10},{10,8},{12,14},{14,12},{1,3},{3,1},... | collective-permute-start | bytes 98312 | tf_op jit(solution)/shard_map/ppermute | solution.py:237
  7.4 15.9 %collective-permute-start.2 = (bf16[2,64,128]{2,1,0:T(8,128)(2,1)}, bf16[2,64,128]{2,1,0:T(8,128)(2,1)S(1)}, u32[]{:S(2)}, u32[]{:S(2)}) collective-permute-start(bf16[2,64,128]{2,1,0:T(8,128)(2,1)} %get-tuple-element.39), channel_id=1, source_target_pairs={{0,4},{2,6},{4,0},{6,2},{8,12},{10,14},{12,8},{14,10},{1,5},{3,7},... | collective-permute-start | bytes 98312 | tf_op jit(solution)/shard_map/ppermute | solution.py:237
  9.0 18.2 %collective-permute-start.3 = (bf16[2,64,128]{2,1,0:T(8,128)(2,1)}, bf16[2,64,128]{2,1,0:T(8,128)(2,1)S(1)}, u32[]{:S(2)}, u32[]{:S(2)}) collective-permute-start(bf16[2,64,128]{2,1,0:T(8,128)(2,1)} %get-tuple-element.40), channel_id=1, source_target_pairs={{0,6},{2,4},{4,2},{6,0},{8,14},{10,12},{12,10},{14,8},{1,7},{3,5},... | collective-permute-start | bytes 98312 | tf_op jit(solution)/shard_map/ppermute | solution.py:237
  9.0 18.3 %collective-permute-start.4 = (bf16[2,64,128]{2,1,0:T(8,128)(2,1)}, bf16[2,64,128]{2,1,0:T(8,128)(2,1)S(1)}, u32[]{:S(2)}, u32[]{:S(2)}) collective-permute-start(bf16[2,64,128]{2,1,0:T(8,128)(2,1)} %get-tuple-element.41), channel_id=1, source_target_pairs={{0,8},{2,10},{4,12},{6,14},{8,0},{10,2},{12,4},{14,6},{1,9},{3,11}... | collective-permute-start | bytes 98312 | tf_op jit(solution)/shard_map/ppermute | solution.py:237
  21.9 28.0 %copy-start.15 = (bf16[2,64,128]{2,1,0:T(8,128)(2,1)}, bf16[2,64,128]{2,1,0:T(8,128)(2,1)S(1)}, u32[]{:S(2)}) copy-start(bf16[2,64,128]{2,1,0:T(8,128)(2,1)S(1)} %collective-permute-done.1.refs_1_) | copy-start | bytes 98308
  22.0 7.0 %collective-permute-start.5 = (bf16[2,64,128]{2,1,0:T(8,128)(2,1)S(1)}, bf16[2,64,128]{2,1,0:T(8,128)(2,1)S(1)}, u32[]{:S(2)}, u32[]{:S(2)}) collective-permute-start(bf16[2,64,128]{2,1,0:T(8,128)(2,1)S(1)} %copy-done.32), channel_id=1, source_target_pairs={{0,10},{2,8},{4,14},{6,12},{8,2},{10,0},{12,6},{14,4},{1,11},{3,9}... | collective-permute-start | bytes 98312 | tf_op jit(solution)/shard_map/ppermute | solution.py:237
  23.3 6.1 %collective-permute-start.6 = (bf16[2,64,128]{2,1,0:T(8,128)(2,1)S(1)}, bf16[2,64,128]{2,1,0:T(8,128)(2,1)S(1)}, u32[]{:S(2)}, u32[]{:S(2)}) collective-permute-start(bf16[2,64,128]{2,1,0:T(8,128)(2,1)S(1)} %copy-done.31), channel_id=1, source_target_pairs={{0,12},{2,14},{4,8},{6,10},{8,4},{10,6},{12,0},{14,2},{1,13},{3,15... | collective-permute-start | bytes 98312 | tf_op jit(solution)/shard_map/ppermute | solution.py:237
  27.2 6.8 %collective-permute-start.7 = (bf16[2,64,128]{2,1,0:T(8,128)(2,1)S(1)}, bf16[2,64,128]{2,1,0:T(8,128)(2,1)S(1)}, u32[]{:S(2)}, u32[]{:S(2)}) collective-permute-start(bf16[2,64,128]{2,1,0:T(8,128)(2,1)S(1)} %copy-done.30), channel_id=1, source_target_pairs={{0,14},{2,12},{4,10},{6,8},{8,6},{10,4},{12,2},{14,0},{1,15},{3,13... | collective-permute-start | bytes 98312 | tf_op jit(solution)/shard_map/ppermute | solution.py:237
  27.3 6.7 %collective-permute-start.8 = (bf16[2,192,128]{2,1,0:T(8,128)(2,1)}, bf16[2,192,128]{2,1,0:T(8,128)(2,1)S(1)}, u32[]{:S(2)}, u32[]{:S(2)}) collective-permute-start(bf16[2,192,128]{2,1,0:T(8,128)(2,1)} %get-tuple-element.46), channel_id=1, source_target_pairs={{0,2},{2,0},{4,6},{6,4},{8,10},{10,8},{12,14},{14,12},{1,3},{3,1},... | collective-permute-start | bytes 294920 | tf_op jit(solution)/shard_map/ppermute | solution.py:237
  29.0 8.1 %collective-permute-start.9 = (bf16[2,192,128]{2,1,0:T(8,128)(2,1)}, bf16[2,192,128]{2,1,0:T(8,128)(2,1)S(1)}, u32[]{:S(2)}, u32[]{:S(2)}) collective-permute-start(bf16[2,192,128]{2,1,0:T(8,128)(2,1)} %get-tuple-element.47), channel_id=1, source_target_pairs={{0,4},{2,6},{4,0},{6,2},{8,12},{10,14},{12,8},{14,10},{1,5},{3,7},... | collective-permute-start | bytes 294920 | tf_op jit(solution)/shard_map/ppermute | solution.py:237
  29.4 9.1 %collective-permute-start.10 = (bf16[2,192,128]{2,1,0:T(8,128)(2,1)}, bf16[2,192,128]{2,1,0:T(8,128)(2,1)S(1)}, u32[]{:S(2)}, u32[]{:S(2)}) collective-permute-start(bf16[2,192,128]{2,1,0:T(8,128)(2,1)} %get-tuple-element.48), channel_id=1, source_target_pairs={{0,6},{2,4},{4,2},{6,0},{8,14},{10,12},{12,10},{14,8},{1,7},{3,5},... | collective-permute-start | bytes 294920 | tf_op jit(solution)/shard_map/ppermute | solution.py:237
  34.0 13.2 %collective-permute-start.11 = (bf16[2,192,128]{2,1,0:T(8,128)(2,1)}, bf16[2,192,128]{2,1,0:T(8,128)(2,1)S(1)}, u32[]{:S(2)}, u32[]{:S(2)}) collective-permute-start(bf16[2,192,128]{2,1,0:T(8,128)(2,1)} %get-tuple-element.49), channel_id=1, source_target_pairs={{0,8},{2,10},{4,12},{6,14},{8,0},{10,2},{12,4},{14,6},{1,9},{3,11}... | collective-permute-start | bytes 294920 | tf_op jit(solution)/shard_map/ppermute | solution.py:237
  34.0 15.8 %collective-permute-start.12 = (bf16[2,192,128]{2,1,0:T(8,128)(2,1)}, bf16[2,192,128]{2,1,0:T(8,128)(2,1)S(1)}, u32[]{:S(2)}, u32[]{:S(2)}) collective-permute-start(bf16[2,192,128]{2,1,0:T(8,128)(2,1)} %get-tuple-element.50), channel_id=1, source_target_pairs={{0,10},{2,8},{4,14},{6,12},{8,2},{10,0},{12,6},{14,4},{1,11},{3,9}... | collective-permute-start | bytes 294920 | tf_op jit(solution)/shard_map/ppermute | solution.py:237
  37.1 12.7 %collective-permute-start.13 = (bf16[2,192,128]{2,1,0:T(8,128)(2,1)}, bf16[2,192,128]{2,1,0:T(8,128)(2,1)S(1)}, u32[]{:S(2)}, u32[]{:S(2)}) collective-permute-start(bf16[2,192,128]{2,1,0:T(8,128)(2,1)} %get-tuple-element.51), channel_id=1, source_target_pairs={{0,12},{2,14},{4,8},{6,10},{8,4},{10,6},{12,0},{14,2},{1,13},{3,15... | collective-permute-start | bytes 294920 | tf_op jit(solution)/shard_map/ppermute | solution.py:237
  38.6 11.3 %collective-permute-start.14 = (bf16[2,192,128]{2,1,0:T(8,128)(2,1)}, bf16[2,192,128]{2,1,0:T(8,128)(2,1)S(1)}, u32[]{:S(2)}, u32[]{:S(2)}) collective-permute-start(bf16[2,192,128]{2,1,0:T(8,128)(2,1)} %get-tuple-element.52), channel_id=1, source_target_pairs={{0,14},{2,12},{4,10},{6,8},{8,6},{10,4},{12,2},{14,0},{1,15},{3,13... | collective-permute-start | bytes 294920 | tf_op jit(solution)/shard_map/ppermute | solution.py:237
  59.5 11.5 %collective-permute-start.22 = (bf16[2,192,128]{2,1,0:T(8,128)(2,1)}, bf16[2,192,128]{2,1,0:T(8,128)(2,1)S(1)}, u32[]{:S(2)}, u32[]{:S(2)}) collective-permute-start(bf16[2,192,128]{2,1,0:T(8,128)(2,1)} %get-tuple-element.62), channel_id=1, source_target_pairs={{0,2},{2,0},{4,6},{6,4},{8,10},{10,8},{12,14},{14,12},{1,3},{3,1},... | collective-permute-start | bytes 294920 | tf_op jit(solution)/shard_map/ppermute | solution.py:237
  60.5 12.4 %collective-permute-start.23 = (bf16[2,192,128]{2,1,0:T(8,128)(2,1)}, bf16[2,192,128]{2,1,0:T(8,128)(2,1)S(1)}, u32[]{:S(2)}, u32[]{:S(2)}) collective-permute-start(bf16[2,192,128]{2,1,0:T(8,128)(2,1)} %get-tuple-element.63), channel_id=1, source_target_pairs={{0,4},{2,6},{4,0},{6,2},{8,12},{10,14},{12,8},{14,10},{1,5},{3,7},... | collective-permute-start | bytes 294920 | tf_op jit(solution)/shard_map/ppermute | solution.py:237
  63.5 4.1 %collective-permute-start.15 = (bf16[2,64,128]{2,1,0:T(8,128)(2,1)}, bf16[2,64,128]{2,1,0:T(8,128)(2,1)S(1)}, u32[]{:S(2)}, u32[]{:S(2)}) collective-permute-start(bf16[2,64,128]{2,1,0:T(8,128)(2,1)} %get-tuple-element.54), channel_id=1, source_target_pairs={{0,2},{2,0},{4,6},{6,4},{8,10},{10,8},{12,14},{14,12},{1,3},{3,1},... | collective-permute-start | bytes 98312 | tf_op jit(solution)/shard_map/ppermute | solution.py:237
  64.4 4.7 %collective-permute-start.16 = (bf16[2,64,128]{2,1,0:T(8,128)(2,1)}, bf16[2,64,128]{2,1,0:T(8,128)(2,1)S(1)}, u32[]{:S(2)}, u32[]{:S(2)}) collective-permute-start(bf16[2,64,128]{2,1,0:T(8,128)(2,1)} %get-tuple-element.55), channel_id=1, source_target_pairs={{0,4},{2,6},{4,0},{6,2},{8,12},{10,14},{12,8},{14,10},{1,5},{3,7},... | collective-permute-start | bytes 98312 | tf_op jit(solution)/shard_map/ppermute | solution.py:237
  64.4 10.9 %collective-permute-start.24 = (bf16[2,192,128]{2,1,0:T(8,128)(2,1)}, bf16[2,192,128]{2,1,0:T(8,128)(2,1)S(1)}, u32[]{:S(2)}, u32[]{:S(2)}) collective-permute-start(bf16[2,192,128]{2,1,0:T(8,128)(2,1)} %get-tuple-element.64), channel_id=1, source_target_pairs={{0,6},{2,4},{4,2},{6,0},{8,14},{10,12},{12,10},{14,8},{1,7},{3,5},... | collective-permute-start | bytes 294920 | tf_op jit(solution)/shard_map/ppermute | solution.py:237
  67.6 42.2 %copy-start.22 = (bf16[2,64,128]{2,1,0:T(8,128)(2,1)}, bf16[2,64,128]{2,1,0:T(8,128)(2,1)S(1)}, u32[]{:S(2)}) copy-start(bf16[2,64,128]{2,1,0:T(8,128)(2,1)S(1)} %collective-permute-done.15.refs_1_) | copy-start | bytes 98308
  67.6 14.1 %collective-permute-start.25 = (bf16[2,192,128]{2,1,0:T(8,128)(2,1)}, bf16[2,192,128]{2,1,0:T(8,128)(2,1)S(1)}, u32[]{:S(2)}, u32[]{:S(2)}) collective-permute-start(bf16[2,192,128]{2,1,0:T(8,128)(2,1)} %get-tuple-element.65), channel_id=1, source_target_pairs={{0,8},{2,10},{4,12},{6,14},{8,0},{10,2},{12,4},{14,6},{1,9},{3,11}... | collective-permute-start | bytes 294920 | tf_op jit(solution)/shard_map/ppermute | solution.py:237
  69.1 40.7 %copy-start.23 = (bf16[2,64,128]{2,1,0:T(8,128)(2,1)}, bf16[2,64,128]{2,1,0:T(8,128)(2,1)S(1)}, u32[]{:S(2)}) copy-start(bf16[2,64,128]{2,1,0:T(8,128)(2,1)S(1)} %collective-permute-done.16.refs_2_) | copy-start | bytes 98308
  69.1 14.7 %collective-permute-start.26 = (bf16[2,192,128]{2,1,0:T(8,128)(2,1)}, bf16[2,192,128]{2,1,0:T(8,128)(2,1)S(1)}, u32[]{:S(2)}, u32[]{:S(2)}) collective-permute-start(bf16[2,192,128]{2,1,0:T(8,128)(2,1)} %get-tuple-element.66), channel_id=1, source_target_pairs={{0,10},{2,8},{4,14},{6,12},{8,2},{10,0},{12,6},{14,4},{1,11},{3,9}... | collective-permute-start | bytes 294920 | tf_op jit(solution)/shard_map/ppermute | solution.py:237
  71.0 13.6 %collective-permute-start.27 = (bf16[2,192,128]{2,1,0:T(8,128)(2,1)}, bf16[2,192,128]{2,1,0:T(8,128)(2,1)S(1)}, u32[]{:S(2)}, u32[]{:S(2)}) collective-permute-start(bf16[2,192,128]{2,1,0:T(8,128)(2,1)} %get-tuple-element.67), channel_id=1, source_target_pairs={{0,12},{2,14},{4,8},{6,10},{8,4},{10,6},{12,0},{14,2},{1,13},{3,15... | collective-permute-start | bytes 294920 | tf_op jit(solution)/shard_map/ppermute | solution.py:237
  72.8 13.6 %collective-permute-start.28 = (bf16[2,192,128]{2,1,0:T(8,128)(2,1)}, bf16[2,192,128]{2,1,0:T(8,128)(2,1)S(1)}, u32[]{:S(2)}, u32[]{:S(2)}) collective-permute-start(bf16[2,192,128]{2,1,0:T(8,128)(2,1)} %get-tuple-element.68), channel_id=1, source_target_pairs={{0,14},{2,12},{4,10},{6,8},{8,6},{10,4},{12,2},{14,0},{1,15},{3,13... | collective-permute-start | bytes 294920 | tf_op jit(solution)/shard_map/ppermute | solution.py:237
  75.3 34.5 %collective-permute-start.17 = (bf16[2,64,128]{2,1,0:T(8,128)(2,1)}, bf16[2,64,128]{2,1,0:T(8,128)(2,1)S(1)}, u32[]{:S(2)}, u32[]{:S(2)}) collective-permute-start(bf16[2,64,128]{2,1,0:T(8,128)(2,1)} %get-tuple-element.56), channel_id=1, source_target_pairs={{0,6},{2,4},{4,2},{6,0},{8,14},{10,12},{12,10},{14,8},{1,7},{3,5},... | collective-permute-start | bytes 98312 | tf_op jit(solution)/shard_map/ppermute | solution.py:237
  81.7 28.1 %collective-permute-start.18 = (bf16[2,64,128]{2,1,0:T(8,128)(2,1)}, bf16[2,64,128]{2,1,0:T(8,128)(2,1)S(1)}, u32[]{:S(2)}, u32[]{:S(2)}) collective-permute-start(bf16[2,64,128]{2,1,0:T(8,128)(2,1)} %get-tuple-element.57), channel_id=1, source_target_pairs={{0,8},{2,10},{4,12},{6,14},{8,0},{10,2},{12,4},{14,6},{1,9},{3,11}... | collective-permute-start | bytes 98312 | tf_op jit(solution)/shard_map/ppermute | solution.py:237
  83.8 26.0 %collective-permute-start.19 = (bf16[2,64,128]{2,1,0:T(8,128)(2,1)}, bf16[2,64,128]{2,1,0:T(8,128)(2,1)S(1)}, u32[]{:S(2)}, u32[]{:S(2)}) collective-permute-start(bf16[2,64,128]{2,1,0:T(8,128)(2,1)} %get-tuple-element.58), channel_id=1, source_target_pairs={{0,10},{2,8},{4,14},{6,12},{8,2},{10,0},{12,6},{14,4},{1,11},{3,9}... | collective-permute-start | bytes 98312 | tf_op jit(solution)/shard_map/ppermute | solution.py:237
  84.6 25.2 %collective-permute-start.20 = (bf16[2,64,128]{2,1,0:T(8,128)(2,1)}, bf16[2,64,128]{2,1,0:T(8,128)(2,1)S(1)}, u32[]{:S(2)}, u32[]{:S(2)}) collective-permute-start(bf16[2,64,128]{2,1,0:T(8,128)(2,1)} %get-tuple-element.59), channel_id=1, source_target_pairs={{0,12},{2,14},{4,8},{6,10},{8,4},{10,6},{12,0},{14,2},{1,13},{3,15... | collective-permute-start | bytes 98312 | tf_op jit(solution)/shard_map/ppermute | solution.py:237
  86.4 23.5 %collective-permute-start.21 = (bf16[2,64,128]{2,1,0:T(8,128)(2,1)}, bf16[2,64,128]{2,1,0:T(8,128)(2,1)S(1)}, u32[]{:S(2)}, u32[]{:S(2)}) collective-permute-start(bf16[2,64,128]{2,1,0:T(8,128)(2,1)} %get-tuple-element.60), channel_id=1, source_target_pairs={{0,14},{2,12},{4,10},{6,8},{8,6},{10,4},{12,2},{14,0},{1,15},{3,13... | collective-permute-start | bytes 98312 | tf_op jit(solution)/shard_map/ppermute | solution.py:237
  (31 other events, 311.2 us)

commit v2 on v0

v2 whole, which is shorter than its diff:
```python
import functools
import math

import jax
import jax.numpy as jnp
import numpy as np
from jax import lax
from jax.experimental import pallas as pl
from jax.experimental.pallas import tpu as pltpu
from jax.sharding import PartitionSpec as P

BF16 = jnp.bfloat16
F32 = jnp.float32
SUB = 16
LANES = 128
CUTS = (1, 1)


def transform_tables(samples, frequencies):
    turns = (1 + np.arange(frequencies))[:, None] * np.arange(samples)[None, :] % samples
    phases = turns * (2.0 * math.pi / samples)
    both = np.stack([np.cos(phases), -np.sin(phases)], axis=1) * samples**-0.5
    small = both.astype(jnp.bfloat16)
    twice = (2.0 * both).astype(jnp.bfloat16)
    forward = np.zeros((frequencies, 2, SUB, samples, SUB), jnp.bfloat16)
    inverse = np.zeros((samples, SUB, frequencies, 2, SUB), jnp.bfloat16)
    for r in range(SUB):
        forward[:, :, r, :, r] = small
        inverse[:, r, :, :, r] = twice.transpose(2, 0, 1)

    def cut(table):
        high, wide = table.shape
        return np.ascontiguousarray(table.reshape(high, wide // LANES, LANES).transpose(1, 0, 2))

    return (
        cut(forward.reshape(frequencies * 2 * SUB, samples * SUB)),
        cut(inverse.reshape(samples * SUB, frequencies * 2 * SUB)),
    )


def params():
    return pltpu.CompilerParams(vmem_limit_bytes=52 * 2**20)


def place_of(me, s, rows, first, count):
    return pl.ds(pl.multiple_of((me ^ s) * rows + first, SUB), count)


def forward_kernel(first, step, early, sends, me_ref, table_hbm, traces_hbm, *refs):
    early_ref = refs[0] if early else None
    out_refs = refs[1 if early else 0 : -4]
    table_ref, traces_ref, table_sem, sems = refs[-4:]
    steps, samples, _, width = traces_ref.shape
    tiles, high, _ = table_ref.shape
    part = min(256, high)
    me = me_ref[0]

    def fetch(i):
        return pltpu.make_async_copy(
            traces_hbm.at[:, pl.ds(first + i * step, step), :], traces_ref.at[i], sems.at[i]
        )

    table_copy = pltpu.make_async_copy(table_hbm, table_ref, table_sem)
    table_copy.start()
    for i in range(steps):
        fetch(i).start()
    if early:
        for s in range(early):
            out_refs[s][:, :first, :] = early_ref[s]
    table_copy.wait()

    @pl.loop(0, steps)
    def _(i):
        fetch(i).wait()
        columns = jnp.concatenate(
            [
                traces_ref[i, :, b : b + SUB, :].reshape(samples * SUB, width)
                for b in range(0, step, SUB)
            ],
            axis=1,
        )
        for low in range(0, high, part):
            group = range(low // (2 * SUB), (low + part) // (2 * SUB))
            table = jnp.concatenate(
                [
                    jnp.concatenate(
                        [table_ref[k, place_of(me, s, 2 * SUB, 0, 2 * SUB), :] for s in group],
                        axis=0,
                    )
                    for k in range(tiles)
                ],
                axis=1,
            )
            found = jnp.dot(table, columns, preferred_element_type=F32).astype(BF16)
            for s in group:
                ref, lead, begin = sends[s]
                for c in range(2):
                    row = (2 * s + c) * SUB - low
                    for b in range(step // SUB):
                        spot = pl.ds(pl.multiple_of(begin + i * step + b * SUB, SUB), SUB)
                        out_refs[ref][lead + (c, spot, slice(None))] = found[
                            row : row + SUB, width * b : width * (b + 1)
                        ]


def forward(me, table, traces, first, count, shapes, sends, early):
    samples, _, width = traces.shape
    step = min(2 * SUB, count)
    extra = [] if early is None else [early]
    return pl.pallas_call(
        functools.partial(forward_kernel, first, step, 0 if early is None else early.shape[0], sends),
        in_specs=[pl.BlockSpec(memory_space=pltpu.SMEM)]
        + [pl.BlockSpec(memory_space=pl.ANY)] * 2
        + [pl.BlockSpec(memory_space=pltpu.VMEM)] * len(extra),
        out_specs=[pl.BlockSpec(memory_space=pltpu.VMEM)] * len(shapes),
        scratch_shapes=[
            pltpu.VMEM(table.shape, BF16),
            pltpu.VMEM((count // step, samples, step, width), BF16),
            pltpu.SemaphoreType.DMA,
            pltpu.SemaphoreType.DMA((count // step,)),
        ],
        out_shape=[jax.ShapeDtypeStruct(shape, BF16) for shape in shapes],
        compiler_params=params(),
        cost_estimate=pl.CostEstimate(
            flops=table.shape[1] * 2 * samples * width * count,
            bytes_accessed=2 * samples * count * width,
            transcendentals=0,
        ),
        name="forward",
    )(me, table, traces, *extra)


def tiles_kernel(rows, messages, block, slot_ref, me_ref, own_hbm, other_hbm, *refs):
    in_refs = refs[: len(messages)]
    out_refs = refs[len(messages) : 2 * len(messages)]
    tile_ref, top_ref, low_ref, sum_ref, sems = refs[-5:]
    _, halves, _, size, _ = tile_ref.shape
    width = in_refs[0].shape[-1]
    steps = halves // block
    me = me_ref[0]

    def fetch(which, q):
        source = (own_hbm, other_hbm)[which]
        part = pl.ds(q * block, block)
        return pltpu.make_async_copy(source.at[part], tile_ref.at[which, part], sems.at[which, q])

    for q in range(steps):
        for which in range(2):
            fetch(which, q).start()

    for ref, (s, first, count) in zip(in_refs, messages):
        place = place_of(me, s, rows, first, count)
        top_ref[place, :width] = ref[0]
        top_ref[place, width:] = ref[1]
        low_ref[place, :width] = -ref[1]
        low_ref[place, width:] = ref[0]
    sum_ref[...] = jnp.zeros_like(sum_ref)

    @pl.loop(0, steps)
    def _(q):
        for which in range(2):
            fetch(which, q).wait()
        for k in range(block):
            for which in range(2):
                slot = q * block + k
                column = slot_ref[2 + which, slot]
                place = pl.ds(pl.multiple_of(column * size, size), size)
                pair = jnp.concatenate(
                    [tile_ref[which, slot, 0], tile_ref[which, slot, 1]], axis=1
                )
                weights = jnp.concatenate([top_ref[place, :], low_ref[place, :]], axis=0)
                spot = pl.ds(pl.multiple_of(slot_ref[which, slot] * size, size), size)
                sum_ref[spot, :] += jnp.dot(pair, weights, preferred_element_type=F32)

    for ref, (s, first, count) in zip(out_refs, messages):
        place = place_of(me, s, rows, first, count)
        ref[0] = sum_ref[place, :width].astype(BF16)
        ref[1] = sum_ref[place, width:].astype(BF16)


def apply_tiles(slots, me, own, other, rows, messages, spectra):
    halves, _, size, _ = own.shape
    width = spectra[0].shape[-1]
    total = sum(count for _, _, count in messages)
    block = math.gcd(8, halves)
    return pl.pallas_call(
        functools.partial(tiles_kernel, rows, messages, block),
        in_specs=[pl.BlockSpec(memory_space=pltpu.SMEM)] * 2
        + [pl.BlockSpec(memory_space=pl.ANY)] * 2
        + [pl.BlockSpec(memory_space=pltpu.VMEM)] * len(messages),
        out_specs=[pl.BlockSpec(memory_space=pltpu.VMEM)] * len(messages),
        scratch_shapes=[
            pltpu.VMEM((2,) + own.shape, BF16),
            pltpu.VMEM((total, 2 * width), BF16),
            pltpu.VMEM((total, 2 * width), BF16),
            pltpu.VMEM((total + size, 2 * width), F32),
            pltpu.SemaphoreType.DMA((2, halves // block)),
        ],
        out_shape=[jax.ShapeDtypeStruct((2, count, width), BF16) for _, _, count in messages],
        compiler_params=params(),
        cost_estimate=pl.CostEstimate(
            flops=2 * 2 * halves * size * 4 * size * width,
            bytes_accessed=4 * own.size,
            transcendentals=0,
        ),
        name="tiles",
    )(slots, me, own, other, *spectra)


def inverse_kernel(first, step, offsets, me_ref, table_ref, *refs):
    parties = len(offsets)
    in_refs = refs[:parties]
    out_hbm, column_ref, held_ref, sems = refs[-4:]
    steps, samples, _, width = held_ref.shape
    part = min(4096, samples * SUB)
    me = me_ref[0]

    def send(i):
        return pltpu.make_async_copy(
            held_ref.at[i], out_hbm.at[:, pl.ds(first + i * step, step), :], sems.at[i]
        )

    @pl.loop(0, steps)
    def _(i):
        for s in range(parties):
            for c in range(2):
                for b in range(step // SUB):
                    spot = pl.ds(pl.multiple_of(offsets[s] + i * step + b * SUB, SUB), SUB)
                    column_ref[
                        place_of(me, s, 2 * SUB, c * SUB, SUB), width * b : width * (b + 1)
                    ] = in_refs[s][c, spot, :]
        for low in range(0, samples * SUB, part):
            table = jnp.concatenate(
                [table_ref[k, low : low + part, :] for k in range(table_ref.shape[0])], axis=1
            )
            found = jnp.dot(table, column_ref[...], preferred_element_type=F32).astype(BF16)
            for b in range(step // SUB):
                held_ref[i, low // SUB : (low + part) // SUB, SUB * b : SUB * (b + 1), :] = found[
                    :, width * b : width * (b + 1)
                ].reshape(part // SUB, SUB, width)
        send(i).start()

    for i in range(steps):
        send(i).wait()


def inverse(me, table, blocks, offsets, first, count, rows, filled):
    width = blocks[0].shape[-1]
    samples = table.shape[1] // SUB
    step = min(2 * SUB, count)
    extra = [] if filled is None else [filled]
    return pl.pallas_call(
        functools.partial(inverse_kernel, first, step, offsets),
        in_specs=[pl.BlockSpec(memory_space=pltpu.SMEM)]
        + [pl.BlockSpec(memory_space=pltpu.VMEM)] * (1 + len(blocks))
        + [pl.BlockSpec(memory_space=pl.ANY)] * len(extra),
        out_specs=pl.BlockSpec(memory_space=pl.ANY),
        scratch_shapes=[
            pltpu.VMEM((len(blocks) * 2 * SUB, step // SUB * width), BF16),
            pltpu.VMEM((count // step, samples, step, width), BF16),
            pltpu.SemaphoreType.DMA((count // step,)),
        ],
        out_shape=jax.ShapeDtypeStruct((samples, rows, width), BF16),
        input_output_aliases={2 + len(blocks): 0} if extra else {},
        compiler_params=params(),
        cost_estimate=pl.CostEstimate(
            flops=len(blocks) * 4 * SUB * samples * width * count,
            bytes_accessed=2 * samples * count * width,
            transcendentals=0,
        ),
        name="inverse",
    )(me, table, *blocks, *extra)


def send(block, s, parties):
    if s == 0:
        return block
    return lax.ppermute(block, "wide", [(k, k ^ s) for k in range(parties)])


def cuts(rows, sizes):
    if rows % (sum(sizes) * 2 * SUB):
        return ((0, rows),)
    unit = rows // sum(sizes)
    return tuple((unit * sum(sizes[:i]), unit * n) for i, n in enumerate(sizes))


def shards(traces, row_counts, tile_cols, tiles):
    samples, rows, width = traces.shape
    parties = lax.axis_size("wide")
    halves = tiles.shape[1]
    forward_table, inverse_table = transform_tables(samples, parties)
    side = lax.axis_index("narrow").astype(jnp.int32)
    me = lax.axis_index("wide").astype(jnp.int32).reshape(1)
    chunks = cuts(rows, CUTS)
    near = parties // 2
    whole = [(s, 0, rows) for s in range(near)]
    far = [[(s, first, count) for s in range(near, parties)] for first, count in chunks]
    messages = [m for part in far for m in part] + whole[::-1]

    other = lax.ppermute(tiles[0], "narrow", [(0, 1), (1, 0)])
    ends = jnp.cumsum(row_counts[0])
    slot_ids = jnp.arange(2 * halves, dtype=jnp.int32)
    slot_rows = jnp.sum((ends[None, :] <= slot_ids[:, None]).astype(jnp.int32), axis=1)
    columns = jnp.clip(tile_cols[0], 0, row_counts.shape[1] - 1)
    turn = lambda a: jnp.where(side == 0, a.reshape(2, halves), a.reshape(2, halves)[::-1])
    slots = jnp.concatenate([turn(slot_rows), turn(columns)], axis=0)

    got = {}
    early = None
    for q, (first, count) in enumerate(chunks):
        last = q == len(chunks) - 1
        shapes = [(2, rows, width)] * near if last else [(near, 2, first + count, width)]
        sends = [(s, (), first) if last else (0, (s,), first) for s in range(near)]
        sends += [(len(shapes) + k, (), 0) for k in range(parties - near)]
        shapes += [(2, count, width)] * (parties - near)
        found = forward(me, forward_table, traces, first, count, shapes, sends, early)
        early = None if last else found[0]
        for m, block in zip(far[q], found[-(parties - near) :]):
            got[m] = send(block, m[0], parties)
        if last:
            for m, block in list(zip(whole, found))[::-1]:
                got[m] = send(block, m[0], parties)

    found = apply_tiles(slots, me, tiles[0], other, rows, messages, [got[m] for m in messages])
    got = {m: send(block, m[0], parties) for m, block in zip(messages, found)}
    result = None
    for (first, count), part in zip(chunks, far):
        blocks = [got[m] for m in whole + part]
        offsets = [first] * near + [0] * (parties - near)
        result = inverse(me, inverse_table, blocks, offsets, first, count, rows, result)
    return result


def solution(mesh):
    in_specs = (
        P(None, ("groups", "wide"), "narrow"),
        P(("groups", "wide"), None),
        P(("groups", "wide"), None),
        P(("groups", "wide"), "narrow", None, None, None),
    )
    out_specs = P(None, ("groups", "wide"), "narrow")
    return jax.shard_map(shards, mesh=mesh, in_specs=in_specs, out_specs=out_specs, check_vma=False)
```

time: 224 us -> 81.5 us (0.36)
  local copies, waits for them, and re-layouts: 62.1 us -> 0.97 us
  matrix products: 56.1 us -> 0 us
  waiting for transfers between devices: 46 us -> 12.9 us
  blocking collectives: 32.8 us -> 0 us
  starting transfers between devices: 6 us -> 38.6 us
  Pallas kernels: 0 us -> 28.4 us
  between operations: 13.5 us -> 0.12 us
  other arithmetic: 6.5 us -> 0.27 us
    dot_general x12 -> x0, matrix products: 56.1 us -> none  [the longest x5 23.2 us: add_block(): return running + jnp.einsum('kr,ckiv->criv', weights, slot_terms)]
    ppermute x0 -> x23, starting transfers between devices: none -> 38.6 us  [the longest x22 38.1 us: send(): return lax.ppermute(block, 'wide', [(k, k ^ s) for k in range(parties)])]
    all_to_all x1 -> x0, blocking collectives: 32.8 us -> none  [shards(): lax.all_to_all(spectra, 'wide', split_axis=0, concat_axis=2, tiled=True)[0]]
    pallas_call x0 -> x5, Pallas kernels: none -> 28.4 us  [the longest x2 11.8 us: inverse(): pl.pallas_call(functools.partial(inverse_kernel, first, step, offsets), i...]
    all_to_all x1 -> x0, waiting for transfers between devices: 26.1 us -> none  [shards(): lax.all_to_all(summed[None], 'wide', split_axis=2, concat_axis=0, tiled=T...]
    convert_element_type x2 -> x0, local copies, waits for them, and re-layouts: 17.6 us -> none  [the longest x1 17.4 us: shards(): return redatumed.astype(jnp.bfloat16)]
    ppermute x0 -> x23, waiting for transfers between devices: none -> 12.9 us  [the longest x22 12.9 us: send(): return lax.ppermute(block, 'wide', [(k, k ^ s) for k in range(parties)])]
    gather x5 -> x0, local copies, waits for them, and re-layouts: 11 us -> none  [add_block(): picked = jnp.take(blocks, column_ids, axis=1)]
  transfers between devices with their start and end apart: 3 -> 23, of which waited for: 3 -> 6; matrix products, arithmetic and copies ran while one was open for 0% -> 1% of each run, Pallas kernels for 0% -> 21%
where the time goes in v2:
time: 81.5 us; the launch traced here: 81.3 us
  starting transfers between devices  38.6 us (47%)
  Pallas kernels  28.4 us (35%)
  waiting for transfers between devices  12.9 us (16%)
  local copies, waits for them, and re-layouts  0.97 us (1%)
    ppermute x22, starting transfers between devices, send(): return lax.ppermute(block, 'wide', [(k, k ^ s) for k in range(parties)])  38.1 us
    ppermute x22, waiting for transfers between devices, send(): return lax.ppermute(block, 'wide', [(k, k ^ s) for k in range(parties)])  12.9 us
    pallas_call x2, Pallas kernels, inverse(): pl.pallas_call(functools.partial(inverse_kernel, first, step, offsets), i...  11.8 us
    pallas_call x2, Pallas kernels, forward(): pl.pallas_call(functools.partial(forward_kernel, first, step, 0 if early...  11.6 us
    pallas_call x1, Pallas kernels, apply_tiles(): pl.pallas_call(functools.partial(tiles_kernel, rows, messages, block), in...  5.06 us
  transfers between devices with their start and end apart: 23, of which 6 were waited for; matrix products, arithmetic and copies ran while one was open for 1% of the time, Pallas kernels for 21%

profile of v2, /device:TPU:0, one launch (start us, length us, event | category | flops | bytes accessed | tf_op | source)
XLA Modules:
  0.0 81.3 jit_solution(12193951178211112770)
XLA Ops:
  0.0 0.5 collective-permute-start
  0.5 6.4 %forward.2 = (bf16[4,2,128,128]{3,2,1,0:T(8,128)(2,1)S(1)}, bf16[2,128,128]{2,1,0:T(8,128)(2,1)S(1)}, bf16[2,128,128]{2,1,0:T(8,128)(2,1)S(1)}, bf16[2,128,128]{2,1,0:T(8,128)(2,1)S(1)}, bf16[2,128,128]{2,1,0:T(8,128)(2,1)S(1)}) custom-call(s32[1]{0:T(128)} %bitcast.me_ref, bf16[32,256,128]{2,1,0:T(8,128)(2,1)} %constant.19.clone.table_hbm, ...), custom_call_target="tpu_custom_call" | custom-call | flops 2147483648 | bytes 8388608 | tf_op jit(solution)/shard_map/forward/pallas_call | solution.py:110
  6.9 3.7 %collective-permute-start.1 = (bf16[2,128,128]{2,1,0:T(8,128)(2,1)S(1)}, bf16[2,128,128]{2,1,0:T(8,128)(2,1)S(1)}, u32[]{:S(2)}, u32[]{:S(2)}) collective-permute-start(bf16[2,128,128]{2,1,0:T(8,128)(2,1)S(1)} %get-tuple-element.30), channel_id=1, source_target_pairs={{0,8},{2,10},{4,12},{6,14},{8,0},{10,2},{12,4},{14,6},{1,9},{3,11}... | collective-permute-start | bytes 196616 | tf_op jit(solution)/shard_map/ppermute | solution.py:278
  10.5 1.3 %collective-permute-start.2 = (bf16[2,128,128]{2,1,0:T(8,128)(2,1)S(1)}, bf16[2,128,128]{2,1,0:T(8,128)(2,1)S(1)}, u32[]{:S(2)}, u32[]{:S(2)}) collective-permute-start(bf16[2,128,128]{2,1,0:T(8,128)(2,1)S(1)} %get-tuple-element.31), channel_id=1, source_target_pairs={{0,10},{2,8},{4,14},{6,12},{8,2},{10,0},{12,6},{14,4},{1,11},{3,9}... | collective-permute-start | bytes 196616 | tf_op jit(solution)/shard_map/ppermute | solution.py:278
  11.8 3.6 %collective-permute-start.3 = (bf16[2,128,128]{2,1,0:T(8,128)(2,1)S(1)}, bf16[2,128,128]{2,1,0:T(8,128)(2,1)S(1)}, u32[]{:S(2)}, u32[]{:S(2)}) collective-permute-start(bf16[2,128,128]{2,1,0:T(8,128)(2,1)S(1)} %get-tuple-element.32), channel_id=1, source_target_pairs={{0,12},{2,14},{4,8},{6,10},{8,4},{10,6},{12,0},{14,2},{1,13},{3,15... | collective-permute-start | bytes 196616 | tf_op jit(solution)/shard_map/ppermute | solution.py:278
  15.4 5.2 %forward.3 = (bf16[2,256,128]{2,1,0:T(8,128)(2,1)S(1)}, bf16[2,256,128]{2,1,0:T(8,128)(2,1)S(1)}, bf16[2,256,128]{2,1,0:T(8,128)(2,1)S(1)}, bf16[2,256,128]{2,1,...) custom-call(s32[1]{0:T(128)} %bitcast.me_ref, ...), custom_call_target="tpu_custom_call" | custom-call | flops 2147483648 | bytes 8388608 | tf_op jit(solution)/shard_map/forward/pallas_call | solution.py:110
  20.6 0.6 copy-done
  21.3 0.1 min.12
  21.5 0.1 reduce
  21.6 1.0 %collective-permute-start.5 = (bf16[2,128,128]{2,1,0:T(8,128)(2,1)S(1)}, bf16[2,128,128]{2,1,0:T(8,128)(2,1)S(1)}, u32[]{:S(2)}, u32[]{:S(2)}) collective-permute-start(bf16[2,128,128]{2,1,0:T(8,128)(2,1)S(1)} %get-tuple-element.35), channel_id=1, source_target_pairs={{0,8},{2,10},{4,12},{6,14},{8,0},{10,2},{12,4},{14,6},{1,9},{3,11}... | collective-permute-start | bytes 196616 | tf_op jit(solution)/shard_map/ppermute | solution.py:278
  22.6 3.1 %collective-permute-start.6 = (bf16[2,128,128]{2,1,0:T(8,128)(2,1)S(1)}, bf16[2,128,128]{2,1,0:T(8,128)(2,1)S(1)}, u32[]{:S(2)}, u32[]{:S(2)}) collective-permute-start(bf16[2,128,128]{2,1,0:T(8,128)(2,1)S(1)} %get-tuple-element.36), channel_id=1, source_target_pairs={{0,10},{2,8},{4,14},{6,12},{8,2},{10,0},{12,6},{14,4},{1,11},{3,9}... | collective-permute-start | bytes 196616 | tf_op jit(solution)/shard_map/ppermute | solution.py:278
  25.7 0.1 convert_reduce_fusion
  26.0 3.7 %collective-permute-start.7 = (bf16[2,128,128]{2,1,0:T(8,128)(2,1)S(1)}, bf16[2,128,128]{2,1,0:T(8,128)(2,1)S(1)}, u32[]{:S(2)}, u32[]{:S(2)}) collective-permute-start(bf16[2,128,128]{2,1,0:T(8,128)(2,1)S(1)} %get-tuple-element.37), channel_id=1, source_target_pairs={{0,12},{2,14},{4,8},{6,10},{8,4},{10,6},{12,0},{14,2},{1,13},{3,15... | collective-permute-start | bytes 196616 | tf_op jit(solution)/shard_map/ppermute | solution.py:278
  29.6 2.0 %collective-permute-start.10 = (bf16[2,256,128]{2,1,0:T(8,128)(2,1)S(1)}, bf16[2,256,128]{2,1,0:T(8,128)(2,1)S(1)}, u32[]{:S(2)}, u32[]{:S(2)}) collective-permute-start(bf16[2,256,128]{2,1,0:T(8,128)(2,1)S(1)} %get-tuple-element.40), channel_id=1, source_target_pairs={{0,4},{2,6},{4,0},{6,2},{8,12},{10,14},{12,8},{14,10},{1,5},{3,7},... | collective-permute-start | bytes 393224 | tf_op jit(solution)/shard_map/ppermute | solution.py:278
  31.6 1.8 %collective-permute-done.6.refs_5_ = bf16[2,128,128]{2,1,0:T(8,128)(2,1)S(1)} collective-permute-done((bf16[2,128,128]{2,1,0:T(8,128)(2,1)S(1)}, bf16[2,128,128]{2,1,0:T(8,128)(2,1)S(1)}, u32[]{:S(2)}, u32[]{:S(2)}) %collective-permute-start.6) | collective-permute-done | bytes 65568 | tf_op jit(solution)/shard_map/ppermute | solution.py:278
  33.3 0.4 collective-permute-done.7.refs_6_
  33.8 3.2 %collective-permute-start.8 = (bf16[2,128,128]{2,1,0:T(8,128)(2,1)S(1)}, bf16[2,128,128]{2,1,0:T(8,128)(2,1)S(1)}, u32[]{:S(2)}, u32[]{:S(2)}) collective-permute-start(bf16[2,128,128]{2,1,0:T(8,128)(2,1)S(1)} %get-tuple-element.38), channel_id=1, source_target_pairs={{0,14},{2,12},{4,10},{6,8},{8,6},{10,4},{12,2},{14,0},{1,15},{3,13... | collective-permute-start | bytes 196616 | tf_op jit(solution)/shard_map/ppermute | solution.py:278
  37.0 3.7 %collective-permute-done.8.refs_7_ = bf16[2,128,128]{2,1,0:T(8,128)(2,1)S(1)} collective-permute-done((bf16[2,128,128]{2,1,0:T(8,128)(2,1)S(1)}, bf16[2,128,128]{2,1,0:T(8,128)(2,1)S(1)}, u32[]{:S(2)}, u32[]{:S(2)}) %collective-permute-start.8) | collective-permute-done | bytes 65568 | tf_op jit(solution)/shard_map/ppermute | solution.py:278
  40.7 5.1 %tiles.1 = (bf16[2,128,128]{2,1,0:T(8,128)(2,1)S(1)}, bf16[2,128,128]{2,1,0:T(8,128)(2,1)S(1)}, bf16[2,128,128]{2,1,0:T(8,128)(2,1)S(1)}, bf16[2,128,128]{2,1,0:...) custom-call(s32[4,40]{1,0:T(4,128)S(1)} %pad_add_fusion.slot_ref, ...), custom_call_target="tpu_custom_call" | custom-call | flops 1342177280 | bytes 5242880 | tf_op jit(solution)/shard_map/tiles/pallas_call | solution.py:186
  45.9 4.0 %collective-permute-start.20 = (bf16[2,128,128]{2,1,0:T(8,128)(2,1)S(1)}, bf16[2,128,128]{2,1,0:T(8,128)(2,1)S(1)}, u32[]{:S(2)}, u32[]{:S(2)}) collective-permute-start(bf16[2,128,128]{2,1,0:T(8,128)(2,1)S(1)} %get-tuple-element.52), channel_id=1, source_target_pairs={{0,10},{2,8},{4,14},{6,12},{8,2},{10,0},{12,6},{14,4},{1,11},{3,9}... | collective-permute-start | bytes 196616 | tf_op jit(solution)/shard_map/ppermute | solution.py:278
  49.9 0.4 collective-permute-start.12
  50.3 0.4 collective-permute-start.13
  50.7 2.7 %collective-permute-start.14 = (bf16[2,256,128]{2,1,0:T(8,128)(2,1)S(1)}, bf16[2,256,128]{2,1,0:T(8,128)(2,1)S(1)}, u32[]{:S(2)}, u32[]{:S(2)}) collective-permute-start(bf16[2,256,128]{2,1,0:T(8,128)(2,1)S(1)} %get-tuple-element.46), channel_id=1, source_target_pairs={{0,6},{2,4},{4,2},{6,0},{8,14},{10,12},{12,10},{14,8},{1,7},{3,5},... | collective-permute-start | bytes 393224 | tf_op jit(solution)/shard_map/ppermute | solution.py:278
  53.4 2.2 %collective-permute-start.21 = (bf16[2,128,128]{2,1,0:T(8,128)(2,1)S(1)}, bf16[2,128,128]{2,1,0:T(8,128)(2,1)S(1)}, u32[]{:S(2)}, u32[]{:S(2)}) collective-permute-start(bf16[2,128,128]{2,1,0:T(8,128)(2,1)S(1)} %get-tuple-element.53), channel_id=1, source_target_pairs={{0,12},{2,14},{4,8},{6,10},{8,4},{10,6},{12,0},{14,2},{1,13},{3,15... | collective-permute-start | bytes 196616 | tf_op jit(solution)/shard_map/ppermute | solution.py:278
  55.6 1.5 %collective-permute-start.22 = (bf16[2,128,128]{2,1,0:T(8,128)(2,1)S(1)}, bf16[2,128,128]{2,1,0:T(8,128)(2,1)S(1)}, u32[]{:S(2)}, u32[]{:S(2)}) collective-permute-start(bf16[2,128,128]{2,1,0:T(8,128)(2,1)S(1)} %get-tuple-element.54), channel_id=1, source_target_pairs={{0,14},{2,12},{4,10},{6,8},{8,6},{10,4},{12,2},{14,0},{1,15},{3,13... | collective-permute-start | bytes 196616 | tf_op jit(solution)/shard_map/ppermute | solution.py:278
  57.0 3.5 %collective-permute-done.21.refs_6_ = bf16[2,128,128]{2,1,0:T(8,128)(2,1)S(1)} collective-permute-done((bf16[2,128,128]{2,1,0:T(8,128)(2,1)S(1)}, bf16[2,128,128]{2,1,0:T(8,128)(2,1)S(1)}, u32[]{:S(2)}, u32[]{:S(2)}) %collective-permute-start.21) | collective-permute-done | bytes 65568 | tf_op jit(solution)/shard_map/ppermute | solution.py:278
  60.6 2.4 %collective-permute-done.22.refs_7_ = bf16[2,128,128]{2,1,0:T(8,128)(2,1)S(1)} collective-permute-done((bf16[2,128,128]{2,1,0:T(8,128)(2,1)S(1)}, bf16[2,128,128]{2,1,0:T(8,128)(2,1)S(1)}, u32[]{:S(2)}, u32[]{:S(2)}) %collective-permute-start.22) | collective-permute-done | bytes 65568 | tf_op jit(solution)/shard_map/ppermute | solution.py:278
  63.0 2.5 %collective-permute-start.16 = (bf16[2,128,128]{2,1,0:T(8,128)(2,1)S(1)}, bf16[2,128,128]{2,1,0:T(8,128)(2,1)S(1)}, u32[]{:S(2)}, u32[]{:S(2)}) collective-permute-start(bf16[2,128,128]{2,1,0:T(8,128)(2,1)S(1)} %get-tuple-element.48), channel_id=1, source_target_pairs={{0,10},{2,8},{4,14},{6,12},{8,2},{10,0},{12,6},{14,4},{1,11},{3,9}... | collective-permute-start | bytes 196616 | tf_op jit(solution)/shard_map/ppermute | solution.py:278
  65.5 3.0 %collective-permute-start.17 = (bf16[2,128,128]{2,1,0:T(8,128)(2,1)S(1)}, bf16[2,128,128]{2,1,0:T(8,128)(2,1)S(1)}, u32[]{:S(2)}, u32[]{:S(2)}) collective-permute-start(bf16[2,128,128]{2,1,0:T(8,128)(2,1)S(1)} %get-tuple-element.49), channel_id=1, source_target_pairs={{0,12},{2,14},{4,8},{6,10},{8,4},{10,6},{12,0},{14,2},{1,13},{3,15... | collective-permute-start | bytes 196616 | tf_op jit(solution)/shard_map/ppermute | solution.py:278
  68.4 5.9 %inverse.2.refs_8_ = bf16[256,256,128]{2,1,0:T(8,128)(2,1)} custom-call(s32[1]{0:T(128)} %bitcast.me_ref, bf16[2,4096,128]{2,1,0:T(8,128)(2,1)} %constant.20.clone.table_ref, bf16[2,256,128]{2,1,0:T(8,128)(2,1)S(1)} %get-tuple-element.43.refs_0_, bf16[2,256,128]{2,1,0:T(8,128)(2,1)S(1)} %collective-permute-done.12.refs_1_, ...), custom_call_target="tpu_custom_call" | custom-call | flops 2147483648 | bytes 8388608 | tf_op jit(solution)/shard_map/inverse/pallas_call | solution.py:252
  74.4 1.0 %collective-permute-done.18.refs_7_ = bf16[2,128,128]{2,1,0:T(8,128)(2,1)S(1)} collective-permute-done((bf16[2,128,128]{2,1,0:T(8,128)(2,1)S(1)}, bf16[2,128,128]{2,1,0:T(8,128)(2,1)S(1)}, u32[]{:S(2)}, u32[]{:S(2)}) %collective-permute-start.18) | collective-permute-done | bytes 65568 | tf_op jit(solution)/shard_map/ppermute | solution.py:278
  75.4 5.9 %inverse.3 = bf16[256,256,128]{2,1,0:T(8,128)(2,1)} custom-call(s32[1]{0:T(128)} %bitcast.me_ref, bf16[2,4096,128]{2,1,0:T(8,128)(2,1)} %constant.20.clone.table_ref, bf16[2,256,128]{2,1,0:T(8,128)(2,1)S(1)} %get-tuple-element.43.refs_0_, bf16[2,256,128]{2,1,0:T(8,128)(2,1)S(1)} %collective-permute-done.12.refs_1_, ...), custom_call_target="tpu_custom_call", output_to_operand_aliasing={{}: (10, {})} | custom-call | flops 2147483648 | bytes 8388608 | tf_op jit(solution)/shard_map/inverse/pallas_call | solution.py:252
  (36 shorter events, 0.4 us)
Async XLA Ops:
  0.0 40.7 %collective-permute-start = (bf16[40,2,128,128]{3,2,1,0:T(8,128)(2,1)}, bf16[40,2,128,128]{3,2,1,0:T(8,128)(2,1)}, u32[]{:S(2)}, u32[]{:S(2)}) collective-permute-start(bf16[40,2,128,128]{3,2,1,0:T(8,128)(2,1)} %bitcast.3), channel_id=1, source_target_pairs={{0,1},{1,0},{2,3},{3,2},{4,5},{5,4},{6,7},{7,6},{8,9},{9,8},{10,11... | collective-permute-start | bytes 7864328 | tf_op jit(solution)/shard_map/ppermute | solution.py:301
  6.9 14.7 %collective-permute-start.1 = (bf16[2,128,128]{2,1,0:T(8,128)(2,1)S(1)}, bf16[2,128,128]{2,1,0:T(8,128)(2,1)S(1)}, u32[]{:S(2)}, u32[]{:S(2)}) collective-permute-start(bf16[2,128,128]{2,1,0:T(8,128)(2,1)S(1)} %get-tuple-element.30), channel_id=1, source_target_pairs={{0,8},{2,10},{4,12},{6,14},{8,0},{10,2},{12,4},{14,6},{1,9},{3,11}... | collective-permute-start | bytes 196616 | tf_op jit(solution)/shard_map/ppermute | solution.py:278
  10.5 12.1 %collective-permute-start.2 = (bf16[2,128,128]{2,1,0:T(8,128)(2,1)S(1)}, bf16[2,128,128]{2,1,0:T(8,128)(2,1)S(1)}, u32[]{:S(2)}, u32[]{:S(2)}) collective-permute-start(bf16[2,128,128]{2,1,0:T(8,128)(2,1)S(1)} %get-tuple-element.31), channel_id=1, source_target_pairs={{0,10},{2,8},{4,14},{6,12},{8,2},{10,0},{12,6},{14,4},{1,11},{3,9}... | collective-permute-start | bytes 196616 | tf_op jit(solution)/shard_map/ppermute | solution.py:278
  11.8 14.2 %collective-permute-start.3 = (bf16[2,128,128]{2,1,0:T(8,128)(2,1)S(1)}, bf16[2,128,128]{2,1,0:T(8,128)(2,1)S(1)}, u32[]{:S(2)}, u32[]{:S(2)}) collective-permute-start(bf16[2,128,128]{2,1,0:T(8,128)(2,1)S(1)} %get-tuple-element.32), channel_id=1, source_target_pairs={{0,12},{2,14},{4,8},{6,10},{8,4},{10,6},{12,0},{14,2},{1,13},{3,15... | collective-permute-start | bytes 196616 | tf_op jit(solution)/shard_map/ppermute | solution.py:278
  15.4 14.2 %collective-permute-start.4 = (bf16[2,128,128]{2,1,0:T(8,128)(2,1)S(1)}, bf16[2,128,128]{2,1,0:T(8,128)(2,1)S(1)}, u32[]{:S(2)}, u32[]{:S(2)}) collective-permute-start(bf16[2,128,128]{2,1,0:T(8,128)(2,1)S(1)} %get-tuple-element.33), channel_id=1, source_target_pairs={{0,14},{2,12},{4,10},{6,8},{8,6},{10,4},{12,2},{14,0},{1,15},{3,13... | collective-permute-start | bytes 196616 | tf_op jit(solution)/shard_map/ppermute | solution.py:278
  15.4 5.8 %copy-start.2 = (s32[1,80]{1,0:T(1,128)S(1)}, s32[1,80]{1,0:T(1,128)}, u32[]{:S(2)}) copy-start(s32[1,80]{1,0:T(1,128)} %param.8) | copy-start | bytes 964
  15.4 6.0 %copy-start.1 = (s32[1,16]{1,0:T(1,128)S(1)}, s32[1,16]{1,0:T(1,128)}, u32[]{:S(2)}) copy-start(s32[1,16]{1,0:T(1,128)} %param.7) | copy-start | bytes 196
  20.6 0.7 copy-start
  21.6 8.0 %collective-permute-start.5 = (bf16[2,128,128]{2,1,0:T(8,128)(2,1)S(1)}, bf16[2,128,128]{2,1,0:T(8,128)(2,1)S(1)}, u32[]{:S(2)}, u32[]{:S(2)}) collective-permute-start(bf16[2,128,128]{2,1,0:T(8,128)(2,1)S(1)} %get-tuple-element.35), channel_id=1, source_target_pairs={{0,8},{2,10},{4,12},{6,14},{8,0},{10,2},{12,4},{14,6},{1,9},{3,11}... | collective-permute-start | bytes 196616 | tf_op jit(solution)/shard_map/ppermute | solution.py:278
  22.6 10.7 %collective-permute-start.6 = (bf16[2,128,128]{2,1,0:T(8,128)(2,1)S(1)}, bf16[2,128,128]{2,1,0:T(8,128)(2,1)S(1)}, u32[]{:S(2)}, u32[]{:S(2)}) collective-permute-start(bf16[2,128,128]{2,1,0:T(8,128)(2,1)S(1)} %get-tuple-element.36), channel_id=1, source_target_pairs={{0,10},{2,8},{4,14},{6,12},{8,2},{10,0},{12,6},{14,4},{1,11},{3,9}... | collective-permute-start | bytes 196616 | tf_op jit(solution)/shard_map/ppermute | solution.py:278
  26.0 7.8 %collective-permute-start.7 = (bf16[2,128,128]{2,1,0:T(8,128)(2,1)S(1)}, bf16[2,128,128]{2,1,0:T(8,128)(2,1)S(1)}, u32[]{:S(2)}, u32[]{:S(2)}) collective-permute-start(bf16[2,128,128]{2,1,0:T(8,128)(2,1)S(1)} %get-tuple-element.37), channel_id=1, source_target_pairs={{0,12},{2,14},{4,8},{6,10},{8,4},{10,6},{12,0},{14,2},{1,13},{3,15... | collective-permute-start | bytes 196616 | tf_op jit(solution)/shard_map/ppermute | solution.py:278
  29.6 11.1 %collective-permute-start.9 = (bf16[2,256,128]{2,1,0:T(8,128)(2,1)S(1)}, bf16[2,256,128]{2,1,0:T(8,128)(2,1)S(1)}, u32[]{:S(2)}, u32[]{:S(2)}) collective-permute-start(bf16[2,256,128]{2,1,0:T(8,128)(2,1)S(1)} %get-tuple-element.39), channel_id=1, source_target_pairs={{0,6},{2,4},{4,2},{6,0},{8,14},{10,12},{12,10},{14,8},{1,7},{3,5},... | collective-permute-start | bytes 393224 | tf_op jit(solution)/shard_map/ppermute | solution.py:278
  29.6 11.1 %collective-permute-start.10 = (bf16[2,256,128]{2,1,0:T(8,128)(2,1)S(1)}, bf16[2,256,128]{2,1,0:T(8,128)(2,1)S(1)}, u32[]{:S(2)}, u32[]{:S(2)}) collective-permute-start(bf16[2,256,128]{2,1,0:T(8,128)(2,1)S(1)} %get-tuple-element.40), channel_id=1, source_target_pairs={{0,4},{2,6},{4,0},{6,2},{8,12},{10,14},{12,8},{14,10},{1,5},{3,7},... | collective-permute-start | bytes 393224 | tf_op jit(solution)/shard_map/ppermute | solution.py:278
  33.3 7.4 %collective-permute-start.11 = (bf16[2,256,128]{2,1,0:T(8,128)(2,1)S(1)}, bf16[2,256,128]{2,1,0:T(8,128)(2,1)S(1)}, u32[]{:S(2)}, u32[]{:S(2)}) collective-permute-start(bf16[2,256,128]{2,1,0:T(8,128)(2,1)S(1)} %get-tuple-element.41), channel_id=1, source_target_pairs={{0,2},{2,0},{4,6},{6,4},{8,10},{10,8},{12,14},{14,12},{1,3},{3,1},... | collective-permute-start | bytes 393224 | tf_op jit(solution)/shard_map/ppermute | solution.py:278
  33.8 7.0 %collective-permute-start.8 = (bf16[2,128,128]{2,1,0:T(8,128)(2,1)S(1)}, bf16[2,128,128]{2,1,0:T(8,128)(2,1)S(1)}, u32[]{:S(2)}, u32[]{:S(2)}) collective-permute-start(bf16[2,128,128]{2,1,0:T(8,128)(2,1)S(1)} %get-tuple-element.38), channel_id=1, source_target_pairs={{0,14},{2,12},{4,10},{6,8},{8,6},{10,4},{12,2},{14,0},{1,15},{3,13... | collective-permute-start | bytes 196616 | tf_op jit(solution)/shard_map/ppermute | solution.py:278
  45.8 7.6 %collective-permute-start.19 = (bf16[2,128,128]{2,1,0:T(8,128)(2,1)S(1)}, bf16[2,128,128]{2,1,0:T(8,128)(2,1)S(1)}, u32[]{:S(2)}, u32[]{:S(2)}) collective-permute-start(bf16[2,128,128]{2,1,0:T(8,128)(2,1)S(1)} %get-tuple-element.51), channel_id=1, source_target_pairs={{0,8},{2,10},{4,12},{6,14},{8,0},{10,2},{12,4},{14,6},{1,9},{3,11}... | collective-permute-start | bytes 196616 | tf_op jit(solution)/shard_map/ppermute | solution.py:278
  45.9 9.7 %collective-permute-start.20 = (bf16[2,128,128]{2,1,0:T(8,128)(2,1)S(1)}, bf16[2,128,128]{2,1,0:T(8,128)(2,1)S(1)}, u32[]{:S(2)}, u32[]{:S(2)}) collective-permute-start(bf16[2,128,128]{2,1,0:T(8,128)(2,1)S(1)} %get-tuple-element.52), channel_id=1, source_target_pairs={{0,10},{2,8},{4,14},{6,12},{8,2},{10,0},{12,6},{14,4},{1,11},{3,9}... | collective-permute-start | bytes 196616 | tf_op jit(solution)/shard_map/ppermute | solution.py:278
  49.9 15.6 %collective-permute-start.12 = (bf16[2,256,128]{2,1,0:T(8,128)(2,1)S(1)}, bf16[2,256,128]{2,1,0:T(8,128)(2,1)S(1)}, u32[]{:S(2)}, u32[]{:S(2)}) collective-permute-start(bf16[2,256,128]{2,1,0:T(8,128)(2,1)S(1)} %get-tuple-element.44), channel_id=1, source_target_pairs={{0,2},{2,0},{4,6},{6,4},{8,10},{10,8},{12,14},{14,12},{1,3},{3,1},... | collective-permute-start | bytes 393224 | tf_op jit(solution)/shard_map/ppermute | solution.py:278
  50.3 18.1 %collective-permute-start.13 = (bf16[2,256,128]{2,1,0:T(8,128)(2,1)S(1)}, bf16[2,256,128]{2,1,0:T(8,128)(2,1)S(1)}, u32[]{:S(2)}, u32[]{:S(2)}) collective-permute-start(bf16[2,256,128]{2,1,0:T(8,128)(2,1)S(1)} %get-tuple-element.45), channel_id=1, source_target_pairs={{0,4},{2,6},{4,0},{6,2},{8,12},{10,14},{12,8},{14,10},{1,5},{3,7},... | collective-permute-start | bytes 393224 | tf_op jit(solution)/shard_map/ppermute | solution.py:278
  50.7 17.7 %collective-permute-start.14 = (bf16[2,256,128]{2,1,0:T(8,128)(2,1)S(1)}, bf16[2,256,128]{2,1,0:T(8,128)(2,1)S(1)}, u32[]{:S(2)}, u32[]{:S(2)}) collective-permute-start(bf16[2,256,128]{2,1,0:T(8,128)(2,1)S(1)} %get-tuple-element.46), channel_id=1, source_target_pairs={{0,6},{2,4},{4,2},{6,0},{8,14},{10,12},{12,10},{14,8},{1,7},{3,5},... | collective-permute-start | bytes 393224 | tf_op jit(solution)/shard_map/ppermute | solution.py:278
  53.4 7.2 %collective-permute-start.21 = (bf16[2,128,128]{2,1,0:T(8,128)(2,1)S(1)}, bf16[2,128,128]{2,1,0:T(8,128)(2,1)S(1)}, u32[]{:S(2)}, u32[]{:S(2)}) collective-permute-start(bf16[2,128,128]{2,1,0:T(8,128)(2,1)S(1)} %get-tuple-element.53), channel_id=1, source_target_pairs={{0,12},{2,14},{4,8},{6,10},{8,4},{10,6},{12,0},{14,2},{1,13},{3,15... | collective-permute-start | bytes 196616 | tf_op jit(solution)/shard_map/ppermute | solution.py:278
  55.6 7.4 %collective-permute-start.22 = (bf16[2,128,128]{2,1,0:T(8,128)(2,1)S(1)}, bf16[2,128,128]{2,1,0:T(8,128)(2,1)S(1)}, u32[]{:S(2)}, u32[]{:S(2)}) collective-permute-start(bf16[2,128,128]{2,1,0:T(8,128)(2,1)S(1)} %get-tuple-element.54), channel_id=1, source_target_pairs={{0,14},{2,12},{4,10},{6,8},{8,6},{10,4},{12,2},{14,0},{1,15},{3,13... | collective-permute-start | bytes 196616 | tf_op jit(solution)/shard_map/ppermute | solution.py:278
  60.6 13.8 %collective-permute-start.15 = (bf16[2,128,128]{2,1,0:T(8,128)(2,1)S(1)}, bf16[2,128,128]{2,1,0:T(8,128)(2,1)S(1)}, u32[]{:S(2)}, u32[]{:S(2)}) collective-permute-start(bf16[2,128,128]{2,1,0:T(8,128)(2,1)S(1)} %get-tuple-element.47), channel_id=1, source_target_pairs={{0,8},{2,10},{4,12},{6,14},{8,0},{10,2},{12,4},{14,6},{1,9},{3,11}... | collective-permute-start | bytes 196616 | tf_op jit(solution)/shard_map/ppermute | solution.py:278
  63.0 11.4 %collective-permute-start.16 = (bf16[2,128,128]{2,1,0:T(8,128)(2,1)S(1)}, bf16[2,128,128]{2,1,0:T(8,128)(2,1)S(1)}, u32[]{:S(2)}, u32[]{:S(2)}) collective-permute-start(bf16[2,128,128]{2,1,0:T(8,128)(2,1)S(1)} %get-tuple-element.48), channel_id=1, source_target_pairs={{0,10},{2,8},{4,14},{6,12},{8,2},{10,0},{12,6},{14,4},{1,11},{3,9}... | collective-permute-start | bytes 196616 | tf_op jit(solution)/shard_map/ppermute | solution.py:278
  65.5 8.9 %collective-permute-start.17 = (bf16[2,128,128]{2,1,0:T(8,128)(2,1)S(1)}, bf16[2,128,128]{2,1,0:T(8,128)(2,1)S(1)}, u32[]{:S(2)}, u32[]{:S(2)}) collective-permute-start(bf16[2,128,128]{2,1,0:T(8,128)(2,1)S(1)} %get-tuple-element.49), channel_id=1, source_target_pairs={{0,12},{2,14},{4,8},{6,10},{8,4},{10,6},{12,0},{14,2},{1,13},{3,15... | collective-permute-start | bytes 196616 | tf_op jit(solution)/shard_map/ppermute | solution.py:278
  68.4 7.0 %collective-permute-start.18 = (bf16[2,128,128]{2,1,0:T(8,128)(2,1)S(1)}, bf16[2,128,128]{2,1,0:T(8,128)(2,1)S(1)}, u32[]{:S(2)}, u32[]{:S(2)}) collective-permute-start(bf16[2,128,128]{2,1,0:T(8,128)(2,1)S(1)} %get-tuple-element.50), channel_id=1, source_target_pairs={{0,14},{2,12},{4,10},{6,8},{8,6},{10,4},{12,2},{14,0},{1,15},{3,13... | collective-permute-start | bytes 196616 | tf_op jit(solution)/shard_map/ppermute | solution.py:278

commit v3 on v2

v3 whole, which is shorter than its diff:
```python
import functools
import math

import jax
import jax.numpy as jnp
import numpy as np
from jax import lax
from jax.experimental import pallas as pl
from jax.experimental.pallas import tpu as pltpu
from jax.sharding import PartitionSpec as P

BF16 = jnp.bfloat16
F32 = jnp.float32
SUB = 16
LANES = 128
MAXROW = 8
CUTS = (1, 1)


def transform_tables(samples, frequencies):
    turns = (1 + np.arange(frequencies))[:, None] * np.arange(samples)[None, :] % samples
    phases = turns * (2.0 * math.pi / samples)
    both = np.stack([np.cos(phases), -np.sin(phases)], axis=1) * samples**-0.5
    small = both.astype(jnp.bfloat16)
    twice = (2.0 * both).astype(jnp.bfloat16)
    forward = np.zeros((frequencies, 2, SUB, samples, SUB), jnp.bfloat16)
    inverse = np.zeros((samples, SUB, frequencies, 2, SUB), jnp.bfloat16)
    for r in range(SUB):
        forward[:, :, r, :, r] = small
        inverse[:, r, :, :, r] = twice.transpose(2, 0, 1)

    def cut(table):
        high, wide = table.shape
        return np.ascontiguousarray(table.reshape(high, wide // LANES, LANES).transpose(1, 0, 2))

    return (
        cut(forward.reshape(frequencies * 2 * SUB, samples * SUB)),
        cut(inverse.reshape(samples * SUB, frequencies * 2 * SUB)),
    )


def params(limit):
    return pltpu.CompilerParams(vmem_limit_bytes=min(limit, 56 * 2**20))


def place_of(me, k, rows, first, count):
    return pl.ds(pl.multiple_of((me ^ k) * rows + first, SUB), count)


def forward_kernel(first, step, me_ref, table_hbm, traces_hbm, *refs):
    early_refs = refs[:1] if first else ()
    near_ref, *far_refs = refs[len(early_refs) : -4]
    near = near_ref.shape[0]
    table_ref, traces_ref, table_sem, sems = refs[-4:]
    steps, samples, _, width = traces_ref.shape
    tiles, high, _ = table_ref.shape
    part = min(256, high)
    me = me_ref[0]

    def fetch(i):
        return pltpu.make_async_copy(
            traces_hbm.at[:, pl.ds(first + i * step, step), :], traces_ref.at[i], sems.at[i]
        )

    table_copy = pltpu.make_async_copy(table_hbm, table_ref, table_sem)
    table_copy.start()
    for i in range(steps):
        fetch(i).start()
    for ref in early_refs:
        near_ref[:, :, :first, :] = ref[...]
    table_copy.wait()

    @pl.loop(0, steps)
    def _(i):
        fetch(i).wait()
        columns = jnp.concatenate(
            [
                traces_ref[i, :, b : b + SUB, :].reshape(samples * SUB, width)
                for b in range(0, step, SUB)
            ],
            axis=1,
        )
        for low in range(0, high, part):
            group = range(low // (2 * SUB), (low + part) // (2 * SUB))
            table = jnp.concatenate(
                [
                    jnp.concatenate(
                        [table_ref[k, place_of(me, s, 2 * SUB, 0, 2 * SUB), :] for s in group],
                        axis=0,
                    )
                    for k in range(tiles)
                ],
                axis=1,
            )
            found = jnp.dot(table, columns, preferred_element_type=F32).astype(BF16)
            for s in group:
                ref, begin = (near_ref.at[s], first) if s < near else (far_refs[s - near], 0)
                for c in range(2):
                    row = (2 * s + c) * SUB - low
                    for b in range(step // SUB):
                        spot = pl.ds(pl.multiple_of(begin + i * step + b * SUB, SUB), SUB)
                        ref[c, spot, :] = found[row : row + SUB, width * b : width * (b + 1)]


def forward(me, table, traces, near, first, count, early):
    samples, _, width = traces.shape
    parties = table.shape[1] // (2 * SUB)
    step = min(2 * SUB, count)
    extra = [early] if first else []
    shapes = [(near, 2, first + count, width)] + [(2, count, width)] * (parties - near)
    return pl.pallas_call(
        functools.partial(forward_kernel, first, step),
        in_specs=[pl.BlockSpec(memory_space=pltpu.SMEM)]
        + [pl.BlockSpec(memory_space=pl.ANY)] * 2
        + [pl.BlockSpec(memory_space=pltpu.VMEM)] * len(extra),
        out_specs=[pl.BlockSpec(memory_space=pltpu.VMEM)] * len(shapes),
        scratch_shapes=[
            pltpu.VMEM(table.shape, BF16),
            pltpu.VMEM((count // step, samples, step, width), BF16),
            pltpu.SemaphoreType.DMA,
            pltpu.SemaphoreType.DMA((count // step,)),
        ],
        out_shape=[jax.ShapeDtypeStruct(shape, BF16) for shape in shapes],
        compiler_params=params(50 * 2**20),
        cost_estimate=pl.CostEstimate(
            flops=table.shape[1] * 2 * samples * width * count,
            bytes_accessed=2 * samples * count * width,
            transcendentals=0,
        ),
        name="forward",
    )(me, table, traces, *extra)


def tiles_kernel(near, chunks, block, count_ref, column_ref, place_ref, own_hbm, other_hbm, *refs):
    rows, width = refs[0].shape[1:]
    far = refs[-7].shape[0] if len(chunks) > 1 else (len(refs) - 6) // 2 - near
    ins = near + far * len(chunks)
    near_in, far_in = refs[:near], refs[near:ins]
    near_out, far_out = refs[ins : ins + near], refs[ins + near : -6]
    tile_ref, top_ref, low_ref, sum_ref, row_ref, sems = refs[-6:]
    _, halves, _, size, _ = tile_ref.shape
    steps = halves // block
    me, side = place_ref[0], place_ref[1]
    tile_rows = count_ref.shape[1]

    def fetch(which, q):
        source = (own_hbm, other_hbm)[which]
        part = pl.ds(q * block, block)
        return pltpu.make_async_copy(source.at[part], tile_ref.at[which, part], sems.at[which, q])

    for q in range(steps):
        for which in range(2):
            fetch(which, q).start()

    for slot in range(2 * halves):
        row_ref[slot] = tile_rows
    begin = jnp.int32(0)
    for row in range(tile_rows + 1):
        for k in range(MAXROW):
            row_ref[begin + k] = row
        begin += count_ref[0, row] if row < tile_rows else 0

    def take(k, first, count, ref):
        place = place_of(me, k, rows, first, count)
        top_ref[place, :width] = ref[0]
        top_ref[place, width:] = ref[1]
        low_ref[place, :width] = -ref[1]
        low_ref[place, width:] = ref[0]

    def give(k, first, count, ref):
        place = place_of(me, k, rows, first, count)
        ref[0] = sum_ref[place, :width].astype(BF16)
        ref[1] = sum_ref[place, width:].astype(BF16)

    for k in range(near):
        take(k, 0, rows, near_in[k])
    for q, (first, count) in enumerate(chunks):
        for j in range(far):
            take(near + j, first, count, far_in[q * far + j])
    sum_ref[...] = jnp.zeros_like(sum_ref)

    @pl.loop(0, steps)
    def _(q):
        for which in range(2):
            fetch(which, q).wait()
        for k in range(block):
            for which in range(2):
                slot = q * block + k
                own = (side ^ which) * halves + slot
                column = jnp.clip(column_ref[0, own], 0, tile_rows - 1)
                place = pl.ds(pl.multiple_of(column * size, size), size)
                pair = jnp.concatenate(
                    [tile_ref[which, slot, 0], tile_ref[which, slot, 1]], axis=1
                )
                weights = jnp.concatenate([top_ref[place, :], low_ref[place, :]], axis=0)
                spot = pl.ds(pl.multiple_of(row_ref[own] * size, size), size)
                sum_ref[spot, :] += jnp.dot(pair, weights, preferred_element_type=F32)

    for k in range(near):
        give(k, 0, rows, near_out[k])
    for j in range(far):
        give(near + j, *chunks[0], far_out[j])
    for ref in far_out[far:]:
        for j in range(far):
            give(near + j, *chunks[1], ref.at[j])


def apply_tiles(counts, columns, place, own, other, chunks, nears, fars):
    halves, _, size, _ = own.shape
    _, rows, width = nears[0].shape
    far = len(fars) // len(chunks)
    total = (len(nears) + far) * rows
    block = math.gcd(8, halves)
    shapes = [nears[0].shape] * len(nears) + [(2, chunks[0][1], width)] * far
    shapes += [(far, 2, part, width) for _, part in chunks[1:]]
    return pl.pallas_call(
        functools.partial(tiles_kernel, len(nears), chunks, block),
        in_specs=[pl.BlockSpec(memory_space=pltpu.SMEM)] * 3
        + [pl.BlockSpec(memory_space=pl.ANY)] * 2
        + [pl.BlockSpec(memory_space=pltpu.VMEM)] * (len(nears) + len(fars)),
        out_specs=[pl.BlockSpec(memory_space=pltpu.VMEM)] * len(shapes),
        scratch_shapes=[
            pltpu.VMEM((2,) + own.shape, BF16),
            pltpu.VMEM((total, 2 * width), BF16),
            pltpu.VMEM((total, 2 * width), BF16),
            pltpu.VMEM((total + size, 2 * width), F32),
            pltpu.SMEM((2 * halves + MAXROW,), jnp.int32),
            pltpu.SemaphoreType.DMA((2, halves // block)),
        ],
        out_shape=[jax.ShapeDtypeStruct(shape, BF16) for shape in shapes],
        compiler_params=params(50 * 2**20),
        cost_estimate=pl.CostEstimate(
            flops=2 * 2 * halves * size * 4 * size * width,
            bytes_accessed=4 * own.size,
            transcendentals=0,
        ),
        name="tiles",
    )(counts, columns, place, own, other, *nears, *fars)


def split_kernel(in_ref, *out_refs):
    for j, ref in enumerate(out_refs):
        ref[...] = in_ref[j]


def split(late):
    return pl.pallas_call(
        split_kernel,
        in_specs=[pl.BlockSpec(memory_space=pltpu.VMEM)],
        out_specs=[pl.BlockSpec(memory_space=pltpu.VMEM)] * late.shape[0],
        out_shape=[jax.ShapeDtypeStruct(late.shape[1:], BF16)] * late.shape[0],
        compiler_params=params(50 * 2**20),
        cost_estimate=pl.CostEstimate(flops=0, bytes_accessed=1 << 24, transcendentals=0),
        name="split",
    )(late)


def inverse_kernel(first, step, parties, near, me_ref, table_ref, *refs):
    in_refs = refs[:parties]
    out_hbm, column_ref, held_ref, sems = refs[-4:]
    steps, samples, _, width = held_ref.shape
    part = min(4096, samples * SUB)
    me = me_ref[0]

    def send(i):
        return pltpu.make_async_copy(
            held_ref.at[i], out_hbm.at[:, pl.ds(first + i * step, step), :], sems.at[i]
        )

    @pl.loop(0, steps)
    def _(i):
        for s in range(parties):
            for c in range(2):
                for b in range(step // SUB):
                    ref, begin = in_refs[s], first if s < near else 0
                    spot = pl.ds(pl.multiple_of(begin + i * step + b * SUB, SUB), SUB)
                    column_ref[
                        place_of(me, s, 2 * SUB, c * SUB, SUB), width * b : width * (b + 1)
                    ] = ref[c, spot, :]
        for low in range(0, samples * SUB, part):
            table = jnp.concatenate(
                [table_ref[k, low : low + part, :] for k in range(table_ref.shape[0])], axis=1
            )
            found = jnp.dot(table, column_ref[...], preferred_element_type=F32).astype(BF16)
            for b in range(step // SUB):
                held_ref[i, low // SUB : (low + part) // SUB, SUB * b : SUB * (b + 1), :] = found[
                    :, width * b : width * (b + 1)
                ].reshape(part // SUB, SUB, width)
        send(i).start()

    for i in range(steps):
        send(i).wait()


def inverse(me, table, nears, fars, first, count, filled):
    _, rows, width = nears[0].shape
    parties = len(nears) + len(fars)
    samples = table.shape[1] // SUB
    step = min(2 * SUB, count)
    extra = [] if filled is None else [filled]
    return pl.pallas_call(
        functools.partial(inverse_kernel, first, step, parties, len(nears)),
        in_specs=[pl.BlockSpec(memory_space=pltpu.SMEM)]
        + [pl.BlockSpec(memory_space=pltpu.VMEM)] * (1 + parties)
        + [pl.BlockSpec(memory_space=pl.ANY)] * len(extra),
        out_specs=pl.BlockSpec(memory_space=pl.ANY),
        scratch_shapes=[
            pltpu.VMEM((parties * 2 * SUB, step // SUB * width), BF16),
            pltpu.VMEM((count // step, samples, step, width), BF16),
            pltpu.SemaphoreType.DMA((count // step,)),
        ],
        out_shape=jax.ShapeDtypeStruct((samples, rows, width), BF16),
        input_output_aliases={2 + parties: 0} if extra else {},
        compiler_params=params(
            2 * samples * (SUB * LANES * table.shape[0] * 5 // 4 + count * width) + 14 * 2**20
        ),
        cost_estimate=pl.CostEstimate(
            flops=parties * 4 * SUB * samples * width * count,
            bytes_accessed=2 * samples * count * width,
            transcendentals=0,
        ),
        name="inverse",
    )(me, table, *nears, *fars, *extra)


def send(block, k, parties):
    return lax.ppermute(block, "wide", [(i, i ^ k) for i in range(parties)]) if k else block


def cuts(rows, sizes):
    if rows % (sum(sizes) * 2 * SUB):
        return ((0, rows),)
    unit = rows // sum(sizes)
    return tuple((unit * sum(sizes[:i]), unit * n) for i, n in enumerate(sizes))


def shards(traces, row_counts, tile_cols, tiles):
    samples, rows, _ = traces.shape
    parties = lax.axis_size("wide")
    forward_table, inverse_table = transform_tables(samples, parties)
    me = jnp.stack([lax.axis_index("wide"), lax.axis_index("narrow")]).astype(jnp.int32)
    chunks = cuts(rows, CUTS)
    near = parties // 2
    far = range(near, parties)

    early = None
    got = []
    for first, count in chunks:
        early, *blocks = forward(me, forward_table, traces, near, first, count, early)
        if not first:
            own_tiles, early = lax.optimization_barrier((tiles[0], early))
        got += [send(block, k, parties) for k, block in zip(far, blocks)]
    other = lax.ppermute(own_tiles, "narrow", [(0, 1), (1, 0)])
    other, early = lax.optimization_barrier((other, early))
    nears = [send(block, k, parties) for k, block in enumerate(split(early))]

    sums = apply_tiles(row_counts, tile_cols, me, own_tiles, other, chunks, nears, got)
    nears, blocks, late = sums[:near], sums[near:parties], sums[parties:]
    got = [[send(block, k, parties) for k, block in zip(far, blocks)]]
    nears = [send(block, k, parties) for k, block in enumerate(nears)]
    for blocks in late:
        got.append([send(block, k, parties) for k, block in zip(far, split(blocks))])
    result = None
    for (first, count), blocks in zip(chunks, got):
        result = inverse(me, inverse_table, nears, blocks, first, count, result)
    return result


def solution(mesh):
    in_specs = (
        P(None, ("groups", "wide"), "narrow"),
        P(("groups", "wide"), None),
        P(("groups", "wide"), None),
        P(("groups", "wide"), "narrow", None, None, None),
    )
    out_specs = P(None, ("groups", "wide"), "narrow")
    return jax.shard_map(shards, mesh=mesh, in_specs=in_specs, out_specs=out_specs, check_vma=False)
```

time: 81.5 us -> 77.2 us (0.947)
  Pallas kernels: 28.4 us -> 25.4 us
  starting transfers between devices: 38.6 us -> 37.5 us
    pallas_call x5 -> x7, Pallas kernels: 28.4 us -> 25.4 us  [the longest x2 10.4 us: forward(): pl.pallas_call(functools.partial(forward_kernel, first, step), in_specs=[...]
    ppermute x23, starting transfers between devices: 38.6 us -> 37.5 us  [the longest x22 37 us: send(): lax.ppermute(block, 'wide', [(i, i ^ k) for i in range(parties)])]
    unnamed x6 -> x12, local copies, waits for them, and re-layouts: 0.66 us -> 1.61 us
  transfers between devices with their start and end apart: 23 -> 23, of which waited for: 6 -> 5; matrix products, arithmetic and copies ran while one was open for 1% -> 0% of each run, Pallas kernels for 21% -> 13%
where the time goes in v3:
time: 77.2 us; the launch traced here: 77 us
  starting transfers between devices  37.5 us (49%)
  Pallas kernels  25.4 us (33%)
  waiting for transfers between devices  12.3 us (16%)
  local copies, waits for them, and re-layouts  1.61 us (2%)
    ppermute x22, starting transfers between devices, send(): lax.ppermute(block, 'wide', [(i, i ^ k) for i in range(parties)])  37 us
    ppermute x22, waiting for transfers between devices, send(): lax.ppermute(block, 'wide', [(i, i ^ k) for i in range(parties)])  12.3 us
    pallas_call x2, Pallas kernels, forward(): pl.pallas_call(functools.partial(forward_kernel, first, step), in_specs=[...  10.4 us
    pallas_call x2, Pallas kernels, inverse(): pl.pallas_call(functools.partial(inverse_kernel, first, step, parties, le...  9.7 us
    pallas_call x1, Pallas kernels, apply_tiles(): pl.pallas_call(functools.partial(tiles_kernel, len(nears), chunks, block)...  5.18 us
    unnamed x12, local copies, waits for them, and re-layouts  1.61 us
  transfers between devices with their start and end apart: 23, of which 5 were waited for; matrix products, arithmetic and copies ran while one was open for 0% of the time, Pallas kernels for 13%

profile of v3, /device:TPU:0, one launch (start us, length us, event | category | flops | bytes accessed | tf_op | source)
XLA Modules:
  0.0 77.0 jit_solution(16568904657629264002)
XLA Ops:
  0.0 0.1 pad_add_fusion.me_ref.place_ref
  0.1 1.6 %copy-done.1 = bf16[32,256,128]{2,1,0:T(8,128)(2,1)S(1)} copy-done((bf16[32,256,128]{2,1,0:T(8,128)(2,1)S(1)}, bf16[32,256,128]{2,1,0:T(8,128)(2,1)}, u32[]{:S(2)}) %copy-start.1) | copy-done | bytes 2097176
  1.7 5.3 %forward.2 = (bf16[4,2,128,128]{3,2,1,0:T(8,128)(2,1)S(1)}, bf16[2,128,128]{2,1,0:T(8,128)(2,1)S(1)}, bf16[2,128,128]{2,1,0:T(8,128)(2,1)S(1)}, bf16[2,128,128]{2,1,0:T(8,128)(2,1)S(1)}, bf16[2,128,128]{2,1,0:T(8,128)(2,1)S(1)}) custom-call(s32[2]{0:T(128)S(1)} %pad_add_fusion.me_ref.place_ref, bf16[32,256,128]{2,1,0:T(8,128)(2,1)S(1)} %copy-done.1, ...), custom_call_target="tpu_custom_call" | custom-call | flops 2147483648 | bytes 8388608 | tf_op jit(solution)/shard_map/forward/pallas_call | solution.py:111
  7.0 0.5 collective-permute-start
  7.5 3.7 %collective-permute-start.4 = (bf16[2,128,128]{2,1,0:T(8,128)(2,1)S(1)}, bf16[2,128,128]{2,1,0:T(8,128)(2,1)S(1)}, u32[]{:S(2)}, u32[]{:S(2)}) collective-permute-start(bf16[2,128,128]{2,1,0:T(8,128)(2,1)S(1)} %get-tuple-element.46), channel_id=1, source_target_pairs={{0,8},{2,10},{4,12},{6,14},{8,0},{10,2},{12,4},{14,6},{1,9},{3,11}... | collective-permute-start | bytes 196616 | tf_op jit(solution)/shard_map/ppermute | solution.py:327
  11.1 1.3 %collective-permute-start.5 = (bf16[2,128,128]{2,1,0:T(8,128)(2,1)S(1)}, bf16[2,128,128]{2,1,0:T(8,128)(2,1)S(1)}, u32[]{:S(2)}, u32[]{:S(2)}) collective-permute-start(bf16[2,128,128]{2,1,0:T(8,128)(2,1)S(1)} %get-tuple-element.47), channel_id=1, source_target_pairs={{0,10},{2,8},{4,14},{6,12},{8,2},{10,0},{12,6},{14,4},{1,11},{3,9}... | collective-permute-start | bytes 196616 | tf_op jit(solution)/shard_map/ppermute | solution.py:327
  12.4 3.6 %collective-permute-start.6 = (bf16[2,128,128]{2,1,0:T(8,128)(2,1)S(1)}, bf16[2,128,128]{2,1,0:T(8,128)(2,1)S(1)}, u32[]{:S(2)}, u32[]{:S(2)}) collective-permute-start(bf16[2,128,128]{2,1,0:T(8,128)(2,1)S(1)} %get-tuple-element.48), channel_id=1, source_target_pairs={{0,12},{2,14},{4,8},{6,10},{8,4},{10,6},{12,0},{14,2},{1,13},{3,15... | collective-permute-start | bytes 196616 | tf_op jit(solution)/shard_map/ppermute | solution.py:327
  16.0 5.2 %forward.3 = (bf16[4,2,256,128]{3,2,1,0:T(8,128)(2,1)S(1)}, bf16[2,128,128]{2,1,0:T(8,128)(2,1)S(1)}, bf16[2,128,128]{2,1,0:T(8,128)(2,1)S(1)}, bf16[2,128,128]{2,1,0:T(8,128)(2,1)S(1)}, bf16[2,128,128]{2,1,0:T(8,128)(2,1)S(1)}) custom-call(s32[2]{0:T(128)S(1)} %pad_add_fusion.me_ref.place_ref, bf16[32,256,128]{2,1,0:T(8,128)(2,1)S(1)} %copy-done.1, ...), custom_call_target="tpu_custom_call" | custom-call | flops 2147483648 | bytes 8388608 | tf_op jit(solution)/shard_map/forward/pallas_call | solution.py:111
  21.2 1.0 %collective-permute-start.8 = (bf16[2,128,128]{2,1,0:T(8,128)(2,1)S(1)}, bf16[2,128,128]{2,1,0:T(8,128)(2,1)S(1)}, u32[]{:S(2)}, u32[]{:S(2)}) collective-permute-start(bf16[2,128,128]{2,1,0:T(8,128)(2,1)S(1)} %get-tuple-element.50), channel_id=1, source_target_pairs={{0,8},{2,10},{4,12},{6,14},{8,0},{10,2},{12,4},{14,6},{1,9},{3,11}... | collective-permute-start | bytes 196616 | tf_op jit(solution)/shard_map/ppermute | solution.py:327
  22.3 3.2 %collective-permute-start.9 = (bf16[2,128,128]{2,1,0:T(8,128)(2,1)S(1)}, bf16[2,128,128]{2,1,0:T(8,128)(2,1)S(1)}, u32[]{:S(2)}, u32[]{:S(2)}) collective-permute-start(bf16[2,128,128]{2,1,0:T(8,128)(2,1)S(1)} %get-tuple-element.51), channel_id=1, source_target_pairs={{0,10},{2,8},{4,14},{6,12},{8,2},{10,0},{12,6},{14,4},{1,11},{3,9}... | collective-permute-start | bytes 196616 | tf_op jit(solution)/shard_map/ppermute | solution.py:327
  25.5 0.3 collective-permute-start.1
  25.8 1.6 %collective-permute-start.2 = (bf16[2,256,128]{2,1,0:T(8,128)(2,1)S(1)}, bf16[2,256,128]{2,1,0:T(8,128)(2,1)S(1)}, u32[]{:S(2)}, u32[]{:S(2)}) collective-permute-start(bf16[2,256,128]{2,1,0:T(8,128)(2,1)S(1)} %get-tuple-element.44), channel_id=1, source_target_pairs={{0,4},{2,6},{4,0},{6,2},{8,12},{10,14},{12,8},{14,10},{1,5},{3,7},... | collective-permute-start | bytes 393224 | tf_op jit(solution)/shard_map/ppermute | solution.py:327
  27.4 1.6 %collective-permute-start.3 = (bf16[2,256,128]{2,1,0:T(8,128)(2,1)S(1)}, bf16[2,256,128]{2,1,0:T(8,128)(2,1)S(1)}, u32[]{:S(2)}, u32[]{:S(2)}) collective-permute-start(bf16[2,256,128]{2,1,0:T(8,128)(2,1)S(1)} %get-tuple-element.45), channel_id=1, source_target_pairs={{0,6},{2,4},{4,2},{6,0},{8,14},{10,12},{12,10},{14,8},{1,7},{3,5},... | collective-permute-start | bytes 393224 | tf_op jit(solution)/shard_map/ppermute | solution.py:327
  29.0 3.6 %collective-permute-start.10 = (bf16[2,128,128]{2,1,0:T(8,128)(2,1)S(1)}, bf16[2,128,128]{2,1,0:T(8,128)(2,1)S(1)}, u32[]{:S(2)}, u32[]{:S(2)}) collective-permute-start(bf16[2,128,128]{2,1,0:T(8,128)(2,1)S(1)} %get-tuple-element.52), channel_id=1, source_target_pairs={{0,12},{2,14},{4,8},{6,10},{8,4},{10,6},{12,0},{14,2},{1,13},{3,15... | collective-permute-start | bytes 196616 | tf_op jit(solution)/shard_map/ppermute | solution.py:327
  32.6 1.3 %collective-permute-start.11 = (bf16[2,128,128]{2,1,0:T(8,128)(2,1)S(1)}, bf16[2,128,128]{2,1,0:T(8,128)(2,1)S(1)}, u32[]{:S(2)}, u32[]{:S(2)}) collective-permute-start(bf16[2,128,128]{2,1,0:T(8,128)(2,1)S(1)} %get-tuple-element.53), channel_id=1, source_target_pairs={{0,14},{2,12},{4,10},{6,8},{8,6},{10,4},{12,2},{14,0},{1,15},{3,13... | collective-permute-start | bytes 196616 | tf_op jit(solution)/shard_map/ppermute | solution.py:327
  33.8 4.1 %collective-permute-done.10.refs_10_ = bf16[2,128,128]{2,1,0:T(8,128)(2,1)S(1)} collective-permute-done((bf16[2,128,128]{2,1,0:T(8,128)(2,1)S(1)}, bf16[2,128,128]{2,1,0:T(8,128)(2,1)S(1)}, u32[]{:S(2)}, u32[]{:S(2)}) %collective-permute-start.10) | collective-permute-done | bytes 65568 | tf_op jit(solution)/shard_map/ppermute | solution.py:327
  37.9 1.6 %collective-permute-done.11.refs_11_ = bf16[2,128,128]{2,1,0:T(8,128)(2,1)S(1)} collective-permute-done((bf16[2,128,128]{2,1,0:T(8,128)(2,1)S(1)}, bf16[2,128,128]{2,1,0:T(8,128)(2,1)S(1)}, u32[]{:S(2)}, u32[]{:S(2)}) %collective-permute-start.11) | collective-permute-done | bytes 65568 | tf_op jit(solution)/shard_map/ppermute | solution.py:327
  39.6 5.2 %tiles.1 = (bf16[2,256,128]{2,1,0:T(8,128)(2,1)S(1)}, bf16[2,256,128]{2,1,0:T(8,128)(2,1)S(1)}, bf16[2,256,128]{2,1,0:T(8,128)(2,1)S(1)}, bf16[2,256,128]{2,1,0:...) custom-call(s32[1,16]{1,0:T(1,128)S(1)} %copy-done.2, ...), custom_call_target="tpu_custom_call" | custom-call | flops 1342177280 | bytes 5242880 | tf_op jit(solution)/shard_map/tiles/pallas_call | solution.py:216
  44.9 3.1 %collective-permute-start.20 = (bf16[2,128,128]{2,1,0:T(8,128)(2,1)S(1)}, bf16[2,128,128]{2,1,0:T(8,128)(2,1)S(1)}, u32[]{:S(2)}, u32[]{:S(2)}) collective-permute-start(bf16[2,128,128]{2,1,0:T(8,128)(2,1)S(1)} %get-tuple-element.64), channel_id=1, source_target_pairs={{0,10},{2,8},{4,14},{6,12},{8,2},{10,0},{12,6},{14,4},{1,11},{3,9}... | collective-permute-start | bytes 196616 | tf_op jit(solution)/shard_map/ppermute | solution.py:327
  48.0 1.3 %collective-permute-start.12 = (bf16[2,256,128]{2,1,0:T(8,128)(2,1)S(1)}, bf16[2,256,128]{2,1,0:T(8,128)(2,1)S(1)}, u32[]{:S(2)}, u32[]{:S(2)}) collective-permute-start(bf16[2,256,128]{2,1,0:T(8,128)(2,1)S(1)} %get-tuple-element.55), channel_id=1, source_target_pairs={{0,2},{2,0},{4,6},{6,4},{8,10},{10,8},{12,14},{14,12},{1,3},{3,1},... | collective-permute-start | bytes 393224 | tf_op jit(solution)/shard_map/ppermute | solution.py:327
  49.2 0.3 collective-permute-start.13
  49.6 1.9 %collective-permute-start.14 = (bf16[2,256,128]{2,1,0:T(8,128)(2,1)S(1)}, bf16[2,256,128]{2,1,0:T(8,128)(2,1)S(1)}, u32[]{:S(2)}, u32[]{:S(2)}) collective-permute-start(bf16[2,256,128]{2,1,0:T(8,128)(2,1)S(1)} %get-tuple-element.57), channel_id=1, source_target_pairs={{0,6},{2,4},{4,2},{6,0},{8,14},{10,12},{12,10},{14,8},{1,7},{3,5},... | collective-permute-start | bytes 393224 | tf_op jit(solution)/shard_map/ppermute | solution.py:327
  51.4 1.0 %collective-permute-done.19.refs_4_ = bf16[2,128,128]{2,1,0:T(8,128)(2,1)S(1)} collective-permute-done((bf16[2,128,128]{2,1,0:T(8,128)(2,1)S(1)}, bf16[2,128,128]{2,1,0:T(8,128)(2,1)S(1)}, u32[]{:S(2)}, u32[]{:S(2)}) %collective-permute-start.19) | collective-permute-done | bytes 65568 | tf_op jit(solution)/shard_map/ppermute | solution.py:327
  52.4 0.9 %collective-permute-start.21 = (bf16[2,128,128]{2,1,0:T(8,128)(2,1)S(1)}, bf16[2,128,128]{2,1,0:T(8,128)(2,1)S(1)}, u32[]{:S(2)}, u32[]{:S(2)}) collective-permute-start(bf16[2,128,128]{2,1,0:T(8,128)(2,1)S(1)} %get-tuple-element.65), channel_id=1, source_target_pairs={{0,12},{2,14},{4,8},{6,10},{8,4},{10,6},{12,0},{14,2},{1,13},{3,15... | collective-permute-start | bytes 196616 | tf_op jit(solution)/shard_map/ppermute | solution.py:327
  53.4 3.0 %collective-permute-start.22 = (bf16[2,128,128]{2,1,0:T(8,128)(2,1)S(1)}, bf16[2,128,128]{2,1,0:T(8,128)(2,1)S(1)}, u32[]{:S(2)}, u32[]{:S(2)}) collective-permute-start(bf16[2,128,128]{2,1,0:T(8,128)(2,1)S(1)} %get-tuple-element.66), channel_id=1, source_target_pairs={{0,14},{2,12},{4,10},{6,8},{8,6},{10,4},{12,2},{14,0},{1,15},{3,13... | collective-permute-start | bytes 196616 | tf_op jit(solution)/shard_map/ppermute | solution.py:327
  56.4 3.2 %collective-permute-done.21.refs_6_ = bf16[2,128,128]{2,1,0:T(8,128)(2,1)S(1)} collective-permute-done((bf16[2,128,128]{2,1,0:T(8,128)(2,1)S(1)}, bf16[2,128,128]{2,1,0:T(8,128)(2,1)S(1)}, u32[]{:S(2)}, u32[]{:S(2)}) %collective-permute-start.21) | collective-permute-done | bytes 65568 | tf_op jit(solution)/shard_map/ppermute | solution.py:327
  59.6 2.4 %collective-permute-done.22.refs_7_ = bf16[2,128,128]{2,1,0:T(8,128)(2,1)S(1)} collective-permute-done((bf16[2,128,128]{2,1,0:T(8,128)(2,1)S(1)}, bf16[2,128,128]{2,1,0:T(8,128)(2,1)S(1)}, u32[]{:S(2)}, u32[]{:S(2)}) %collective-permute-start.22) | collective-permute-done | bytes 65568 | tf_op jit(solution)/shard_map/ppermute | solution.py:327
  62.0 2.2 %collective-permute-start.16 = (bf16[2,128,128]{2,1,0:T(8,128)(2,1)S(1)}, bf16[2,128,128]{2,1,0:T(8,128)(2,1)S(1)}, u32[]{:S(2)}, u32[]{:S(2)}) collective-permute-start(bf16[2,128,128]{2,1,0:T(8,128)(2,1)S(1)} %get-tuple-element.60), channel_id=1, source_target_pairs={{0,10},{2,8},{4,14},{6,12},{8,2},{10,0},{12,6},{14,4},{1,11},{3,9}... | collective-permute-start | bytes 196616 | tf_op jit(solution)/shard_map/ppermute | solution.py:327
  64.2 0.4 collective-permute-start.17
  64.6 2.7 %collective-permute-start.18 = (bf16[2,128,128]{2,1,0:T(8,128)(2,1)S(1)}, bf16[2,128,128]{2,1,0:T(8,128)(2,1)S(1)}, u32[]{:S(2)}, u32[]{:S(2)}) collective-permute-start(bf16[2,128,128]{2,1,0:T(8,128)(2,1)S(1)} %get-tuple-element.62), channel_id=1, source_target_pairs={{0,14},{2,12},{4,10},{6,8},{8,6},{10,4},{12,2},{14,0},{1,15},{3,13... | collective-permute-start | bytes 196616 | tf_op jit(solution)/shard_map/ppermute | solution.py:327
  67.3 4.8 %inverse.2.refs_8_ = bf16[256,256,128]{2,1,0:T(8,128)(2,1)} custom-call(s32[2]{0:T(128)S(1)} %pad_add_fusion.me_ref.place_ref, bf16[2,4096,128]{2,1,0:T(8,128)(2,1)S(1)} %copy-done, bf16[2,256,128]{2,1,0:T(8,128)(2,1)S(1)} %get-tuple-element.54.refs_0_, bf16[2,256,128]{2,1,0:T(8,128)(2,1)S(1)} %collective-permute-done.12.refs_1_, ...), custom_call_target="tpu_custom_call" | custom-call | flops 2147483648 | bytes 8388608 | tf_op jit(solution)/shard_map/inverse/pallas_call | solution.py:301
  72.2 4.9 %inverse.3 = bf16[256,256,128]{2,1,0:T(8,128)(2,1)} custom-call(s32[2]{0:T(128)S(1)} %pad_add_fusion.me_ref.place_ref, bf16[2,4096,128]{2,1,0:T(8,128)(2,1)S(1)} %copy-done, bf16[2,256,128]{2,1,0:T(8,128)(2,1)S(1)} %get-tuple-element.54.refs_0_, bf16[2,256,128]{2,1,0:T(8,128)(2,1)S(1)} %collective-permute-done.12.refs_1_, ...), custom_call_target="tpu_custom_call", output_to_operand_aliasing={{}: (10, {})} | custom-call | flops 2147483648 | bytes 8388608 | tf_op jit(solution)/shard_map/inverse/pallas_call | solution.py:301
  (34 shorter events, 0.2 us)
Async XLA Ops:
  0.1 1.6 %copy-start.1 = (bf16[32,256,128]{2,1,0:T(8,128)(2,1)S(1)}, bf16[32,256,128]{2,1,0:T(8,128)(2,1)}, u32[]{:S(2)}) copy-start(bf16[32,256,128]{2,1,0:T(8,128)(2,1)} %constant.12.clone.table_hbm) | copy-start | bytes 6291460
  1.7 5.3 %copy-start.4 = (bf16[1,40,2,128,128]{4,3,2,1,0:T(8,128)(2,1)S(1)}, bf16[1,40,2,128,128]{4,3,2,1,0:T(8,128)(2,1)}, u32[]{:S(2)}) copy-start(bf16[1,40,2,128,128]{4,3,2,1,0:T(8,128)(2,1)} %param.9) | copy-start | bytes 7864324
  7.0 14.2 %collective-permute-start = (bf16[40,2,128,128]{3,2,1,0:T(8,128)(2,1)S(1)}, bf16[40,2,128,128]{3,2,1,0:T(8,128)(2,1)S(1)}, u32[]{:S(2)}, u32[]{:S(2)}) collective-permute-start(bf16[40,2,128,128]{3,2,1,0:T(8,128)(2,1)S(1)} %bitcast.4), channel_id=1, source_target_pairs={{0,1},{1,0},{2,3},{3,2},{4,5},{5,4},{6,7},{7,6},{8,9},{9,8},{10,11... | collective-permute-start | bytes 7864328 | tf_op jit(solution)/shard_map/ppermute | solution.py:353
  7.5 14.8 %collective-permute-start.4 = (bf16[2,128,128]{2,1,0:T(8,128)(2,1)S(1)}, bf16[2,128,128]{2,1,0:T(8,128)(2,1)S(1)}, u32[]{:S(2)}, u32[]{:S(2)}) collective-permute-start(bf16[2,128,128]{2,1,0:T(8,128)(2,1)S(1)} %get-tuple-element.46), channel_id=1, source_target_pairs={{0,8},{2,10},{4,12},{6,14},{8,0},{10,2},{12,4},{14,6},{1,9},{3,11}... | collective-permute-start | bytes 196616 | tf_op jit(solution)/shard_map/ppermute | solution.py:327
  11.1 14.3 %collective-permute-start.5 = (bf16[2,128,128]{2,1,0:T(8,128)(2,1)S(1)}, bf16[2,128,128]{2,1,0:T(8,128)(2,1)S(1)}, u32[]{:S(2)}, u32[]{:S(2)}) collective-permute-start(bf16[2,128,128]{2,1,0:T(8,128)(2,1)S(1)} %get-tuple-element.47), channel_id=1, source_target_pairs={{0,10},{2,8},{4,14},{6,12},{8,2},{10,0},{12,6},{14,4},{1,11},{3,9}... | collective-permute-start | bytes 196616 | tf_op jit(solution)/shard_map/ppermute | solution.py:327
  12.4 13.4 %collective-permute-start.6 = (bf16[2,128,128]{2,1,0:T(8,128)(2,1)S(1)}, bf16[2,128,128]{2,1,0:T(8,128)(2,1)S(1)}, u32[]{:S(2)}, u32[]{:S(2)}) collective-permute-start(bf16[2,128,128]{2,1,0:T(8,128)(2,1)S(1)} %get-tuple-element.48), channel_id=1, source_target_pairs={{0,12},{2,14},{4,8},{6,10},{8,4},{10,6},{12,0},{14,2},{1,13},{3,15... | collective-permute-start | bytes 196616 | tf_op jit(solution)/shard_map/ppermute | solution.py:327
  16.0 23.5 %copy-start.2 = (s32[1,16]{1,0:T(1,128)S(1)}, s32[1,16]{1,0:T(1,128)}, u32[]{:S(2)}) copy-start(s32[1,16]{1,0:T(1,128)} %count_ref.1) | copy-start | bytes 196
  16.0 23.5 %copy-start.3 = (s32[1,80]{1,0:T(1,128)S(1)}, s32[1,80]{1,0:T(1,128)}, u32[]{:S(2)}) copy-start(s32[1,80]{1,0:T(1,128)} %column_ref.1) | copy-start | bytes 964
  16.0 11.3 %collective-permute-start.7 = (bf16[2,128,128]{2,1,0:T(8,128)(2,1)S(1)}, bf16[2,128,128]{2,1,0:T(8,128)(2,1)S(1)}, u32[]{:S(2)}, u32[]{:S(2)}) collective-permute-start(bf16[2,128,128]{2,1,0:T(8,128)(2,1)S(1)} %get-tuple-element.49), channel_id=1, source_target_pairs={{0,14},{2,12},{4,10},{6,8},{8,6},{10,4},{12,2},{14,0},{1,15},{3,13... | collective-permute-start | bytes 196616 | tf_op jit(solution)/shard_map/ppermute | solution.py:327
  21.2 18.3 %copy-start.5 = (bf16[40,2,128,128]{3,2,1,0:T(8,128)(2,1)}, bf16[40,2,128,128]{3,2,1,0:T(8,128)(2,1)S(1)}, u32[]{:S(2)}) copy-start(bf16[40,2,128,128]{3,2,1,0:T(8,128)(2,1)S(1)} %collective-permute-done.other_hbm) | copy-start | bytes 7864324
  21.2 7.7 %collective-permute-start.8 = (bf16[2,128,128]{2,1,0:T(8,128)(2,1)S(1)}, bf16[2,128,128]{2,1,0:T(8,128)(2,1)S(1)}, u32[]{:S(2)}, u32[]{:S(2)}) collective-permute-start(bf16[2,128,128]{2,1,0:T(8,128)(2,1)S(1)} %get-tuple-element.50), channel_id=1, source_target_pairs={{0,8},{2,10},{4,12},{6,14},{8,0},{10,2},{12,4},{14,6},{1,9},{3,11}... | collective-permute-start | bytes 196616 | tf_op jit(solution)/shard_map/ppermute | solution.py:327
  22.3 10.3 %collective-permute-start.9 = (bf16[2,128,128]{2,1,0:T(8,128)(2,1)S(1)}, bf16[2,128,128]{2,1,0:T(8,128)(2,1)S(1)}, u32[]{:S(2)}, u32[]{:S(2)}) collective-permute-start(bf16[2,128,128]{2,1,0:T(8,128)(2,1)S(1)} %get-tuple-element.51), channel_id=1, source_target_pairs={{0,10},{2,8},{4,14},{6,12},{8,2},{10,0},{12,6},{14,4},{1,11},{3,9}... | collective-permute-start | bytes 196616 | tf_op jit(solution)/shard_map/ppermute | solution.py:327
  25.5 14.1 %collective-permute-start.1 = (bf16[2,256,128]{2,1,0:T(8,128)(2,1)S(1)}, bf16[2,256,128]{2,1,0:T(8,128)(2,1)S(1)}, u32[]{:S(2)}, u32[]{:S(2)}) collective-permute-start(bf16[2,256,128]{2,1,0:T(8,128)(2,1)S(1)} %get-tuple-element.43), channel_id=1, source_target_pairs={{0,2},{2,0},{4,6},{6,4},{8,10},{10,8},{12,14},{14,12},{1,3},{3,1},... | collective-permute-start | bytes 393224 | tf_op jit(solution)/shard_map/ppermute | solution.py:327
  25.8 13.7 %collective-permute-start.2 = (bf16[2,256,128]{2,1,0:T(8,128)(2,1)S(1)}, bf16[2,256,128]{2,1,0:T(8,128)(2,1)S(1)}, u32[]{:S(2)}, u32[]{:S(2)}) collective-permute-start(bf16[2,256,128]{2,1,0:T(8,128)(2,1)S(1)} %get-tuple-element.44), channel_id=1, source_target_pairs={{0,4},{2,6},{4,0},{6,2},{8,12},{10,14},{12,8},{14,10},{1,5},{3,7},... | collective-permute-start | bytes 393224 | tf_op jit(solution)/shard_map/ppermute | solution.py:327
  27.4 12.2 %collective-permute-start.3 = (bf16[2,256,128]{2,1,0:T(8,128)(2,1)S(1)}, bf16[2,256,128]{2,1,0:T(8,128)(2,1)S(1)}, u32[]{:S(2)}, u32[]{:S(2)}) collective-permute-start(bf16[2,256,128]{2,1,0:T(8,128)(2,1)S(1)} %get-tuple-element.45), channel_id=1, source_target_pairs={{0,6},{2,4},{4,2},{6,0},{8,14},{10,12},{12,10},{14,8},{1,7},{3,5},... | collective-permute-start | bytes 393224 | tf_op jit(solution)/shard_map/ppermute | solution.py:327
  29.0 8.9 %collective-permute-start.10 = (bf16[2,128,128]{2,1,0:T(8,128)(2,1)S(1)}, bf16[2,128,128]{2,1,0:T(8,128)(2,1)S(1)}, u32[]{:S(2)}, u32[]{:S(2)}) collective-permute-start(bf16[2,128,128]{2,1,0:T(8,128)(2,1)S(1)} %get-tuple-element.52), channel_id=1, source_target_pairs={{0,12},{2,14},{4,8},{6,10},{8,4},{10,6},{12,0},{14,2},{1,13},{3,15... | collective-permute-start | bytes 196616 | tf_op jit(solution)/shard_map/ppermute | solution.py:327
  32.6 7.0 %collective-permute-start.11 = (bf16[2,128,128]{2,1,0:T(8,128)(2,1)S(1)}, bf16[2,128,128]{2,1,0:T(8,128)(2,1)S(1)}, u32[]{:S(2)}, u32[]{:S(2)}) collective-permute-start(bf16[2,128,128]{2,1,0:T(8,128)(2,1)S(1)} %get-tuple-element.53), channel_id=1, source_target_pairs={{0,14},{2,12},{4,10},{6,8},{8,6},{10,4},{12,2},{14,0},{1,15},{3,13... | collective-permute-start | bytes 196616 | tf_op jit(solution)/shard_map/ppermute | solution.py:327
  39.6 27.7 %copy-start = (bf16[2,4096,128]{2,1,0:T(8,128)(2,1)S(1)}, bf16[2,4096,128]{2,1,0:T(8,128)(2,1)}, u32[]{:S(2)}) copy-start(bf16[2,4096,128]{2,1,0:T(8,128)(2,1)} %constant.13.clone.table_ref) | copy-start | bytes 6291460
  44.8 7.6 %collective-permute-start.19 = (bf16[2,128,128]{2,1,0:T(8,128)(2,1)S(1)}, bf16[2,128,128]{2,1,0:T(8,128)(2,1)S(1)}, u32[]{:S(2)}, u32[]{:S(2)}) collective-permute-start(bf16[2,128,128]{2,1,0:T(8,128)(2,1)S(1)} %get-tuple-element.63), channel_id=1, source_target_pairs={{0,8},{2,10},{4,12},{6,14},{8,0},{10,2},{12,4},{14,6},{1,9},{3,11}... | collective-permute-start | bytes 196616 | tf_op jit(solution)/shard_map/ppermute | solution.py:327
  44.9 8.5 %collective-permute-start.20 = (bf16[2,128,128]{2,1,0:T(8,128)(2,1)S(1)}, bf16[2,128,128]{2,1,0:T(8,128)(2,1)S(1)}, u32[]{:S(2)}, u32[]{:S(2)}) collective-permute-start(bf16[2,128,128]{2,1,0:T(8,128)(2,1)S(1)} %get-tuple-element.64), channel_id=1, source_target_pairs={{0,10},{2,8},{4,14},{6,12},{8,2},{10,0},{12,6},{14,4},{1,11},{3,9}... | collective-permute-start | bytes 196616 | tf_op jit(solution)/shard_map/ppermute | solution.py:327
  48.0 16.3 %collective-permute-start.12 = (bf16[2,256,128]{2,1,0:T(8,128)(2,1)S(1)}, bf16[2,256,128]{2,1,0:T(8,128)(2,1)S(1)}, u32[]{:S(2)}, u32[]{:S(2)}) collective-permute-start(bf16[2,256,128]{2,1,0:T(8,128)(2,1)S(1)} %get-tuple-element.55), channel_id=1, source_target_pairs={{0,2},{2,0},{4,6},{6,4},{8,10},{10,8},{12,14},{14,12},{1,3},{3,1},... | collective-permute-start | bytes 393224 | tf_op jit(solution)/shard_map/ppermute | solution.py:327
  49.2 15.4 %collective-permute-start.13 = (bf16[2,256,128]{2,1,0:T(8,128)(2,1)S(1)}, bf16[2,256,128]{2,1,0:T(8,128)(2,1)S(1)}, u32[]{:S(2)}, u32[]{:S(2)}) collective-permute-start(bf16[2,256,128]{2,1,0:T(8,128)(2,1)S(1)} %get-tuple-element.56), channel_id=1, source_target_pairs={{0,4},{2,6},{4,0},{6,2},{8,12},{10,14},{12,8},{14,10},{1,5},{3,7},... | collective-permute-start | bytes 393224 | tf_op jit(solution)/shard_map/ppermute | solution.py:327
  49.6 17.7 %collective-permute-start.14 = (bf16[2,256,128]{2,1,0:T(8,128)(2,1)S(1)}, bf16[2,256,128]{2,1,0:T(8,128)(2,1)S(1)}, u32[]{:S(2)}, u32[]{:S(2)}) collective-permute-start(bf16[2,256,128]{2,1,0:T(8,128)(2,1)S(1)} %get-tuple-element.57), channel_id=1, source_target_pairs={{0,6},{2,4},{4,2},{6,0},{8,14},{10,12},{12,10},{14,8},{1,7},{3,5},... | collective-permute-start | bytes 393224 | tf_op jit(solution)/shard_map/ppermute | solution.py:327
  52.4 7.2 %collective-permute-start.21 = (bf16[2,128,128]{2,1,0:T(8,128)(2,1)S(1)}, bf16[2,128,128]{2,1,0:T(8,128)(2,1)S(1)}, u32[]{:S(2)}, u32[]{:S(2)}) collective-permute-start(bf16[2,128,128]{2,1,0:T(8,128)(2,1)S(1)} %get-tuple-element.65), channel_id=1, source_target_pairs={{0,12},{2,14},{4,8},{6,10},{8,4},{10,6},{12,0},{14,2},{1,13},{3,15... | collective-permute-start | bytes 196616 | tf_op jit(solution)/shard_map/ppermute | solution.py:327
  53.4 8.6 %collective-permute-start.22 = (bf16[2,128,128]{2,1,0:T(8,128)(2,1)S(1)}, bf16[2,128,128]{2,1,0:T(8,128)(2,1)S(1)}, u32[]{:S(2)}, u32[]{:S(2)}) collective-permute-start(bf16[2,128,128]{2,1,0:T(8,128)(2,1)S(1)} %get-tuple-element.66), channel_id=1, source_target_pairs={{0,14},{2,12},{4,10},{6,8},{8,6},{10,4},{12,2},{14,0},{1,15},{3,13... | collective-permute-start | bytes 196616 | tf_op jit(solution)/shard_map/ppermute | solution.py:327
  59.6 12.5 %collective-permute-start.15 = (bf16[2,128,128]{2,1,0:T(8,128)(2,1)S(1)}, bf16[2,128,128]{2,1,0:T(8,128)(2,1)S(1)}, u32[]{:S(2)}, u32[]{:S(2)}) collective-permute-start(bf16[2,128,128]{2,1,0:T(8,128)(2,1)S(1)} %get-tuple-element.59), channel_id=1, source_target_pairs={{0,8},{2,10},{4,12},{6,14},{8,0},{10,2},{12,4},{14,6},{1,9},{3,11}... | collective-permute-start | bytes 196616 | tf_op jit(solution)/shard_map/ppermute | solution.py:327
  62.0 10.1 %collective-permute-start.16 = (bf16[2,128,128]{2,1,0:T(8,128)(2,1)S(1)}, bf16[2,128,128]{2,1,0:T(8,128)(2,1)S(1)}, u32[]{:S(2)}, u32[]{:S(2)}) collective-permute-start(bf16[2,128,128]{2,1,0:T(8,128)(2,1)S(1)} %get-tuple-element.60), channel_id=1, source_target_pairs={{0,10},{2,8},{4,14},{6,12},{8,2},{10,0},{12,6},{14,4},{1,11},{3,9}... | collective-permute-start | bytes 196616 | tf_op jit(solution)/shard_map/ppermute | solution.py:327
  64.2 7.9 %collective-permute-start.17 = (bf16[2,128,128]{2,1,0:T(8,128)(2,1)S(1)}, bf16[2,128,128]{2,1,0:T(8,128)(2,1)S(1)}, u32[]{:S(2)}, u32[]{:S(2)}) collective-permute-start(bf16[2,128,128]{2,1,0:T(8,128)(2,1)S(1)} %get-tuple-element.61), channel_id=1, source_target_pairs={{0,12},{2,14},{4,8},{6,10},{8,4},{10,6},{12,0},{14,2},{1,13},{3,15... | collective-permute-start | bytes 196616 | tf_op jit(solution)/shard_map/ppermute | solution.py:327
  64.6 7.6 %collective-permute-start.18 = (bf16[2,128,128]{2,1,0:T(8,128)(2,1)S(1)}, bf16[2,128,128]{2,1,0:T(8,128)(2,1)S(1)}, u32[]{:S(2)}, u32[]{:S(2)}) collective-permute-start(bf16[2,128,128]{2,1,0:T(8,128)(2,1)S(1)} %get-tuple-element.62), channel_id=1, source_target_pairs={{0,14},{2,12},{4,10},{6,8},{8,6},{10,4},{12,2},{14,0},{1,15},{3,13... | collective-permute-start | bytes 196616 | tf_op jit(solution)/shard_map/ppermute | solution.py:327

commit v4 on v3

--- a/solution.py
+++ b/solution.py
@@ -17,26 +17,31 @@
 CUTS = (1, 1)
 
 
+def even_terms(samples):
+    return -(-(samples // 2 + 1) * SUB // LANES) * LANES // SUB
+
+
 def transform_tables(samples, frequencies):
     turns = (1 + np.arange(frequencies))[:, None] * np.arange(samples)[None, :] % samples
     phases = turns * (2.0 * math.pi / samples)
     both = np.stack([np.cos(phases), -np.sin(phases)], axis=1) * samples**-0.5
     small = both.astype(jnp.bfloat16)
     twice = (2.0 * both).astype(jnp.bfloat16)
-    forward = np.zeros((frequencies, 2, SUB, samples, SUB), jnp.bfloat16)
+    half = samples // 2
+    even = np.zeros((frequencies, SUB, even_terms(samples), SUB), jnp.bfloat16)
+    odd = np.zeros((frequencies, SUB, half, SUB), jnp.bfloat16)
     inverse = np.zeros((samples, SUB, frequencies, 2, SUB), jnp.bfloat16)
     for r in range(SUB):
-        forward[:, :, r, :, r] = small
+        even[:, r, : half + 1, r] = small[:, 0, : half + 1]
+        odd[:, r, 1:, r] = small[:, 1, 1:half]
         inverse[:, r, :, :, r] = twice.transpose(2, 0, 1)
 
-    def cut(table):
-        high, wide = table.shape
-        return np.ascontiguousarray(table.reshape(high, wide // LANES, LANES).transpose(1, 0, 2))
-
-    return (
-        cut(forward.reshape(frequencies * 2 * SUB, samples * SUB)),
-        cut(inverse.reshape(samples * SUB, frequencies * 2 * SUB)),
-    )
+    def cut(table, high):
+        table = table.reshape(high, -1, LANES)
+        return np.ascontiguousarray(table.transpose(1, 0, 2))
+
+    forward = np.concatenate([cut(even, frequencies * SUB), cut(odd, frequencies * SUB)])
+    return forward, cut(inverse, samples * SUB)
 
 
 def params(limit):
@@ -54,7 +59,7 @@
     table_ref, traces_ref, table_sem, sems = refs[-4:]
     steps, samples, _, width = traces_ref.shape
     tiles, high, _ = table_ref.shape
-    part = min(256, high)
+    part = min(128, high)
     me = me_ref[0]
 
     def fetch(i):
@@ -73,30 +78,49 @@
     @pl.loop(0, steps)
     def _(i):
         fetch(i).wait()
-        columns = jnp.concatenate(
-            [
-                traces_ref[i, :, b : b + SUB, :].reshape(samples * SUB, width)
-                for b in range(0, step, SUB)
-            ],
-            axis=1,
-        )
-        for low in range(0, high, part):
-            group = range(low // (2 * SUB), (low + part) // (2 * SUB))
-            table = jnp.concatenate(
+
+        def sample(t, b):
+            return traces_ref[i, t, b : b + SUB, :]
+
+        def even(t, b):
+            if t in (0, half):
+                return sample(t, b)
+            return sample(t, b) + sample(samples - t, b) if t < half else empty
+
+        def odd(t, b):
+            return sample(t, b) - sample(samples - t, b) if t else empty
+
+        half = samples // 2
+        empty = jnp.zeros((SUB, width), BF16)
+        cosines = even_terms(samples) * SUB // LANES
+        for c, (fold, terms, pieces) in enumerate(
+            (
+                (even, even_terms(samples), range(cosines)),
+                (odd, half, range(cosines, tiles)),
+            )
+        ):
+            columns = jnp.concatenate(
                 [
-                    jnp.concatenate(
-                        [table_ref[k, place_of(me, s, 2 * SUB, 0, 2 * SUB), :] for s in group],
-                        axis=0,
-                    )
-                    for k in range(tiles)
+                    jnp.concatenate([fold(t, b) for t in range(terms)], axis=0)
+                    for b in range(0, step, SUB)
                 ],
                 axis=1,
             )
-            found = jnp.dot(table, columns, preferred_element_type=F32).astype(BF16)
-            for s in group:
-                ref, begin = (near_ref.at[s], first) if s < near else (far_refs[s - near], 0)
-                for c in range(2):
-                    row = (2 * s + c) * SUB - low
+            for low in range(0, high, part):
+                group = range(low // SUB, (low + part) // SUB)
+                table = jnp.concatenate(
+                    [
+                        jnp.concatenate(
+                            [table_ref[k, place_of(me, s, SUB, 0, SUB), :] for s in group], axis=0
+                        )
+                        for k in pieces
+                    ],
+                    axis=1,
+                )
+                found = jnp.dot(table, columns, preferred_element_type=F32).astype(BF16)
+                for s in group:
+                    ref, begin = (near_ref.at[s], first) if s < near else (far_refs[s - near], 0)
+                    row = s * SUB - low
                     for b in range(step // SUB):
                         spot = pl.ds(pl.multiple_of(begin + i * step + b * SUB, SUB), SUB)
                         ref[c, spot, :] = found[row : row + SUB, width * b : width * (b + 1)]
@@ -104,7 +128,7 @@
 
 def forward(me, table, traces, near, first, count, early):
     samples, _, width = traces.shape
-    parties = table.shape[1] // (2 * SUB)
+    parties = table.shape[1] // SUB
     step = min(2 * SUB, count)
     extra = [early] if first else []
     shapes = [(near, 2, first + count, width)] + [(2, count, width)] * (parties - near)
@@ -121,9 +145,9 @@
             pltpu.SemaphoreType.DMA((count // step,)),
         ],
         out_shape=[jax.ShapeDtypeStruct(shape, BF16) for shape in shapes],
-        compiler_params=params(50 * 2**20),
+        compiler_params=params(52 * 2**20),
         cost_estimate=pl.CostEstimate(
-            flops=table.shape[1] * 2 * samples * width * count,
+            flops=table.shape[1] * 4 * samples * width * count,
             bytes_accessed=2 * samples * count * width,
             transcendentals=0,
         ),
@@ -228,7 +252,7 @@
             pltpu.SemaphoreType.DMA((2, halves // block)),
         ],
         out_shape=[jax.ShapeDtypeStruct(shape, BF16) for shape in shapes],
-        compiler_params=params(50 * 2**20),
+        compiler_params=params(28 * 2**20),
         cost_estimate=pl.CostEstimate(
             flops=2 * 2 * halves * size * 4 * size * width,
             bytes_accessed=4 * own.size,
@@ -347,14 +371,12 @@
     got = []
     for first, count in chunks:
         early, *blocks = forward(me, forward_table, traces, near, first, count, early)
-        if not first:
-            own_tiles, early = lax.optimization_barrier((tiles[0], early))
         got += [send(block, k, parties) for k, block in zip(far, blocks)]
-    other = lax.ppermute(own_tiles, "narrow", [(0, 1), (1, 0)])
+    other = lax.ppermute(tiles[0], "narrow", [(0, 1), (1, 0)])
     other, early = lax.optimization_barrier((other, early))
     nears = [send(block, k, parties) for k, block in enumerate(split(early))]
 
-    sums = apply_tiles(row_counts, tile_cols, me, own_tiles, other, chunks, nears, got)
+    sums = apply_tiles(row_counts, tile_cols, me, tiles[0], other, chunks, nears, got)
     nears, blocks, late = sums[:near], sums[near:parties], sums[parties:]
     got = [[send(block, k, parties) for k, block in zip(far, blocks)]]
     nears = [send(block, k, parties) for k, block in enumerate(nears)]

time: 77.2 us -> 75.5 us (0.978)
  Pallas kernels: 25.4 us -> 24.1 us
    unnamed x12 -> x10, local copies, waits for them, and re-layouts: 1.61 us -> 1.25 us
  transfers between devices with their start and end apart: 23 -> 23, of which waited for: 5 -> 5; matrix products, arithmetic and copies ran while one was open for 0% -> 0% of each run, Pallas kernels for 13% -> 19%
where the time goes in v4:
time: 75.5 us; the launch traced here: 75.4 us
  starting transfers between devices  37.2 us (49%)
  Pallas kernels  24.1 us (32%)
  waiting for transfers between devices  12.6 us (17%)
  local copies, waits for them, and re-layouts  1.25 us (2%)
    ppermute x22, starting transfers between devices, send(): lax.ppermute(block, 'wide', [(i, i ^ k) for i in range(parties)])  36.7 us
    ppermute x22, waiting for transfers between devices, send(): lax.ppermute(block, 'wide', [(i, i ^ k) for i in range(parties)])  12.6 us
    pallas_call x2, Pallas kernels, forward(): pl.pallas_call(functools.partial(forward_kernel, first, step), in_specs=[...  9.79 us
    pallas_call x2, Pallas kernels, inverse(): pl.pallas_call(functools.partial(inverse_kernel, first, step, parties, le...  9.72 us
    pallas_call x1, Pallas kernels, apply_tiles(): pl.pallas_call(functools.partial(tiles_kernel, len(nears), chunks, block)...  4.52 us
  transfers between devices with their start and end apart: 23, of which 5 were waited for; matrix products, arithmetic and copies ran while one was open for 0% of the time, Pallas kernels for 19%

profile of v4, /device:TPU:0, one launch (start us, length us, event | category | flops | bytes accessed | tf_op | source)
XLA Modules:
  0.0 75.4 jit_solution(7833282842948529350)
XLA Ops:
  0.0 0.5 collective-permute-start
  0.5 0.1 pad_add_fusion.me_ref.place_ref
  0.5 1.2 %copy-done.1 = bf16[33,128,128]{2,1,0:T(8,128)(2,1)S(1)} copy-done((bf16[33,128,128]{2,1,0:T(8,128)(2,1)S(1)}, bf16[33,128,128]{2,1,0:T(8,128)(2,1)}, u32[]{:S(2)}) %copy-start.1) | copy-done | bytes 1081368
  1.8 4.7 %forward.2 = (bf16[4,2,128,128]{3,2,1,0:T(8,128)(2,1)S(1)}, bf16[2,128,128]{2,1,0:T(8,128)(2,1)S(1)}, bf16[2,128,128]{2,1,0:T(8,128)(2,1)S(1)}, bf16[2,128,128]{2,1,0:T(8,128)(2,1)S(1)}, bf16[2,128,128]{2,1,0:T(8,128)(2,1)S(1)}) custom-call(s32[2]{0:T(128)S(1)} %pad_add_fusion.me_ref.place_ref, bf16[33,128,128]{2,1,0:T(8,128)(2,1)S(1)} %copy-done.1, ...), custom_call_target="tpu_custom_call" | custom-call | flops 2147483648 | bytes 8388608 | tf_op jit(solution)/shard_map/forward/pallas_call | solution.py:135
  6.4 3.7 %collective-permute-start.4 = (bf16[2,128,128]{2,1,0:T(8,128)(2,1)S(1)}, bf16[2,128,128]{2,1,0:T(8,128)(2,1)S(1)}, u32[]{:S(2)}, u32[]{:S(2)}) collective-permute-start(bf16[2,128,128]{2,1,0:T(8,128)(2,1)S(1)} %get-tuple-element.42), channel_id=1, source_target_pairs={{0,8},{2,10},{4,12},{6,14},{8,0},{10,2},{12,4},{14,6},{1,9},{3,11}... | collective-permute-start | bytes 196616 | tf_op jit(solution)/shard_map/ppermute | solution.py:351
  10.1 1.3 %collective-permute-start.5 = (bf16[2,128,128]{2,1,0:T(8,128)(2,1)S(1)}, bf16[2,128,128]{2,1,0:T(8,128)(2,1)S(1)}, u32[]{:S(2)}, u32[]{:S(2)}) collective-permute-start(bf16[2,128,128]{2,1,0:T(8,128)(2,1)S(1)} %get-tuple-element.43), channel_id=1, source_target_pairs={{0,10},{2,8},{4,14},{6,12},{8,2},{10,0},{12,6},{14,4},{1,11},{3,9}... | collective-permute-start | bytes 196616 | tf_op jit(solution)/shard_map/ppermute | solution.py:351
  11.4 3.6 %collective-permute-start.6 = (bf16[2,128,128]{2,1,0:T(8,128)(2,1)S(1)}, bf16[2,128,128]{2,1,0:T(8,128)(2,1)S(1)}, u32[]{:S(2)}, u32[]{:S(2)}) collective-permute-start(bf16[2,128,128]{2,1,0:T(8,128)(2,1)S(1)} %get-tuple-element.44), channel_id=1, source_target_pairs={{0,12},{2,14},{4,8},{6,10},{8,4},{10,6},{12,0},{14,2},{1,13},{3,15... | collective-permute-start | bytes 196616 | tf_op jit(solution)/shard_map/ppermute | solution.py:351
  15.0 5.1 %forward.3 = (bf16[4,2,256,128]{3,2,1,0:T(8,128)(2,1)S(1)}, bf16[2,128,128]{2,1,0:T(8,128)(2,1)S(1)}, bf16[2,128,128]{2,1,0:T(8,128)(2,1)S(1)}, bf16[2,128,128]{2,1,0:T(8,128)(2,1)S(1)}, bf16[2,128,128]{2,1,0:T(8,128)(2,1)S(1)}) custom-call(s32[2]{0:T(128)S(1)} %pad_add_fusion.me_ref.place_ref, bf16[33,128,128]{2,1,0:T(8,128)(2,1)} %constant.12.clone.table_hbm, ...), custom_call_target="tpu_custom_call" | custom-call | flops 2147483648 | bytes 8388608 | tf_op jit(solution)/shard_map/forward/pallas_call | solution.py:135
  20.1 1.0 %collective-permute-start.8 = (bf16[2,128,128]{2,1,0:T(8,128)(2,1)S(1)}, bf16[2,128,128]{2,1,0:T(8,128)(2,1)S(1)}, u32[]{:S(2)}, u32[]{:S(2)}) collective-permute-start(bf16[2,128,128]{2,1,0:T(8,128)(2,1)S(1)} %get-tuple-element.46), channel_id=1, source_target_pairs={{0,8},{2,10},{4,12},{6,14},{8,0},{10,2},{12,4},{14,6},{1,9},{3,11}... | collective-permute-start | bytes 196616 | tf_op jit(solution)/shard_map/ppermute | solution.py:351
  21.2 3.1 %collective-permute-start.9 = (bf16[2,128,128]{2,1,0:T(8,128)(2,1)S(1)}, bf16[2,128,128]{2,1,0:T(8,128)(2,1)S(1)}, u32[]{:S(2)}, u32[]{:S(2)}) collective-permute-start(bf16[2,128,128]{2,1,0:T(8,128)(2,1)S(1)} %get-tuple-element.47), channel_id=1, source_target_pairs={{0,10},{2,8},{4,14},{6,12},{8,2},{10,0},{12,6},{14,4},{1,11},{3,9}... | collective-permute-start | bytes 196616 | tf_op jit(solution)/shard_map/ppermute | solution.py:351
  24.4 0.3 collective-permute-start.1
  24.7 1.6 %collective-permute-start.2 = (bf16[2,256,128]{2,1,0:T(8,128)(2,1)S(1)}, bf16[2,256,128]{2,1,0:T(8,128)(2,1)S(1)}, u32[]{:S(2)}, u32[]{:S(2)}) collective-permute-start(bf16[2,256,128]{2,1,0:T(8,128)(2,1)S(1)} %get-tuple-element.40), channel_id=1, source_target_pairs={{0,4},{2,6},{4,0},{6,2},{8,12},{10,14},{12,8},{14,10},{1,5},{3,7},... | collective-permute-start | bytes 393224 | tf_op jit(solution)/shard_map/ppermute | solution.py:351
  26.3 1.6 %collective-permute-start.3 = (bf16[2,256,128]{2,1,0:T(8,128)(2,1)S(1)}, bf16[2,256,128]{2,1,0:T(8,128)(2,1)S(1)}, u32[]{:S(2)}, u32[]{:S(2)}) collective-permute-start(bf16[2,256,128]{2,1,0:T(8,128)(2,1)S(1)} %get-tuple-element.41), channel_id=1, source_target_pairs={{0,6},{2,4},{4,2},{6,0},{8,14},{10,12},{12,10},{14,8},{1,7},{3,5},... | collective-permute-start | bytes 393224 | tf_op jit(solution)/shard_map/ppermute | solution.py:351
  27.9 3.6 %collective-permute-start.10 = (bf16[2,128,128]{2,1,0:T(8,128)(2,1)S(1)}, bf16[2,128,128]{2,1,0:T(8,128)(2,1)S(1)}, u32[]{:S(2)}, u32[]{:S(2)}) collective-permute-start(bf16[2,128,128]{2,1,0:T(8,128)(2,1)S(1)} %get-tuple-element.48), channel_id=1, source_target_pairs={{0,12},{2,14},{4,8},{6,10},{8,4},{10,6},{12,0},{14,2},{1,13},{3,15... | collective-permute-start | bytes 196616 | tf_op jit(solution)/shard_map/ppermute | solution.py:351
  31.5 1.4 %collective-permute-start.11 = (bf16[2,128,128]{2,1,0:T(8,128)(2,1)S(1)}, bf16[2,128,128]{2,1,0:T(8,128)(2,1)S(1)}, u32[]{:S(2)}, u32[]{:S(2)}) collective-permute-start(bf16[2,128,128]{2,1,0:T(8,128)(2,1)S(1)} %get-tuple-element.49), channel_id=1, source_target_pairs={{0,14},{2,12},{4,10},{6,8},{8,6},{10,4},{12,2},{14,0},{1,15},{3,13... | collective-permute-start | bytes 196616 | tf_op jit(solution)/shard_map/ppermute | solution.py:351
  32.9 3.8 %collective-permute-done.10.refs_10_ = bf16[2,128,128]{2,1,0:T(8,128)(2,1)S(1)} collective-permute-done((bf16[2,128,128]{2,1,0:T(8,128)(2,1)S(1)}, bf16[2,128,128]{2,1,0:T(8,128)(2,1)S(1)}, u32[]{:S(2)}, u32[]{:S(2)}) %collective-permute-start.10) | collective-permute-done | bytes 65568 | tf_op jit(solution)/shard_map/ppermute | solution.py:351
  36.7 1.7 %collective-permute-done.11.refs_11_ = bf16[2,128,128]{2,1,0:T(8,128)(2,1)S(1)} collective-permute-done((bf16[2,128,128]{2,1,0:T(8,128)(2,1)S(1)}, bf16[2,128,128]{2,1,0:T(8,128)(2,1)S(1)}, u32[]{:S(2)}, u32[]{:S(2)}) %collective-permute-start.11) | collective-permute-done | bytes 65568 | tf_op jit(solution)/shard_map/ppermute | solution.py:351
  38.5 4.5 %tiles.1 = (bf16[2,256,128]{2,1,0:T(8,128)(2,1)S(1)}, bf16[2,256,128]{2,1,0:T(8,128)(2,1)S(1)}, bf16[2,256,128]{2,1,0:T(8,128)(2,1)S(1)}, bf16[2,256,128]{2,1,0:...) custom-call(s32[1,16]{1,0:T(1,128)S(1)} %copy-done.3, ...), custom_call_target="tpu_custom_call" | custom-call | flops 1342177280 | bytes 5242880 | tf_op jit(solution)/shard_map/tiles/pallas_call | solution.py:240
  43.1 3.1 %collective-permute-start.20 = (bf16[2,128,128]{2,1,0:T(8,128)(2,1)S(1)}, bf16[2,128,128]{2,1,0:T(8,128)(2,1)S(1)}, u32[]{:S(2)}, u32[]{:S(2)}) collective-permute-start(bf16[2,128,128]{2,1,0:T(8,128)(2,1)S(1)} %get-tuple-element.60), channel_id=1, source_target_pairs={{0,10},{2,8},{4,14},{6,12},{8,2},{10,0},{12,6},{14,4},{1,11},{3,9}... | collective-permute-start | bytes 196616 | tf_op jit(solution)/shard_map/ppermute | solution.py:351
  46.2 1.3 %collective-permute-start.12 = (bf16[2,256,128]{2,1,0:T(8,128)(2,1)S(1)}, bf16[2,256,128]{2,1,0:T(8,128)(2,1)S(1)}, u32[]{:S(2)}, u32[]{:S(2)}) collective-permute-start(bf16[2,256,128]{2,1,0:T(8,128)(2,1)S(1)} %get-tuple-element.51), channel_id=1, source_target_pairs={{0,2},{2,0},{4,6},{6,4},{8,10},{10,8},{12,14},{14,12},{1,3},{3,1},... | collective-permute-start | bytes 393224 | tf_op jit(solution)/shard_map/ppermute | solution.py:351
  47.5 0.6 collective-permute-start.13
  48.1 1.6 %collective-permute-start.14 = (bf16[2,256,128]{2,1,0:T(8,128)(2,1)S(1)}, bf16[2,256,128]{2,1,0:T(8,128)(2,1)S(1)}, u32[]{:S(2)}, u32[]{:S(2)}) collective-permute-start(bf16[2,256,128]{2,1,0:T(8,128)(2,1)S(1)} %get-tuple-element.53), channel_id=1, source_target_pairs={{0,6},{2,4},{4,2},{6,0},{8,14},{10,12},{12,10},{14,8},{1,7},{3,5},... | collective-permute-start | bytes 393224 | tf_op jit(solution)/shard_map/ppermute | solution.py:351
  49.7 1.2 %collective-permute-done.19.refs_4_ = bf16[2,128,128]{2,1,0:T(8,128)(2,1)S(1)} collective-permute-done((bf16[2,128,128]{2,1,0:T(8,128)(2,1)S(1)}, bf16[2,128,128]{2,1,0:T(8,128)(2,1)S(1)}, u32[]{:S(2)}, u32[]{:S(2)}) %collective-permute-start.19) | collective-permute-done | bytes 65568 | tf_op jit(solution)/shard_map/ppermute | solution.py:351
  50.9 0.8 %collective-permute-start.21 = (bf16[2,128,128]{2,1,0:T(8,128)(2,1)S(1)}, bf16[2,128,128]{2,1,0:T(8,128)(2,1)S(1)}, u32[]{:S(2)}, u32[]{:S(2)}) collective-permute-start(bf16[2,128,128]{2,1,0:T(8,128)(2,1)S(1)} %get-tuple-element.61), channel_id=1, source_target_pairs={{0,12},{2,14},{4,8},{6,10},{8,4},{10,6},{12,0},{14,2},{1,13},{3,15... | collective-permute-start | bytes 196616 | tf_op jit(solution)/shard_map/ppermute | solution.py:351
  51.7 3.0 %collective-permute-start.22 = (bf16[2,128,128]{2,1,0:T(8,128)(2,1)S(1)}, bf16[2,128,128]{2,1,0:T(8,128)(2,1)S(1)}, u32[]{:S(2)}, u32[]{:S(2)}) collective-permute-start(bf16[2,128,128]{2,1,0:T(8,128)(2,1)S(1)} %get-tuple-element.62), channel_id=1, source_target_pairs={{0,14},{2,12},{4,10},{6,8},{8,6},{10,4},{12,2},{14,0},{1,15},{3,13... | collective-permute-start | bytes 196616 | tf_op jit(solution)/shard_map/ppermute | solution.py:351
  54.7 3.3 %collective-permute-done.21.refs_6_ = bf16[2,128,128]{2,1,0:T(8,128)(2,1)S(1)} collective-permute-done((bf16[2,128,128]{2,1,0:T(8,128)(2,1)S(1)}, bf16[2,128,128]{2,1,0:T(8,128)(2,1)S(1)}, u32[]{:S(2)}, u32[]{:S(2)}) %collective-permute-start.21) | collective-permute-done | bytes 65568 | tf_op jit(solution)/shard_map/ppermute | solution.py:351
  57.9 2.5 %collective-permute-done.22.refs_7_ = bf16[2,128,128]{2,1,0:T(8,128)(2,1)S(1)} collective-permute-done((bf16[2,128,128]{2,1,0:T(8,128)(2,1)S(1)}, bf16[2,128,128]{2,1,0:T(8,128)(2,1)S(1)}, u32[]{:S(2)}, u32[]{:S(2)}) %collective-permute-start.22) | collective-permute-done | bytes 65568 | tf_op jit(solution)/shard_map/ppermute | solution.py:351
  60.5 2.2 %collective-permute-start.16 = (bf16[2,128,128]{2,1,0:T(8,128)(2,1)S(1)}, bf16[2,128,128]{2,1,0:T(8,128)(2,1)S(1)}, u32[]{:S(2)}, u32[]{:S(2)}) collective-permute-start(bf16[2,128,128]{2,1,0:T(8,128)(2,1)S(1)} %get-tuple-element.56), channel_id=1, source_target_pairs={{0,10},{2,8},{4,14},{6,12},{8,2},{10,0},{12,6},{14,4},{1,11},{3,9}... | collective-permute-start | bytes 196616 | tf_op jit(solution)/shard_map/ppermute | solution.py:351
  62.6 0.3 collective-permute-start.17
  62.9 2.6 %collective-permute-start.18 = (bf16[2,128,128]{2,1,0:T(8,128)(2,1)S(1)}, bf16[2,128,128]{2,1,0:T(8,128)(2,1)S(1)}, u32[]{:S(2)}, u32[]{:S(2)}) collective-permute-start(bf16[2,128,128]{2,1,0:T(8,128)(2,1)S(1)} %get-tuple-element.58), channel_id=1, source_target_pairs={{0,14},{2,12},{4,10},{6,8},{8,6},{10,4},{12,2},{14,0},{1,15},{3,13... | collective-permute-start | bytes 196616 | tf_op jit(solution)/shard_map/ppermute | solution.py:351
  65.6 4.9 %inverse.2.refs_8_ = bf16[256,256,128]{2,1,0:T(8,128)(2,1)} custom-call(s32[2]{0:T(128)S(1)} %pad_add_fusion.me_ref.place_ref, bf16[2,4096,128]{2,1,0:T(8,128)(2,1)S(1)} %copy-done, bf16[2,256,128]{2,1,0:T(8,128)(2,1)S(1)} %get-tuple-element.50.refs_0_, bf16[2,256,128]{2,1,0:T(8,128)(2,1)S(1)} %collective-permute-done.12.refs_1_, ...), custom_call_target="tpu_custom_call" | custom-call | flops 2147483648 | bytes 8388608 | tf_op jit(solution)/shard_map/inverse/pallas_call | solution.py:325
  70.5 4.9 %inverse.3 = bf16[256,256,128]{2,1,0:T(8,128)(2,1)} custom-call(s32[2]{0:T(128)S(1)} %pad_add_fusion.me_ref.place_ref, bf16[2,4096,128]{2,1,0:T(8,128)(2,1)S(1)} %copy-done, bf16[2,256,128]{2,1,0:T(8,128)(2,1)S(1)} %get-tuple-element.50.refs_0_, bf16[2,256,128]{2,1,0:T(8,128)(2,1)S(1)} %collective-permute-done.12.refs_1_, ...), custom_call_target="tpu_custom_call", output_to_operand_aliasing={{}: (10, {})} | custom-call | flops 2147483648 | bytes 8388608 | tf_op jit(solution)/shard_map/inverse/pallas_call | solution.py:325
  (32 shorter events, 0.2 us)
Async XLA Ops:
  0.0 20.1 %collective-permute-start = (bf16[40,2,128,128]{3,2,1,0:T(8,128)(2,1)}, bf16[40,2,128,128]{3,2,1,0:T(8,128)(2,1)S(1)}, u32[]{:S(2)}, u32[]{:S(2)}) collective-permute-start(bf16[40,2,128,128]{3,2,1,0:T(8,128)(2,1)} %bitcast.3), channel_id=1, source_target_pairs={{0,1},{1,0},{2,3},{3,2},{4,5},{5,4},{6,7},{7,6},{8,9},{9,8},{10,11... | collective-permute-start | bytes 7864328 | tf_op jit(solution)/shard_map/ppermute | solution.py:375
  0.5 1.2 %copy-start.1 = (bf16[33,128,128]{2,1,0:T(8,128)(2,1)S(1)}, bf16[33,128,128]{2,1,0:T(8,128)(2,1)}, u32[]{:S(2)}) copy-start(bf16[33,128,128]{2,1,0:T(8,128)(2,1)} %constant.12.clone.table_hbm) | copy-start | bytes 3244036
  6.4 14.8 %collective-permute-start.4 = (bf16[2,128,128]{2,1,0:T(8,128)(2,1)S(1)}, bf16[2,128,128]{2,1,0:T(8,128)(2,1)S(1)}, u32[]{:S(2)}, u32[]{:S(2)}) collective-permute-start(bf16[2,128,128]{2,1,0:T(8,128)(2,1)S(1)} %get-tuple-element.42), channel_id=1, source_target_pairs={{0,8},{2,10},{4,12},{6,14},{8,0},{10,2},{12,4},{14,6},{1,9},{3,11}... | collective-permute-start | bytes 196616 | tf_op jit(solution)/shard_map/ppermute | solution.py:351
  10.1 14.3 %collective-permute-start.5 = (bf16[2,128,128]{2,1,0:T(8,128)(2,1)S(1)}, bf16[2,128,128]{2,1,0:T(8,128)(2,1)S(1)}, u32[]{:S(2)}, u32[]{:S(2)}) collective-permute-start(bf16[2,128,128]{2,1,0:T(8,128)(2,1)S(1)} %get-tuple-element.43), channel_id=1, source_target_pairs={{0,10},{2,8},{4,14},{6,12},{8,2},{10,0},{12,6},{14,4},{1,11},{3,9}... | collective-permute-start | bytes 196616 | tf_op jit(solution)/shard_map/ppermute | solution.py:351
  11.4 13.3 %collective-permute-start.6 = (bf16[2,128,128]{2,1,0:T(8,128)(2,1)S(1)}, bf16[2,128,128]{2,1,0:T(8,128)(2,1)S(1)}, u32[]{:S(2)}, u32[]{:S(2)}) collective-permute-start(bf16[2,128,128]{2,1,0:T(8,128)(2,1)S(1)} %get-tuple-element.44), channel_id=1, source_target_pairs={{0,12},{2,14},{4,8},{6,10},{8,4},{10,6},{12,0},{14,2},{1,13},{3,15... | collective-permute-start | bytes 196616 | tf_op jit(solution)/shard_map/ppermute | solution.py:351
  15.0 11.3 %collective-permute-start.7 = (bf16[2,128,128]{2,1,0:T(8,128)(2,1)S(1)}, bf16[2,128,128]{2,1,0:T(8,128)(2,1)S(1)}, u32[]{:S(2)}, u32[]{:S(2)}) collective-permute-start(bf16[2,128,128]{2,1,0:T(8,128)(2,1)S(1)} %get-tuple-element.45), channel_id=1, source_target_pairs={{0,14},{2,12},{4,10},{6,8},{8,6},{10,4},{12,2},{14,0},{1,15},{3,13... | collective-permute-start | bytes 196616 | tf_op jit(solution)/shard_map/ppermute | solution.py:351
  15.0 23.5 %copy-start.2 = (bf16[1,40,2,128,128]{4,3,2,1,0:T(8,128)(2,1)S(1)}, bf16[1,40,2,128,128]{4,3,2,1,0:T(8,128)(2,1)}, u32[]{:S(2)}) copy-start(bf16[1,40,2,128,128]{4,3,2,1,0:T(8,128)(2,1)} %param.9) | copy-start | bytes 7864324
  15.0 23.5 %copy-start.3 = (s32[1,16]{1,0:T(1,128)S(1)}, s32[1,16]{1,0:T(1,128)}, u32[]{:S(2)}) copy-start(s32[1,16]{1,0:T(1,128)} %count_ref.1) | copy-start | bytes 196
  15.0 23.5 %copy-start.4 = (s32[1,80]{1,0:T(1,128)S(1)}, s32[1,80]{1,0:T(1,128)}, u32[]{:S(2)}) copy-start(s32[1,80]{1,0:T(1,128)} %column_ref.1) | copy-start | bytes 964
  20.1 7.7 %collective-permute-start.8 = (bf16[2,128,128]{2,1,0:T(8,128)(2,1)S(1)}, bf16[2,128,128]{2,1,0:T(8,128)(2,1)S(1)}, u32[]{:S(2)}, u32[]{:S(2)}) collective-permute-start(bf16[2,128,128]{2,1,0:T(8,128)(2,1)S(1)} %get-tuple-element.46), channel_id=1, source_target_pairs={{0,8},{2,10},{4,12},{6,14},{8,0},{10,2},{12,4},{14,6},{1,9},{3,11}... | collective-permute-start | bytes 196616 | tf_op jit(solution)/shard_map/ppermute | solution.py:351
  21.2 10.2 %collective-permute-start.9 = (bf16[2,128,128]{2,1,0:T(8,128)(2,1)S(1)}, bf16[2,128,128]{2,1,0:T(8,128)(2,1)S(1)}, u32[]{:S(2)}, u32[]{:S(2)}) collective-permute-start(bf16[2,128,128]{2,1,0:T(8,128)(2,1)S(1)} %get-tuple-element.47), channel_id=1, source_target_pairs={{0,10},{2,8},{4,14},{6,12},{8,2},{10,0},{12,6},{14,4},{1,11},{3,9}... | collective-permute-start | bytes 196616 | tf_op jit(solution)/shard_map/ppermute | solution.py:351
  24.4 14.1 %collective-permute-start.1 = (bf16[2,256,128]{2,1,0:T(8,128)(2,1)S(1)}, bf16[2,256,128]{2,1,0:T(8,128)(2,1)S(1)}, u32[]{:S(2)}, u32[]{:S(2)}) collective-permute-start(bf16[2,256,128]{2,1,0:T(8,128)(2,1)S(1)} %get-tuple-element.39), channel_id=1, source_target_pairs={{0,2},{2,0},{4,6},{6,4},{8,10},{10,8},{12,14},{14,12},{1,3},{3,1},... | collective-permute-start | bytes 393224 | tf_op jit(solution)/shard_map/ppermute | solution.py:351
  24.7 13.7 %collective-permute-start.2 = (bf16[2,256,128]{2,1,0:T(8,128)(2,1)S(1)}, bf16[2,256,128]{2,1,0:T(8,128)(2,1)S(1)}, u32[]{:S(2)}, u32[]{:S(2)}) collective-permute-start(bf16[2,256,128]{2,1,0:T(8,128)(2,1)S(1)} %get-tuple-element.40), channel_id=1, source_target_pairs={{0,4},{2,6},{4,0},{6,2},{8,12},{10,14},{12,8},{14,10},{1,5},{3,7},... | collective-permute-start | bytes 393224 | tf_op jit(solution)/shard_map/ppermute | solution.py:351
  26.3 12.2 %collective-permute-start.3 = (bf16[2,256,128]{2,1,0:T(8,128)(2,1)S(1)}, bf16[2,256,128]{2,1,0:T(8,128)(2,1)S(1)}, u32[]{:S(2)}, u32[]{:S(2)}) collective-permute-start(bf16[2,256,128]{2,1,0:T(8,128)(2,1)S(1)} %get-tuple-element.41), channel_id=1, source_target_pairs={{0,6},{2,4},{4,2},{6,0},{8,14},{10,12},{12,10},{14,8},{1,7},{3,5},... | collective-permute-start | bytes 393224 | tf_op jit(solution)/shard_map/ppermute | solution.py:351
  27.9 8.8 %collective-permute-start.10 = (bf16[2,128,128]{2,1,0:T(8,128)(2,1)S(1)}, bf16[2,128,128]{2,1,0:T(8,128)(2,1)S(1)}, u32[]{:S(2)}, u32[]{:S(2)}) collective-permute-start(bf16[2,128,128]{2,1,0:T(8,128)(2,1)S(1)} %get-tuple-element.48), channel_id=1, source_target_pairs={{0,12},{2,14},{4,8},{6,10},{8,4},{10,6},{12,0},{14,2},{1,13},{3,15... | collective-permute-start | bytes 196616 | tf_op jit(solution)/shard_map/ppermute | solution.py:351
  31.5 7.0 %collective-permute-start.11 = (bf16[2,128,128]{2,1,0:T(8,128)(2,1)S(1)}, bf16[2,128,128]{2,1,0:T(8,128)(2,1)S(1)}, u32[]{:S(2)}, u32[]{:S(2)}) collective-permute-start(bf16[2,128,128]{2,1,0:T(8,128)(2,1)S(1)} %get-tuple-element.49), channel_id=1, source_target_pairs={{0,14},{2,12},{4,10},{6,8},{8,6},{10,4},{12,2},{14,0},{1,15},{3,13... | collective-permute-start | bytes 196616 | tf_op jit(solution)/shard_map/ppermute | solution.py:351
  38.5 27.1 %copy-start = (bf16[2,4096,128]{2,1,0:T(8,128)(2,1)S(1)}, bf16[2,4096,128]{2,1,0:T(8,128)(2,1)}, u32[]{:S(2)}) copy-start(bf16[2,4096,128]{2,1,0:T(8,128)(2,1)} %constant.13.clone.table_ref) | copy-start | bytes 6291460
  43.0 7.9 %collective-permute-start.19 = (bf16[2,128,128]{2,1,0:T(8,128)(2,1)S(1)}, bf16[2,128,128]{2,1,0:T(8,128)(2,1)S(1)}, u32[]{:S(2)}, u32[]{:S(2)}) collective-permute-start(bf16[2,128,128]{2,1,0:T(8,128)(2,1)S(1)} %get-tuple-element.59), channel_id=1, source_target_pairs={{0,8},{2,10},{4,12},{6,14},{8,0},{10,2},{12,4},{14,6},{1,9},{3,11}... | collective-permute-start | bytes 196616 | tf_op jit(solution)/shard_map/ppermute | solution.py:351
  43.1 8.6 %collective-permute-start.20 = (bf16[2,128,128]{2,1,0:T(8,128)(2,1)S(1)}, bf16[2,128,128]{2,1,0:T(8,128)(2,1)S(1)}, u32[]{:S(2)}, u32[]{:S(2)}) collective-permute-start(bf16[2,128,128]{2,1,0:T(8,128)(2,1)S(1)} %get-tuple-element.60), channel_id=1, source_target_pairs={{0,10},{2,8},{4,14},{6,12},{8,2},{10,0},{12,6},{14,4},{1,11},{3,9}... | collective-permute-start | bytes 196616 | tf_op jit(solution)/shard_map/ppermute | solution.py:351
  46.2 16.4 %collective-permute-start.12 = (bf16[2,256,128]{2,1,0:T(8,128)(2,1)S(1)}, bf16[2,256,128]{2,1,0:T(8,128)(2,1)S(1)}, u32[]{:S(2)}, u32[]{:S(2)}) collective-permute-start(bf16[2,256,128]{2,1,0:T(8,128)(2,1)S(1)} %get-tuple-element.51), channel_id=1, source_target_pairs={{0,2},{2,0},{4,6},{6,4},{8,10},{10,8},{12,14},{14,12},{1,3},{3,1},... | collective-permute-start | bytes 393224 | tf_op jit(solution)/shard_map/ppermute | solution.py:351
  47.5 15.5 %collective-permute-start.13 = (bf16[2,256,128]{2,1,0:T(8,128)(2,1)S(1)}, bf16[2,256,128]{2,1,0:T(8,128)(2,1)S(1)}, u32[]{:S(2)}, u32[]{:S(2)}) collective-permute-start(bf16[2,256,128]{2,1,0:T(8,128)(2,1)S(1)} %get-tuple-element.52), channel_id=1, source_target_pairs={{0,4},{2,6},{4,0},{6,2},{8,12},{10,14},{12,8},{14,10},{1,5},{3,7},... | collective-permute-start | bytes 393224 | tf_op jit(solution)/shard_map/ppermute | solution.py:351
  48.1 17.5 %collective-permute-start.14 = (bf16[2,256,128]{2,1,0:T(8,128)(2,1)S(1)}, bf16[2,256,128]{2,1,0:T(8,128)(2,1)S(1)}, u32[]{:S(2)}, u32[]{:S(2)}) collective-permute-start(bf16[2,256,128]{2,1,0:T(8,128)(2,1)S(1)} %get-tuple-element.53), channel_id=1, source_target_pairs={{0,6},{2,4},{4,2},{6,0},{8,14},{10,12},{12,10},{14,8},{1,7},{3,5},... | collective-permute-start | bytes 393224 | tf_op jit(solution)/shard_map/ppermute | solution.py:351
  50.9 7.0 %collective-permute-start.21 = (bf16[2,128,128]{2,1,0:T(8,128)(2,1)S(1)}, bf16[2,128,128]{2,1,0:T(8,128)(2,1)S(1)}, u32[]{:S(2)}, u32[]{:S(2)}) collective-permute-start(bf16[2,128,128]{2,1,0:T(8,128)(2,1)S(1)} %get-tuple-element.61), channel_id=1, source_target_pairs={{0,12},{2,14},{4,8},{6,10},{8,4},{10,6},{12,0},{14,2},{1,13},{3,15... | collective-permute-start | bytes 196616 | tf_op jit(solution)/shard_map/ppermute | solution.py:351
  51.7 8.8 %collective-permute-start.22 = (bf16[2,128,128]{2,1,0:T(8,128)(2,1)S(1)}, bf16[2,128,128]{2,1,0:T(8,128)(2,1)S(1)}, u32[]{:S(2)}, u32[]{:S(2)}) collective-permute-start(bf16[2,128,128]{2,1,0:T(8,128)(2,1)S(1)} %get-tuple-element.62), channel_id=1, source_target_pairs={{0,14},{2,12},{4,10},{6,8},{8,6},{10,4},{12,2},{14,0},{1,15},{3,13... | collective-permute-start | bytes 196616 | tf_op jit(solution)/shard_map/ppermute | solution.py:351
  57.9 12.5 %collective-permute-start.15 = (bf16[2,128,128]{2,1,0:T(8,128)(2,1)S(1)}, bf16[2,128,128]{2,1,0:T(8,128)(2,1)S(1)}, u32[]{:S(2)}, u32[]{:S(2)}) collective-permute-start(bf16[2,128,128]{2,1,0:T(8,128)(2,1)S(1)} %get-tuple-element.55), channel_id=1, source_target_pairs={{0,8},{2,10},{4,12},{6,14},{8,0},{10,2},{12,4},{14,6},{1,9},{3,11}... | collective-permute-start | bytes 196616 | tf_op jit(solution)/shard_map/ppermute | solution.py:351
  60.5 10.0 %collective-permute-start.16 = (bf16[2,128,128]{2,1,0:T(8,128)(2,1)S(1)}, bf16[2,128,128]{2,1,0:T(8,128)(2,1)S(1)}, u32[]{:S(2)}, u32[]{:S(2)}) collective-permute-start(bf16[2,128,128]{2,1,0:T(8,128)(2,1)S(1)} %get-tuple-element.56), channel_id=1, source_target_pairs={{0,10},{2,8},{4,14},{6,12},{8,2},{10,0},{12,6},{14,4},{1,11},{3,9}... | collective-permute-start | bytes 196616 | tf_op jit(solution)/shard_map/ppermute | solution.py:351
  62.6 7.8 %collective-permute-start.17 = (bf16[2,128,128]{2,1,0:T(8,128)(2,1)S(1)}, bf16[2,128,128]{2,1,0:T(8,128)(2,1)S(1)}, u32[]{:S(2)}, u32[]{:S(2)}) collective-permute-start(bf16[2,128,128]{2,1,0:T(8,128)(2,1)S(1)} %get-tuple-element.57), channel_id=1, source_target_pairs={{0,12},{2,14},{4,8},{6,10},{8,4},{10,6},{12,0},{14,2},{1,13},{3,15... | collective-permute-start | bytes 196616 | tf_op jit(solution)/shard_map/ppermute | solution.py:351
  62.9 7.5 %collective-permute-start.18 = (bf16[2,128,128]{2,1,0:T(8,128)(2,1)S(1)}, bf16[2,128,128]{2,1,0:T(8,128)(2,1)S(1)}, u32[]{:S(2)}, u32[]{:S(2)}) collective-permute-start(bf16[2,128,128]{2,1,0:T(8,128)(2,1)S(1)} %get-tuple-element.58), channel_id=1, source_target_pairs={{0,14},{2,12},{4,10},{6,8},{8,6},{10,4},{12,2},{14,0},{1,15},{3,13... | collective-permute-start | bytes 196616 | tf_op jit(solution)/shard_map/ppermute | solution.py:351

commit v5 on v4

--- a/solution.py
+++ b/solution.py
@@ -234,7 +234,7 @@
     _, rows, width = nears[0].shape
     far = len(fars) // len(chunks)
     total = (len(nears) + far) * rows
-    block = math.gcd(8, halves)
+    block = math.gcd(20, halves)
     shapes = [nears[0].shape] * len(nears) + [(2, chunks[0][1], width)] * far
     shapes += [(far, 2, part, width) for _, part in chunks[1:]]
     return pl.pallas_call(

time: 75.5 us -> 75.4 us (level)
  transfers between devices with their start and end apart: 23 -> 23, of which waited for: 5 -> 5; matrix products, arithmetic and copies ran while one was open for 0% -> 0% of each run, Pallas kernels for 19% -> 20%
where the time goes in v5:
time: 75.4 us; the launch traced here: 75.3 us
  starting transfers between devices  37.2 us (49%)
  Pallas kernels  24 us (32%)
  waiting for transfers between devices  12.6 us (17%)
  local copies, waits for them, and re-layouts  1.25 us (2%)
    ppermute x22, starting transfers between devices, send(): lax.ppermute(block, 'wide', [(i, i ^ k) for i in range(parties)])  36.8 us
    ppermute x22, waiting for transfers between devices, send(): lax.ppermute(block, 'wide', [(i, i ^ k) for i in range(parties)])  12.6 us
    pallas_call x2, Pallas kernels, forward(): pl.pallas_call(functools.partial(forward_kernel, first, step), in_specs=[...  9.79 us
    pallas_call x2, Pallas kernels, inverse(): pl.pallas_call(functools.partial(inverse_kernel, first, step, parties, le...  9.71 us
    pallas_call x1, Pallas kernels, apply_tiles(): pl.pallas_call(functools.partial(tiles_kernel, len(nears), chunks, block)...  4.44 us
  transfers between devices with their start and end apart: 23, of which 5 were waited for; matrix products, arithmetic and copies ran while one was open for 0% of the time, Pallas kernels for 20%

profile of v5, /device:TPU:0, one launch (start us, length us, event | category | flops | bytes accessed | tf_op | source)
XLA Modules:
  0.0 75.3 jit_solution(14749311719884128979)
XLA Ops:
  0.0 0.5 collective-permute-start
  0.5 0.1 pad_add_fusion.me_ref.place_ref
  0.5 1.2 %copy-done.1 = bf16[33,128,128]{2,1,0:T(8,128)(2,1)S(1)} copy-done((bf16[33,128,128]{2,1,0:T(8,128)(2,1)S(1)}, bf16[33,128,128]{2,1,0:T(8,128)(2,1)}, u32[]{:S(2)}) %copy-start.1) | copy-done | bytes 1081368
  1.8 4.7 %forward.2 = (bf16[4,2,128,128]{3,2,1,0:T(8,128)(2,1)S(1)}, bf16[2,128,128]{2,1,0:T(8,128)(2,1)S(1)}, bf16[2,128,128]{2,1,0:T(8,128)(2,1)S(1)}, bf16[2,128,128]{2,1,0:T(8,128)(2,1)S(1)}, bf16[2,128,128]{2,1,0:T(8,128)(2,1)S(1)}) custom-call(s32[2]{0:T(128)S(1)} %pad_add_fusion.me_ref.place_ref, bf16[33,128,128]{2,1,0:T(8,128)(2,1)S(1)} %copy-done.1, ...), custom_call_target="tpu_custom_call" | custom-call | flops 2147483648 | bytes 8388608 | tf_op jit(solution)/shard_map/forward/pallas_call | solution.py:135
  6.4 3.7 %collective-permute-start.4 = (bf16[2,128,128]{2,1,0:T(8,128)(2,1)S(1)}, bf16[2,128,128]{2,1,0:T(8,128)(2,1)S(1)}, u32[]{:S(2)}, u32[]{:S(2)}) collective-permute-start(bf16[2,128,128]{2,1,0:T(8,128)(2,1)S(1)} %get-tuple-element.42), channel_id=1, source_target_pairs={{0,8},{2,10},{4,12},{6,14},{8,0},{10,2},{12,4},{14,6},{1,9},{3,11}... | collective-permute-start | bytes 196616 | tf_op jit(solution)/shard_map/ppermute | solution.py:351
  10.1 1.3 %collective-permute-start.5 = (bf16[2,128,128]{2,1,0:T(8,128)(2,1)S(1)}, bf16[2,128,128]{2,1,0:T(8,128)(2,1)S(1)}, u32[]{:S(2)}, u32[]{:S(2)}) collective-permute-start(bf16[2,128,128]{2,1,0:T(8,128)(2,1)S(1)} %get-tuple-element.43), channel_id=1, source_target_pairs={{0,10},{2,8},{4,14},{6,12},{8,2},{10,0},{12,6},{14,4},{1,11},{3,9}... | collective-permute-start | bytes 196616 | tf_op jit(solution)/shard_map/ppermute | solution.py:351
  11.4 3.6 %collective-permute-start.6 = (bf16[2,128,128]{2,1,0:T(8,128)(2,1)S(1)}, bf16[2,128,128]{2,1,0:T(8,128)(2,1)S(1)}, u32[]{:S(2)}, u32[]{:S(2)}) collective-permute-start(bf16[2,128,128]{2,1,0:T(8,128)(2,1)S(1)} %get-tuple-element.44), channel_id=1, source_target_pairs={{0,12},{2,14},{4,8},{6,10},{8,4},{10,6},{12,0},{14,2},{1,13},{3,15... | collective-permute-start | bytes 196616 | tf_op jit(solution)/shard_map/ppermute | solution.py:351
  15.0 5.1 %forward.3 = (bf16[4,2,256,128]{3,2,1,0:T(8,128)(2,1)S(1)}, bf16[2,128,128]{2,1,0:T(8,128)(2,1)S(1)}, bf16[2,128,128]{2,1,0:T(8,128)(2,1)S(1)}, bf16[2,128,128]{2,1,0:T(8,128)(2,1)S(1)}, bf16[2,128,128]{2,1,0:T(8,128)(2,1)S(1)}) custom-call(s32[2]{0:T(128)S(1)} %pad_add_fusion.me_ref.place_ref, bf16[33,128,128]{2,1,0:T(8,128)(2,1)} %constant.12.clone.table_hbm, ...), custom_call_target="tpu_custom_call" | custom-call | flops 2147483648 | bytes 8388608 | tf_op jit(solution)/shard_map/forward/pallas_call | solution.py:135
  20.1 1.0 %collective-permute-start.8 = (bf16[2,128,128]{2,1,0:T(8,128)(2,1)S(1)}, bf16[2,128,128]{2,1,0:T(8,128)(2,1)S(1)}, u32[]{:S(2)}, u32[]{:S(2)}) collective-permute-start(bf16[2,128,128]{2,1,0:T(8,128)(2,1)S(1)} %get-tuple-element.46), channel_id=1, source_target_pairs={{0,8},{2,10},{4,12},{6,14},{8,0},{10,2},{12,4},{14,6},{1,9},{3,11}... | collective-permute-start | bytes 196616 | tf_op jit(solution)/shard_map/ppermute | solution.py:351
  21.2 3.1 %collective-permute-start.9 = (bf16[2,128,128]{2,1,0:T(8,128)(2,1)S(1)}, bf16[2,128,128]{2,1,0:T(8,128)(2,1)S(1)}, u32[]{:S(2)}, u32[]{:S(2)}) collective-permute-start(bf16[2,128,128]{2,1,0:T(8,128)(2,1)S(1)} %get-tuple-element.47), channel_id=1, source_target_pairs={{0,10},{2,8},{4,14},{6,12},{8,2},{10,0},{12,6},{14,4},{1,11},{3,9}... | collective-permute-start | bytes 196616 | tf_op jit(solution)/shard_map/ppermute | solution.py:351
  24.4 0.3 collective-permute-start.1
  24.7 1.6 %collective-permute-start.2 = (bf16[2,256,128]{2,1,0:T(8,128)(2,1)S(1)}, bf16[2,256,128]{2,1,0:T(8,128)(2,1)S(1)}, u32[]{:S(2)}, u32[]{:S(2)}) collective-permute-start(bf16[2,256,128]{2,1,0:T(8,128)(2,1)S(1)} %get-tuple-element.40), channel_id=1, source_target_pairs={{0,4},{2,6},{4,0},{6,2},{8,12},{10,14},{12,8},{14,10},{1,5},{3,7},... | collective-permute-start | bytes 393224 | tf_op jit(solution)/shard_map/ppermute | solution.py:351
  26.3 1.6 %collective-permute-start.3 = (bf16[2,256,128]{2,1,0:T(8,128)(2,1)S(1)}, bf16[2,256,128]{2,1,0:T(8,128)(2,1)S(1)}, u32[]{:S(2)}, u32[]{:S(2)}) collective-permute-start(bf16[2,256,128]{2,1,0:T(8,128)(2,1)S(1)} %get-tuple-element.41), channel_id=1, source_target_pairs={{0,6},{2,4},{4,2},{6,0},{8,14},{10,12},{12,10},{14,8},{1,7},{3,5},... | collective-permute-start | bytes 393224 | tf_op jit(solution)/shard_map/ppermute | solution.py:351
  27.9 3.6 %collective-permute-start.10 = (bf16[2,128,128]{2,1,0:T(8,128)(2,1)S(1)}, bf16[2,128,128]{2,1,0:T(8,128)(2,1)S(1)}, u32[]{:S(2)}, u32[]{:S(2)}) collective-permute-start(bf16[2,128,128]{2,1,0:T(8,128)(2,1)S(1)} %get-tuple-element.48), channel_id=1, source_target_pairs={{0,12},{2,14},{4,8},{6,10},{8,4},{10,6},{12,0},{14,2},{1,13},{3,15... | collective-permute-start | bytes 196616 | tf_op jit(solution)/shard_map/ppermute | solution.py:351
  31.5 1.4 %collective-permute-start.11 = (bf16[2,128,128]{2,1,0:T(8,128)(2,1)S(1)}, bf16[2,128,128]{2,1,0:T(8,128)(2,1)S(1)}, u32[]{:S(2)}, u32[]{:S(2)}) collective-permute-start(bf16[2,128,128]{2,1,0:T(8,128)(2,1)S(1)} %get-tuple-element.49), channel_id=1, source_target_pairs={{0,14},{2,12},{4,10},{6,8},{8,6},{10,4},{12,2},{14,0},{1,15},{3,13... | collective-permute-start | bytes 196616 | tf_op jit(solution)/shard_map/ppermute | solution.py:351
  32.9 3.8 %collective-permute-done.10.refs_10_ = bf16[2,128,128]{2,1,0:T(8,128)(2,1)S(1)} collective-permute-done((bf16[2,128,128]{2,1,0:T(8,128)(2,1)S(1)}, bf16[2,128,128]{2,1,0:T(8,128)(2,1)S(1)}, u32[]{:S(2)}, u32[]{:S(2)}) %collective-permute-start.10) | collective-permute-done | bytes 65568 | tf_op jit(solution)/shard_map/ppermute | solution.py:351
  36.7 1.7 %collective-permute-done.11.refs_11_ = bf16[2,128,128]{2,1,0:T(8,128)(2,1)S(1)} collective-permute-done((bf16[2,128,128]{2,1,0:T(8,128)(2,1)S(1)}, bf16[2,128,128]{2,1,0:T(8,128)(2,1)S(1)}, u32[]{:S(2)}, u32[]{:S(2)}) %collective-permute-start.11) | collective-permute-done | bytes 65568 | tf_op jit(solution)/shard_map/ppermute | solution.py:351
  38.5 4.4 %tiles.1 = (bf16[2,256,128]{2,1,0:T(8,128)(2,1)S(1)}, bf16[2,256,128]{2,1,0:T(8,128)(2,1)S(1)}, bf16[2,256,128]{2,1,0:T(8,128)(2,1)S(1)}, bf16[2,256,128]{2,1,0:...) custom-call(s32[1,16]{1,0:T(1,128)S(1)} %copy-done.3, ...), custom_call_target="tpu_custom_call" | custom-call | flops 1342177280 | bytes 5242880 | tf_op jit(solution)/shard_map/tiles/pallas_call | solution.py:240
  43.0 3.1 %collective-permute-start.20 = (bf16[2,128,128]{2,1,0:T(8,128)(2,1)S(1)}, bf16[2,128,128]{2,1,0:T(8,128)(2,1)S(1)}, u32[]{:S(2)}, u32[]{:S(2)}) collective-permute-start(bf16[2,128,128]{2,1,0:T(8,128)(2,1)S(1)} %get-tuple-element.60), channel_id=1, source_target_pairs={{0,10},{2,8},{4,14},{6,12},{8,2},{10,0},{12,6},{14,4},{1,11},{3,9}... | collective-permute-start | bytes 196616 | tf_op jit(solution)/shard_map/ppermute | solution.py:351
  46.1 1.3 %collective-permute-start.12 = (bf16[2,256,128]{2,1,0:T(8,128)(2,1)S(1)}, bf16[2,256,128]{2,1,0:T(8,128)(2,1)S(1)}, u32[]{:S(2)}, u32[]{:S(2)}) collective-permute-start(bf16[2,256,128]{2,1,0:T(8,128)(2,1)S(1)} %get-tuple-element.51), channel_id=1, source_target_pairs={{0,2},{2,0},{4,6},{6,4},{8,10},{10,8},{12,14},{14,12},{1,3},{3,1},... | collective-permute-start | bytes 393224 | tf_op jit(solution)/shard_map/ppermute | solution.py:351
  47.4 0.5 collective-permute-start.13
  47.9 1.7 %collective-permute-start.14 = (bf16[2,256,128]{2,1,0:T(8,128)(2,1)S(1)}, bf16[2,256,128]{2,1,0:T(8,128)(2,1)S(1)}, u32[]{:S(2)}, u32[]{:S(2)}) collective-permute-start(bf16[2,256,128]{2,1,0:T(8,128)(2,1)S(1)} %get-tuple-element.53), channel_id=1, source_target_pairs={{0,6},{2,4},{4,2},{6,0},{8,14},{10,12},{12,10},{14,8},{1,7},{3,5},... | collective-permute-start | bytes 393224 | tf_op jit(solution)/shard_map/ppermute | solution.py:351
  49.6 1.2 %collective-permute-done.19.refs_4_ = bf16[2,128,128]{2,1,0:T(8,128)(2,1)S(1)} collective-permute-done((bf16[2,128,128]{2,1,0:T(8,128)(2,1)S(1)}, bf16[2,128,128]{2,1,0:T(8,128)(2,1)S(1)}, u32[]{:S(2)}, u32[]{:S(2)}) %collective-permute-start.19) | collective-permute-done | bytes 65568 | tf_op jit(solution)/shard_map/ppermute | solution.py:351
  50.8 1.0 %collective-permute-start.21 = (bf16[2,128,128]{2,1,0:T(8,128)(2,1)S(1)}, bf16[2,128,128]{2,1,0:T(8,128)(2,1)S(1)}, u32[]{:S(2)}, u32[]{:S(2)}) collective-permute-start(bf16[2,128,128]{2,1,0:T(8,128)(2,1)S(1)} %get-tuple-element.61), channel_id=1, source_target_pairs={{0,12},{2,14},{4,8},{6,10},{8,4},{10,6},{12,0},{14,2},{1,13},{3,15... | collective-permute-start | bytes 196616 | tf_op jit(solution)/shard_map/ppermute | solution.py:351
  51.8 2.8 %collective-permute-start.22 = (bf16[2,128,128]{2,1,0:T(8,128)(2,1)S(1)}, bf16[2,128,128]{2,1,0:T(8,128)(2,1)S(1)}, u32[]{:S(2)}, u32[]{:S(2)}) collective-permute-start(bf16[2,128,128]{2,1,0:T(8,128)(2,1)S(1)} %get-tuple-element.62), channel_id=1, source_target_pairs={{0,14},{2,12},{4,10},{6,8},{8,6},{10,4},{12,2},{14,0},{1,15},{3,13... | collective-permute-start | bytes 196616 | tf_op jit(solution)/shard_map/ppermute | solution.py:351
  54.6 3.2 %collective-permute-done.21.refs_6_ = bf16[2,128,128]{2,1,0:T(8,128)(2,1)S(1)} collective-permute-done((bf16[2,128,128]{2,1,0:T(8,128)(2,1)S(1)}, bf16[2,128,128]{2,1,0:T(8,128)(2,1)S(1)}, u32[]{:S(2)}, u32[]{:S(2)}) %collective-permute-start.21) | collective-permute-done | bytes 65568 | tf_op jit(solution)/shard_map/ppermute | solution.py:351
  57.8 2.5 %collective-permute-done.22.refs_7_ = bf16[2,128,128]{2,1,0:T(8,128)(2,1)S(1)} collective-permute-done((bf16[2,128,128]{2,1,0:T(8,128)(2,1)S(1)}, bf16[2,128,128]{2,1,0:T(8,128)(2,1)S(1)}, u32[]{:S(2)}, u32[]{:S(2)}) %collective-permute-start.22) | collective-permute-done | bytes 65568 | tf_op jit(solution)/shard_map/ppermute | solution.py:351
  60.4 2.1 %collective-permute-start.16 = (bf16[2,128,128]{2,1,0:T(8,128)(2,1)S(1)}, bf16[2,128,128]{2,1,0:T(8,128)(2,1)S(1)}, u32[]{:S(2)}, u32[]{:S(2)}) collective-permute-start(bf16[2,128,128]{2,1,0:T(8,128)(2,1)S(1)} %get-tuple-element.56), channel_id=1, source_target_pairs={{0,10},{2,8},{4,14},{6,12},{8,2},{10,0},{12,6},{14,4},{1,11},{3,9}... | collective-permute-start | bytes 196616 | tf_op jit(solution)/shard_map/ppermute | solution.py:351
  62.5 0.4 collective-permute-start.17
  62.9 2.6 %collective-permute-start.18 = (bf16[2,128,128]{2,1,0:T(8,128)(2,1)S(1)}, bf16[2,128,128]{2,1,0:T(8,128)(2,1)S(1)}, u32[]{:S(2)}, u32[]{:S(2)}) collective-permute-start(bf16[2,128,128]{2,1,0:T(8,128)(2,1)S(1)} %get-tuple-element.58), channel_id=1, source_target_pairs={{0,14},{2,12},{4,10},{6,8},{8,6},{10,4},{12,2},{14,0},{1,15},{3,13... | collective-permute-start | bytes 196616 | tf_op jit(solution)/shard_map/ppermute | solution.py:351
  65.5 4.8 %inverse.2.refs_8_ = bf16[256,256,128]{2,1,0:T(8,128)(2,1)} custom-call(s32[2]{0:T(128)S(1)} %pad_add_fusion.me_ref.place_ref, bf16[2,4096,128]{2,1,0:T(8,128)(2,1)S(1)} %copy-done, bf16[2,256,128]{2,1,0:T(8,128)(2,1)S(1)} %get-tuple-element.50.refs_0_, bf16[2,256,128]{2,1,0:T(8,128)(2,1)S(1)} %collective-permute-done.12.refs_1_, ...), custom_call_target="tpu_custom_call" | custom-call | flops 2147483648 | bytes 8388608 | tf_op jit(solution)/shard_map/inverse/pallas_call | solution.py:325
  70.4 4.9 %inverse.3 = bf16[256,256,128]{2,1,0:T(8,128)(2,1)} custom-call(s32[2]{0:T(128)S(1)} %pad_add_fusion.me_ref.place_ref, bf16[2,4096,128]{2,1,0:T(8,128)(2,1)S(1)} %copy-done, bf16[2,256,128]{2,1,0:T(8,128)(2,1)S(1)} %get-tuple-element.50.refs_0_, bf16[2,256,128]{2,1,0:T(8,128)(2,1)S(1)} %collective-permute-done.12.refs_1_, ...), custom_call_target="tpu_custom_call", output_to_operand_aliasing={{}: (10, {})} | custom-call | flops 2147483648 | bytes 8388608 | tf_op jit(solution)/shard_map/inverse/pallas_call | solution.py:325
  (32 shorter events, 0.2 us)
Async XLA Ops:
  0.0 20.1 %collective-permute-start = (bf16[40,2,128,128]{3,2,1,0:T(8,128)(2,1)}, bf16[40,2,128,128]{3,2,1,0:T(8,128)(2,1)S(1)}, u32[]{:S(2)}, u32[]{:S(2)}) collective-permute-start(bf16[40,2,128,128]{3,2,1,0:T(8,128)(2,1)} %bitcast.3), channel_id=1, source_target_pairs={{0,1},{1,0},{2,3},{3,2},{4,5},{5,4},{6,7},{7,6},{8,9},{9,8},{10,11... | collective-permute-start | bytes 7864328 | tf_op jit(solution)/shard_map/ppermute | solution.py:375
  0.5 1.2 %copy-start.1 = (bf16[33,128,128]{2,1,0:T(8,128)(2,1)S(1)}, bf16[33,128,128]{2,1,0:T(8,128)(2,1)}, u32[]{:S(2)}) copy-start(bf16[33,128,128]{2,1,0:T(8,128)(2,1)} %constant.12.clone.table_hbm) | copy-start | bytes 3244036
  6.4 14.8 %collective-permute-start.4 = (bf16[2,128,128]{2,1,0:T(8,128)(2,1)S(1)}, bf16[2,128,128]{2,1,0:T(8,128)(2,1)S(1)}, u32[]{:S(2)}, u32[]{:S(2)}) collective-permute-start(bf16[2,128,128]{2,1,0:T(8,128)(2,1)S(1)} %get-tuple-element.42), channel_id=1, source_target_pairs={{0,8},{2,10},{4,12},{6,14},{8,0},{10,2},{12,4},{14,6},{1,9},{3,11}... | collective-permute-start | bytes 196616 | tf_op jit(solution)/shard_map/ppermute | solution.py:351
  10.1 14.3 %collective-permute-start.5 = (bf16[2,128,128]{2,1,0:T(8,128)(2,1)S(1)}, bf16[2,128,128]{2,1,0:T(8,128)(2,1)S(1)}, u32[]{:S(2)}, u32[]{:S(2)}) collective-permute-start(bf16[2,128,128]{2,1,0:T(8,128)(2,1)S(1)} %get-tuple-element.43), channel_id=1, source_target_pairs={{0,10},{2,8},{4,14},{6,12},{8,2},{10,0},{12,6},{14,4},{1,11},{3,9}... | collective-permute-start | bytes 196616 | tf_op jit(solution)/shard_map/ppermute | solution.py:351
  11.4 13.3 %collective-permute-start.6 = (bf16[2,128,128]{2,1,0:T(8,128)(2,1)S(1)}, bf16[2,128,128]{2,1,0:T(8,128)(2,1)S(1)}, u32[]{:S(2)}, u32[]{:S(2)}) collective-permute-start(bf16[2,128,128]{2,1,0:T(8,128)(2,1)S(1)} %get-tuple-element.44), channel_id=1, source_target_pairs={{0,12},{2,14},{4,8},{6,10},{8,4},{10,6},{12,0},{14,2},{1,13},{3,15... | collective-permute-start | bytes 196616 | tf_op jit(solution)/shard_map/ppermute | solution.py:351
  15.0 11.3 %collective-permute-start.7 = (bf16[2,128,128]{2,1,0:T(8,128)(2,1)S(1)}, bf16[2,128,128]{2,1,0:T(8,128)(2,1)S(1)}, u32[]{:S(2)}, u32[]{:S(2)}) collective-permute-start(bf16[2,128,128]{2,1,0:T(8,128)(2,1)S(1)} %get-tuple-element.45), channel_id=1, source_target_pairs={{0,14},{2,12},{4,10},{6,8},{8,6},{10,4},{12,2},{14,0},{1,15},{3,13... | collective-permute-start | bytes 196616 | tf_op jit(solution)/shard_map/ppermute | solution.py:351
  15.0 23.5 %copy-start.2 = (bf16[1,40,2,128,128]{4,3,2,1,0:T(8,128)(2,1)S(1)}, bf16[1,40,2,128,128]{4,3,2,1,0:T(8,128)(2,1)}, u32[]{:S(2)}) copy-start(bf16[1,40,2,128,128]{4,3,2,1,0:T(8,128)(2,1)} %param.9) | copy-start | bytes 7864324
  15.0 23.5 %copy-start.3 = (s32[1,16]{1,0:T(1,128)S(1)}, s32[1,16]{1,0:T(1,128)}, u32[]{:S(2)}) copy-start(s32[1,16]{1,0:T(1,128)} %count_ref.1) | copy-start | bytes 196
  15.0 23.5 %copy-start.4 = (s32[1,80]{1,0:T(1,128)S(1)}, s32[1,80]{1,0:T(1,128)}, u32[]{:S(2)}) copy-start(s32[1,80]{1,0:T(1,128)} %column_ref.1) | copy-start | bytes 964
  20.1 7.7 %collective-permute-start.8 = (bf16[2,128,128]{2,1,0:T(8,128)(2,1)S(1)}, bf16[2,128,128]{2,1,0:T(8,128)(2,1)S(1)}, u32[]{:S(2)}, u32[]{:S(2)}) collective-permute-start(bf16[2,128,128]{2,1,0:T(8,128)(2,1)S(1)} %get-tuple-element.46), channel_id=1, source_target_pairs={{0,8},{2,10},{4,12},{6,14},{8,0},{10,2},{12,4},{14,6},{1,9},{3,11}... | collective-permute-start | bytes 196616 | tf_op jit(solution)/shard_map/ppermute | solution.py:351
  21.2 10.2 %collective-permute-start.9 = (bf16[2,128,128]{2,1,0:T(8,128)(2,1)S(1)}, bf16[2,128,128]{2,1,0:T(8,128)(2,1)S(1)}, u32[]{:S(2)}, u32[]{:S(2)}) collective-permute-start(bf16[2,128,128]{2,1,0:T(8,128)(2,1)S(1)} %get-tuple-element.47), channel_id=1, source_target_pairs={{0,10},{2,8},{4,14},{6,12},{8,2},{10,0},{12,6},{14,4},{1,11},{3,9}... | collective-permute-start | bytes 196616 | tf_op jit(solution)/shard_map/ppermute | solution.py:351
  24.4 14.1 %collective-permute-start.1 = (bf16[2,256,128]{2,1,0:T(8,128)(2,1)S(1)}, bf16[2,256,128]{2,1,0:T(8,128)(2,1)S(1)}, u32[]{:S(2)}, u32[]{:S(2)}) collective-permute-start(bf16[2,256,128]{2,1,0:T(8,128)(2,1)S(1)} %get-tuple-element.39), channel_id=1, source_target_pairs={{0,2},{2,0},{4,6},{6,4},{8,10},{10,8},{12,14},{14,12},{1,3},{3,1},... | collective-permute-start | bytes 393224 | tf_op jit(solution)/shard_map/ppermute | solution.py:351
  24.7 13.7 %collective-permute-start.2 = (bf16[2,256,128]{2,1,0:T(8,128)(2,1)S(1)}, bf16[2,256,128]{2,1,0:T(8,128)(2,1)S(1)}, u32[]{:S(2)}, u32[]{:S(2)}) collective-permute-start(bf16[2,256,128]{2,1,0:T(8,128)(2,1)S(1)} %get-tuple-element.40), channel_id=1, source_target_pairs={{0,4},{2,6},{4,0},{6,2},{8,12},{10,14},{12,8},{14,10},{1,5},{3,7},... | collective-permute-start | bytes 393224 | tf_op jit(solution)/shard_map/ppermute | solution.py:351
  26.3 12.2 %collective-permute-start.3 = (bf16[2,256,128]{2,1,0:T(8,128)(2,1)S(1)}, bf16[2,256,128]{2,1,0:T(8,128)(2,1)S(1)}, u32[]{:S(2)}, u32[]{:S(2)}) collective-permute-start(bf16[2,256,128]{2,1,0:T(8,128)(2,1)S(1)} %get-tuple-element.41), channel_id=1, source_target_pairs={{0,6},{2,4},{4,2},{6,0},{8,14},{10,12},{12,10},{14,8},{1,7},{3,5},... | collective-permute-start | bytes 393224 | tf_op jit(solution)/shard_map/ppermute | solution.py:351
  27.9 8.8 %collective-permute-start.10 = (bf16[2,128,128]{2,1,0:T(8,128)(2,1)S(1)}, bf16[2,128,128]{2,1,0:T(8,128)(2,1)S(1)}, u32[]{:S(2)}, u32[]{:S(2)}) collective-permute-start(bf16[2,128,128]{2,1,0:T(8,128)(2,1)S(1)} %get-tuple-element.48), channel_id=1, source_target_pairs={{0,12},{2,14},{4,8},{6,10},{8,4},{10,6},{12,0},{14,2},{1,13},{3,15... | collective-permute-start | bytes 196616 | tf_op jit(solution)/shard_map/ppermute | solution.py:351
  31.5 7.0 %collective-permute-start.11 = (bf16[2,128,128]{2,1,0:T(8,128)(2,1)S(1)}, bf16[2,128,128]{2,1,0:T(8,128)(2,1)S(1)}, u32[]{:S(2)}, u32[]{:S(2)}) collective-permute-start(bf16[2,128,128]{2,1,0:T(8,128)(2,1)S(1)} %get-tuple-element.49), channel_id=1, source_target_pairs={{0,14},{2,12},{4,10},{6,8},{8,6},{10,4},{12,2},{14,0},{1,15},{3,13... | collective-permute-start | bytes 196616 | tf_op jit(solution)/shard_map/ppermute | solution.py:351
  38.5 27.0 %copy-start = (bf16[2,4096,128]{2,1,0:T(8,128)(2,1)S(1)}, bf16[2,4096,128]{2,1,0:T(8,128)(2,1)}, u32[]{:S(2)}) copy-start(bf16[2,4096,128]{2,1,0:T(8,128)(2,1)} %constant.13.clone.table_ref) | copy-start | bytes 6291460
  42.9 7.9 %collective-permute-start.19 = (bf16[2,128,128]{2,1,0:T(8,128)(2,1)S(1)}, bf16[2,128,128]{2,1,0:T(8,128)(2,1)S(1)}, u32[]{:S(2)}, u32[]{:S(2)}) collective-permute-start(bf16[2,128,128]{2,1,0:T(8,128)(2,1)S(1)} %get-tuple-element.59), channel_id=1, source_target_pairs={{0,8},{2,10},{4,12},{6,14},{8,0},{10,2},{12,4},{14,6},{1,9},{3,11}... | collective-permute-start | bytes 196616 | tf_op jit(solution)/shard_map/ppermute | solution.py:351
  43.0 8.8 %collective-permute-start.20 = (bf16[2,128,128]{2,1,0:T(8,128)(2,1)S(1)}, bf16[2,128,128]{2,1,0:T(8,128)(2,1)S(1)}, u32[]{:S(2)}, u32[]{:S(2)}) collective-permute-start(bf16[2,128,128]{2,1,0:T(8,128)(2,1)S(1)} %get-tuple-element.60), channel_id=1, source_target_pairs={{0,10},{2,8},{4,14},{6,12},{8,2},{10,0},{12,6},{14,4},{1,11},{3,9}... | collective-permute-start | bytes 196616 | tf_op jit(solution)/shard_map/ppermute | solution.py:351
  46.1 16.4 %collective-permute-start.12 = (bf16[2,256,128]{2,1,0:T(8,128)(2,1)S(1)}, bf16[2,256,128]{2,1,0:T(8,128)(2,1)S(1)}, u32[]{:S(2)}, u32[]{:S(2)}) collective-permute-start(bf16[2,256,128]{2,1,0:T(8,128)(2,1)S(1)} %get-tuple-element.51), channel_id=1, source_target_pairs={{0,2},{2,0},{4,6},{6,4},{8,10},{10,8},{12,14},{14,12},{1,3},{3,1},... | collective-permute-start | bytes 393224 | tf_op jit(solution)/shard_map/ppermute | solution.py:351
  47.4 15.5 %collective-permute-start.13 = (bf16[2,256,128]{2,1,0:T(8,128)(2,1)S(1)}, bf16[2,256,128]{2,1,0:T(8,128)(2,1)S(1)}, u32[]{:S(2)}, u32[]{:S(2)}) collective-permute-start(bf16[2,256,128]{2,1,0:T(8,128)(2,1)S(1)} %get-tuple-element.52), channel_id=1, source_target_pairs={{0,4},{2,6},{4,0},{6,2},{8,12},{10,14},{12,8},{14,10},{1,5},{3,7},... | collective-permute-start | bytes 393224 | tf_op jit(solution)/shard_map/ppermute | solution.py:351
  47.9 17.6 %collective-permute-start.14 = (bf16[2,256,128]{2,1,0:T(8,128)(2,1)S(1)}, bf16[2,256,128]{2,1,0:T(8,128)(2,1)S(1)}, u32[]{:S(2)}, u32[]{:S(2)}) collective-permute-start(bf16[2,256,128]{2,1,0:T(8,128)(2,1)S(1)} %get-tuple-element.53), channel_id=1, source_target_pairs={{0,6},{2,4},{4,2},{6,0},{8,14},{10,12},{12,10},{14,8},{1,7},{3,5},... | collective-permute-start | bytes 393224 | tf_op jit(solution)/shard_map/ppermute | solution.py:351
  50.8 7.0 %collective-permute-start.21 = (bf16[2,128,128]{2,1,0:T(8,128)(2,1)S(1)}, bf16[2,128,128]{2,1,0:T(8,128)(2,1)S(1)}, u32[]{:S(2)}, u32[]{:S(2)}) collective-permute-start(bf16[2,128,128]{2,1,0:T(8,128)(2,1)S(1)} %get-tuple-element.61), channel_id=1, source_target_pairs={{0,12},{2,14},{4,8},{6,10},{8,4},{10,6},{12,0},{14,2},{1,13},{3,15... | collective-permute-start | bytes 196616 | tf_op jit(solution)/shard_map/ppermute | solution.py:351
  51.8 8.6 %collective-permute-start.22 = (bf16[2,128,128]{2,1,0:T(8,128)(2,1)S(1)}, bf16[2,128,128]{2,1,0:T(8,128)(2,1)S(1)}, u32[]{:S(2)}, u32[]{:S(2)}) collective-permute-start(bf16[2,128,128]{2,1,0:T(8,128)(2,1)S(1)} %get-tuple-element.62), channel_id=1, source_target_pairs={{0,14},{2,12},{4,10},{6,8},{8,6},{10,4},{12,2},{14,0},{1,15},{3,13... | collective-permute-start | bytes 196616 | tf_op jit(solution)/shard_map/ppermute | solution.py:351
  57.8 12.5 %collective-permute-start.15 = (bf16[2,128,128]{2,1,0:T(8,128)(2,1)S(1)}, bf16[2,128,128]{2,1,0:T(8,128)(2,1)S(1)}, u32[]{:S(2)}, u32[]{:S(2)}) collective-permute-start(bf16[2,128,128]{2,1,0:T(8,128)(2,1)S(1)} %get-tuple-element.55), channel_id=1, source_target_pairs={{0,8},{2,10},{4,12},{6,14},{8,0},{10,2},{12,4},{14,6},{1,9},{3,11}... | collective-permute-start | bytes 196616 | tf_op jit(solution)/shard_map/ppermute | solution.py:351
  60.4 10.0 %collective-permute-start.16 = (bf16[2,128,128]{2,1,0:T(8,128)(2,1)S(1)}, bf16[2,128,128]{2,1,0:T(8,128)(2,1)S(1)}, u32[]{:S(2)}, u32[]{:S(2)}) collective-permute-start(bf16[2,128,128]{2,1,0:T(8,128)(2,1)S(1)} %get-tuple-element.56), channel_id=1, source_target_pairs={{0,10},{2,8},{4,14},{6,12},{8,2},{10,0},{12,6},{14,4},{1,11},{3,9}... | collective-permute-start | bytes 196616 | tf_op jit(solution)/shard_map/ppermute | solution.py:351
  62.5 7.9 %collective-permute-start.17 = (bf16[2,128,128]{2,1,0:T(8,128)(2,1)S(1)}, bf16[2,128,128]{2,1,0:T(8,128)(2,1)S(1)}, u32[]{:S(2)}, u32[]{:S(2)}) collective-permute-start(bf16[2,128,128]{2,1,0:T(8,128)(2,1)S(1)} %get-tuple-element.57), channel_id=1, source_target_pairs={{0,12},{2,14},{4,8},{6,10},{8,4},{10,6},{12,0},{14,2},{1,13},{3,15... | collective-permute-start | bytes 196616 | tf_op jit(solution)/shard_map/ppermute | solution.py:351
  62.9 7.5 %collective-permute-start.18 = (bf16[2,128,128]{2,1,0:T(8,128)(2,1)S(1)}, bf16[2,128,128]{2,1,0:T(8,128)(2,1)S(1)}, u32[]{:S(2)}, u32[]{:S(2)}) collective-permute-start(bf16[2,128,128]{2,1,0:T(8,128)(2,1)S(1)} %get-tuple-element.58), channel_id=1, source_target_pairs={{0,14},{2,12},{4,10},{6,8},{8,6},{10,4},{12,2},{14,0},{1,15},{3,13... | collective-permute-start | bytes 196616 | tf_op jit(solution)/shard_map/ppermute | solution.py:351

commit v6 on v5

--- a/solution.py
+++ b/solution.py
@@ -135,7 +135,7 @@
     return pl.pallas_call(
         functools.partial(forward_kernel, first, step),
         in_specs=[pl.BlockSpec(memory_space=pltpu.SMEM)]
-        + [pl.BlockSpec(memory_space=pl.ANY)] * 2
+        + [pl.BlockSpec(memory_space=pltpu.HBM)] * 2
         + [pl.BlockSpec(memory_space=pltpu.VMEM)] * len(extra),
         out_specs=[pl.BlockSpec(memory_space=pltpu.VMEM)] * len(shapes),
         scratch_shapes=[
@@ -157,7 +157,7 @@
 
 def tiles_kernel(near, chunks, block, count_ref, column_ref, place_ref, own_hbm, other_hbm, *refs):
     rows, width = refs[0].shape[1:]
-    far = refs[-7].shape[0] if len(chunks) > 1 else (len(refs) - 6) // 2 - near
+    far = (len(refs) - 6 - 2 * near) // (2 * len(chunks))
     ins = near + far * len(chunks)
     near_in, far_in = refs[:near], refs[near:ins]
     near_out, far_out = refs[ins : ins + near], refs[ins + near : -6]
@@ -222,11 +222,9 @@
 
     for k in range(near):
         give(k, 0, rows, near_out[k])
-    for j in range(far):
-        give(near + j, *chunks[0], far_out[j])
-    for ref in far_out[far:]:
+    for q, (first, count) in enumerate(chunks):
         for j in range(far):
-            give(near + j, *chunks[1], ref.at[j])
+            give(near + j, first, count, far_out[q * far + j])
 
 
 def apply_tiles(counts, columns, place, own, other, chunks, nears, fars):
@@ -235,12 +233,12 @@
     far = len(fars) // len(chunks)
     total = (len(nears) + far) * rows
     block = math.gcd(20, halves)
-    shapes = [nears[0].shape] * len(nears) + [(2, chunks[0][1], width)] * far
-    shapes += [(far, 2, part, width) for _, part in chunks[1:]]
+    shapes = [nears[0].shape] * len(nears)
+    shapes += [(2, part, width) for _, part in chunks for _ in range(far)]
     return pl.pallas_call(
         functools.partial(tiles_kernel, len(nears), chunks, block),
         in_specs=[pl.BlockSpec(memory_space=pltpu.SMEM)] * 3
-        + [pl.BlockSpec(memory_space=pl.ANY)] * 2
+        + [pl.BlockSpec(memory_space=pltpu.HBM)] * 2
         + [pl.BlockSpec(memory_space=pltpu.VMEM)] * (len(nears) + len(fars)),
         out_specs=[pl.BlockSpec(memory_space=pltpu.VMEM)] * len(shapes),
         scratch_shapes=[
@@ -371,17 +369,20 @@
     got = []
     for first, count in chunks:
         early, *blocks = forward(me, forward_table, traces, near, first, count, early)
+        if not first:
+            own_tiles, early = lax.optimization_barrier((tiles[0], early))
         got += [send(block, k, parties) for k, block in zip(far, blocks)]
-    other = lax.ppermute(tiles[0], "narrow", [(0, 1), (1, 0)])
+    other = lax.ppermute(own_tiles, "narrow", [(0, 1), (1, 0)])
     other, early = lax.optimization_barrier((other, early))
     nears = [send(block, k, parties) for k, block in enumerate(split(early))]
 
-    sums = apply_tiles(row_counts, tile_cols, me, tiles[0], other, chunks, nears, got)
-    nears, blocks, late = sums[:near], sums[near:parties], sums[parties:]
-    got = [[send(block, k, parties) for k, block in zip(far, blocks)]]
+    sums = apply_tiles(row_counts, tile_cols, me, own_tiles, other, chunks, nears, got)
+    nears, blocks = sums[:near], sums[near:]
     nears = [send(block, k, parties) for k, block in enumerate(nears)]
-    for blocks in late:
-        got.append([send(block, k, parties) for k, block in zip(far, split(blocks))])
+    got = [
+        [send(block, k, parties) for k, block in zip(far, blocks[q * len(far) :])]
+        for q in range(len(chunks))
+    ]
     result = None
     for (first, count), blocks in zip(chunks, got):
         result = inverse(me, inverse_table, nears, blocks, first, count, result)

time: 75.4 us -> 75.6 us (level)
  transfers between devices with their start and end apart: 23 -> 23, of which waited for: 5 -> 5; matrix products, arithmetic and copies ran while one was open for 0% -> 0% of each run, Pallas kernels for 20% -> 13%
where the time goes in v6:
time: 75.6 us; the launch traced here: 75.5 us
  starting transfers between devices  37.1 us (49%)
  Pallas kernels  23.8 us (31%)
  waiting for transfers between devices  13.1 us (17%)
  local copies, waits for them, and re-layouts  1.25 us (2%)
    ppermute x22, starting transfers between devices, send(): lax.ppermute(block, 'wide', [(i, i ^ k) for i in range(parties)])  36.5 us
    ppermute x22, waiting for transfers between devices, send(): lax.ppermute(block, 'wide', [(i, i ^ k) for i in range(parties)])  13.1 us
    pallas_call x2, Pallas kernels, inverse(): pl.pallas_call(functools.partial(inverse_kernel, first, step, parties, le...  9.71 us
    pallas_call x2, Pallas kernels, forward(): pl.pallas_call(functools.partial(forward_kernel, first, step), in_specs=[...  9.66 us
    pallas_call x1, Pallas kernels, apply_tiles(): pl.pallas_call(functools.partial(tiles_kernel, len(nears), chunks, block)...  4.44 us
  transfers between devices with their start and end apart: 23, of which 5 were waited for; matrix products, arithmetic and copies ran while one was open for 0% of the time, Pallas kernels for 13%

profile of v6, /device:TPU:0, one launch (start us, length us, event | category | flops | bytes accessed | tf_op | source)
XLA Modules:
  0.0 75.5 jit_solution(16860543010399175045)
XLA Ops:
  0.0 0.1 pad_add_fusion.me_ref.place_ref
  0.1 1.2 %copy-done.1 = bf16[33,128,128]{2,1,0:T(8,128)(2,1)S(1)} copy-done((bf16[33,128,128]{2,1,0:T(8,128)(2,1)S(1)}, bf16[33,128,128]{2,1,0:T(8,128)(2,1)}, u32[]{:S(2)}) %copy-start.1) | copy-done | bytes 1081368
  1.3 4.8 %forward.2 = (bf16[4,2,128,128]{3,2,1,0:T(8,128)(2,1)S(1)}, bf16[2,128,128]{2,1,0:T(8,128)(2,1)S(1)}, bf16[2,128,128]{2,1,0:T(8,128)(2,1)S(1)}, bf16[2,128,128]{2,1,0:T(8,128)(2,1)S(1)}, bf16[2,128,128]{2,1,0:T(8,128)(2,1)S(1)}) custom-call(s32[2]{0:T(128)S(1)} %pad_add_fusion.me_ref.place_ref, bf16[33,128,128]{2,1,0:T(8,128)(2,1)S(1)} %copy-done.1, ...), custom_call_target="tpu_custom_call" | custom-call | flops 2147483648 | bytes 8388608 | tf_op jit(solution)/shard_map/forward/pallas_call | solution.py:135
  6.1 0.5 collective-permute-start
  6.6 3.7 %collective-permute-start.4 = (bf16[2,128,128]{2,1,0:T(8,128)(2,1)S(1)}, bf16[2,128,128]{2,1,0:T(8,128)(2,1)S(1)}, u32[]{:S(2)}, u32[]{:S(2)}) collective-permute-start(bf16[2,128,128]{2,1,0:T(8,128)(2,1)S(1)} %get-tuple-element.45), channel_id=1, source_target_pairs={{0,8},{2,10},{4,12},{6,14},{8,0},{10,2},{12,4},{14,6},{1,9},{3,11}... | collective-permute-start | bytes 196616 | tf_op jit(solution)/shard_map/ppermute | solution.py:349
  10.3 1.3 %collective-permute-start.5 = (bf16[2,128,128]{2,1,0:T(8,128)(2,1)S(1)}, bf16[2,128,128]{2,1,0:T(8,128)(2,1)S(1)}, u32[]{:S(2)}, u32[]{:S(2)}) collective-permute-start(bf16[2,128,128]{2,1,0:T(8,128)(2,1)S(1)} %get-tuple-element.46), channel_id=1, source_target_pairs={{0,10},{2,8},{4,14},{6,12},{8,2},{10,0},{12,6},{14,4},{1,11},{3,9}... | collective-permute-start | bytes 196616 | tf_op jit(solution)/shard_map/ppermute | solution.py:349
  11.6 3.6 %collective-permute-start.6 = (bf16[2,128,128]{2,1,0:T(8,128)(2,1)S(1)}, bf16[2,128,128]{2,1,0:T(8,128)(2,1)S(1)}, u32[]{:S(2)}, u32[]{:S(2)}) collective-permute-start(bf16[2,128,128]{2,1,0:T(8,128)(2,1)S(1)} %get-tuple-element.47), channel_id=1, source_target_pairs={{0,12},{2,14},{4,8},{6,10},{8,4},{10,6},{12,0},{14,2},{1,13},{3,15... | collective-permute-start | bytes 196616 | tf_op jit(solution)/shard_map/ppermute | solution.py:349
  15.2 4.9 %forward.3 = (bf16[4,2,256,128]{3,2,1,0:T(8,128)(2,1)S(1)}, bf16[2,128,128]{2,1,0:T(8,128)(2,1)S(1)}, bf16[2,128,128]{2,1,0:T(8,128)(2,1)S(1)}, bf16[2,128,128]{2,1,0:T(8,128)(2,1)S(1)}, bf16[2,128,128]{2,1,0:T(8,128)(2,1)S(1)}) custom-call(s32[2]{0:T(128)S(1)} %pad_add_fusion.me_ref.place_ref, bf16[33,128,128]{2,1,0:T(8,128)(2,1)} %constant.12.clone.table_hbm, ...), custom_call_target="tpu_custom_call" | custom-call | flops 2147483648 | bytes 8388608 | tf_op jit(solution)/shard_map/forward/pallas_call | solution.py:135
  20.1 1.0 %collective-permute-start.8 = (bf16[2,128,128]{2,1,0:T(8,128)(2,1)S(1)}, bf16[2,128,128]{2,1,0:T(8,128)(2,1)S(1)}, u32[]{:S(2)}, u32[]{:S(2)}) collective-permute-start(bf16[2,128,128]{2,1,0:T(8,128)(2,1)S(1)} %get-tuple-element.49), channel_id=1, source_target_pairs={{0,8},{2,10},{4,12},{6,14},{8,0},{10,2},{12,4},{14,6},{1,9},{3,11}... | collective-permute-start | bytes 196616 | tf_op jit(solution)/shard_map/ppermute | solution.py:349
  21.2 3.2 %collective-permute-start.9 = (bf16[2,128,128]{2,1,0:T(8,128)(2,1)S(1)}, bf16[2,128,128]{2,1,0:T(8,128)(2,1)S(1)}, u32[]{:S(2)}, u32[]{:S(2)}) collective-permute-start(bf16[2,128,128]{2,1,0:T(8,128)(2,1)S(1)} %get-tuple-element.50), channel_id=1, source_target_pairs={{0,10},{2,8},{4,14},{6,12},{8,2},{10,0},{12,6},{14,4},{1,11},{3,9}... | collective-permute-start | bytes 196616 | tf_op jit(solution)/shard_map/ppermute | solution.py:349
  24.3 0.3 collective-permute-start.1
  24.6 1.6 %collective-permute-start.2 = (bf16[2,256,128]{2,1,0:T(8,128)(2,1)S(1)}, bf16[2,256,128]{2,1,0:T(8,128)(2,1)S(1)}, u32[]{:S(2)}, u32[]{:S(2)}) collective-permute-start(bf16[2,256,128]{2,1,0:T(8,128)(2,1)S(1)} %get-tuple-element.43), channel_id=1, source_target_pairs={{0,4},{2,6},{4,0},{6,2},{8,12},{10,14},{12,8},{14,10},{1,5},{3,7},... | collective-permute-start | bytes 393224 | tf_op jit(solution)/shard_map/ppermute | solution.py:349
  26.2 1.6 %collective-permute-start.3 = (bf16[2,256,128]{2,1,0:T(8,128)(2,1)S(1)}, bf16[2,256,128]{2,1,0:T(8,128)(2,1)S(1)}, u32[]{:S(2)}, u32[]{:S(2)}) collective-permute-start(bf16[2,256,128]{2,1,0:T(8,128)(2,1)S(1)} %get-tuple-element.44), channel_id=1, source_target_pairs={{0,6},{2,4},{4,2},{6,0},{8,14},{10,12},{12,10},{14,8},{1,7},{3,5},... | collective-permute-start | bytes 393224 | tf_op jit(solution)/shard_map/ppermute | solution.py:349
  27.8 3.6 %collective-permute-start.10 = (bf16[2,128,128]{2,1,0:T(8,128)(2,1)S(1)}, bf16[2,128,128]{2,1,0:T(8,128)(2,1)S(1)}, u32[]{:S(2)}, u32[]{:S(2)}) collective-permute-start(bf16[2,128,128]{2,1,0:T(8,128)(2,1)S(1)} %get-tuple-element.51), channel_id=1, source_target_pairs={{0,12},{2,14},{4,8},{6,10},{8,4},{10,6},{12,0},{14,2},{1,13},{3,15... | collective-permute-start | bytes 196616 | tf_op jit(solution)/shard_map/ppermute | solution.py:349
  31.4 1.6 %collective-permute-start.11 = (bf16[2,128,128]{2,1,0:T(8,128)(2,1)S(1)}, bf16[2,128,128]{2,1,0:T(8,128)(2,1)S(1)}, u32[]{:S(2)}, u32[]{:S(2)}) collective-permute-start(bf16[2,128,128]{2,1,0:T(8,128)(2,1)S(1)} %get-tuple-element.52), channel_id=1, source_target_pairs={{0,14},{2,12},{4,10},{6,8},{8,6},{10,4},{12,2},{14,0},{1,15},{3,13... | collective-permute-start | bytes 196616 | tf_op jit(solution)/shard_map/ppermute | solution.py:349
  33.0 3.2 %collective-permute-done.10.refs_10_ = bf16[2,128,128]{2,1,0:T(8,128)(2,1)S(1)} collective-permute-done((bf16[2,128,128]{2,1,0:T(8,128)(2,1)S(1)}, bf16[2,128,128]{2,1,0:T(8,128)(2,1)S(1)}, u32[]{:S(2)}, u32[]{:S(2)}) %collective-permute-start.10) | collective-permute-done | bytes 65568 | tf_op jit(solution)/shard_map/ppermute | solution.py:349
  36.2 2.2 %collective-permute-done.11.refs_11_ = bf16[2,128,128]{2,1,0:T(8,128)(2,1)S(1)} collective-permute-done((bf16[2,128,128]{2,1,0:T(8,128)(2,1)S(1)}, bf16[2,128,128]{2,1,0:T(8,128)(2,1)S(1)}, u32[]{:S(2)}, u32[]{:S(2)}) %collective-permute-start.11) | collective-permute-done | bytes 65568 | tf_op jit(solution)/shard_map/ppermute | solution.py:349
  38.4 4.4 %tiles.1 = (bf16[2,256,128]{2,1,0:T(8,128)(2,1)S(1)}, bf16[2,256,128]{2,1,0:T(8,128)(2,1)S(1)}, bf16[2,256,128]{2,1,0:T(8,128)(2,1)S(1)}, bf16[2,256,128]{2,1,0:...) custom-call(s32[1,16]{1,0:T(1,128)S(1)} %copy-done.3, ...), custom_call_target="tpu_custom_call" | custom-call | flops 1342177280 | bytes 5242880 | tf_op jit(solution)/shard_map/tiles/pallas_call | solution.py:238
  42.9 3.2 %collective-permute-start.20 = (bf16[2,128,128]{2,1,0:T(8,128)(2,1)S(1)}, bf16[2,128,128]{2,1,0:T(8,128)(2,1)S(1)}, u32[]{:S(2)}, u32[]{:S(2)}) collective-permute-start(bf16[2,128,128]{2,1,0:T(8,128)(2,1)S(1)} %get-tuple-element.62), channel_id=1, source_target_pairs={{0,10},{2,8},{4,14},{6,12},{8,2},{10,0},{12,6},{14,4},{1,11},{3,9}... | collective-permute-start | bytes 196616 | tf_op jit(solution)/shard_map/ppermute | solution.py:349
  46.1 1.2 %collective-permute-start.12 = (bf16[2,256,128]{2,1,0:T(8,128)(2,1)S(1)}, bf16[2,256,128]{2,1,0:T(8,128)(2,1)S(1)}, u32[]{:S(2)}, u32[]{:S(2)}) collective-permute-start(bf16[2,256,128]{2,1,0:T(8,128)(2,1)S(1)} %get-tuple-element.54), channel_id=1, source_target_pairs={{0,2},{2,0},{4,6},{6,4},{8,10},{10,8},{12,14},{14,12},{1,3},{3,1},... | collective-permute-start | bytes 393224 | tf_op jit(solution)/shard_map/ppermute | solution.py:349
  47.3 0.8 collective-permute-start.13
  48.1 1.5 %collective-permute-start.14 = (bf16[2,256,128]{2,1,0:T(8,128)(2,1)S(1)}, bf16[2,256,128]{2,1,0:T(8,128)(2,1)S(1)}, u32[]{:S(2)}, u32[]{:S(2)}) collective-permute-start(bf16[2,256,128]{2,1,0:T(8,128)(2,1)S(1)} %get-tuple-element.56), channel_id=1, source_target_pairs={{0,6},{2,4},{4,2},{6,0},{8,14},{10,12},{12,10},{14,8},{1,7},{3,5},... | collective-permute-start | bytes 393224 | tf_op jit(solution)/shard_map/ppermute | solution.py:349
  49.6 1.4 %collective-permute-done.19.refs_4_ = bf16[2,128,128]{2,1,0:T(8,128)(2,1)S(1)} collective-permute-done((bf16[2,128,128]{2,1,0:T(8,128)(2,1)S(1)}, bf16[2,128,128]{2,1,0:T(8,128)(2,1)S(1)}, u32[]{:S(2)}, u32[]{:S(2)}) %collective-permute-start.19) | collective-permute-done | bytes 65568 | tf_op jit(solution)/shard_map/ppermute | solution.py:349
  51.0 1.2 %collective-permute-start.21 = (bf16[2,128,128]{2,1,0:T(8,128)(2,1)S(1)}, bf16[2,128,128]{2,1,0:T(8,128)(2,1)S(1)}, u32[]{:S(2)}, u32[]{:S(2)}) collective-permute-start(bf16[2,128,128]{2,1,0:T(8,128)(2,1)S(1)} %get-tuple-element.63), channel_id=1, source_target_pairs={{0,12},{2,14},{4,8},{6,10},{8,4},{10,6},{12,0},{14,2},{1,13},{3,15... | collective-permute-start | bytes 196616 | tf_op jit(solution)/shard_map/ppermute | solution.py:349
  52.2 2.1 %collective-permute-start.22 = (bf16[2,128,128]{2,1,0:T(8,128)(2,1)S(1)}, bf16[2,128,128]{2,1,0:T(8,128)(2,1)S(1)}, u32[]{:S(2)}, u32[]{:S(2)}) collective-permute-start(bf16[2,128,128]{2,1,0:T(8,128)(2,1)S(1)} %get-tuple-element.64), channel_id=1, source_target_pairs={{0,14},{2,12},{4,10},{6,8},{8,6},{10,4},{12,2},{14,0},{1,15},{3,13... | collective-permute-start | bytes 196616 | tf_op jit(solution)/shard_map/ppermute | solution.py:349
  54.3 3.7 %collective-permute-done.21.refs_6_ = bf16[2,128,128]{2,1,0:T(8,128)(2,1)S(1)} collective-permute-done((bf16[2,128,128]{2,1,0:T(8,128)(2,1)S(1)}, bf16[2,128,128]{2,1,0:T(8,128)(2,1)S(1)}, u32[]{:S(2)}, u32[]{:S(2)}) %collective-permute-start.21) | collective-permute-done | bytes 65568 | tf_op jit(solution)/shard_map/ppermute | solution.py:349
  58.0 2.5 %collective-permute-done.22.refs_7_ = bf16[2,128,128]{2,1,0:T(8,128)(2,1)S(1)} collective-permute-done((bf16[2,128,128]{2,1,0:T(8,128)(2,1)S(1)}, bf16[2,128,128]{2,1,0:T(8,128)(2,1)S(1)}, u32[]{:S(2)}, u32[]{:S(2)}) %collective-permute-start.22) | collective-permute-done | bytes 65568 | tf_op jit(solution)/shard_map/ppermute | solution.py:349
  60.6 1.9 %collective-permute-start.16 = (bf16[2,128,128]{2,1,0:T(8,128)(2,1)S(1)}, bf16[2,128,128]{2,1,0:T(8,128)(2,1)S(1)}, u32[]{:S(2)}, u32[]{:S(2)}) collective-permute-start(bf16[2,128,128]{2,1,0:T(8,128)(2,1)S(1)} %get-tuple-element.58), channel_id=1, source_target_pairs={{0,10},{2,8},{4,14},{6,12},{8,2},{10,0},{12,6},{14,4},{1,11},{3,9}... | collective-permute-start | bytes 196616 | tf_op jit(solution)/shard_map/ppermute | solution.py:349
  62.5 0.7 collective-permute-start.17
  63.2 2.5 %collective-permute-start.18 = (bf16[2,128,128]{2,1,0:T(8,128)(2,1)S(1)}, bf16[2,128,128]{2,1,0:T(8,128)(2,1)S(1)}, u32[]{:S(2)}, u32[]{:S(2)}) collective-permute-start(bf16[2,128,128]{2,1,0:T(8,128)(2,1)S(1)} %get-tuple-element.60), channel_id=1, source_target_pairs={{0,14},{2,12},{4,10},{6,8},{8,6},{10,4},{12,2},{14,0},{1,15},{3,13... | collective-permute-start | bytes 196616 | tf_op jit(solution)/shard_map/ppermute | solution.py:349
  65.7 4.9 %inverse.2.refs_8_ = bf16[256,256,128]{2,1,0:T(8,128)(2,1)} custom-call(s32[2]{0:T(128)S(1)} %pad_add_fusion.me_ref.place_ref, bf16[2,4096,128]{2,1,0:T(8,128)(2,1)S(1)} %copy-done, bf16[2,256,128]{2,1,0:T(8,128)(2,1)S(1)} %get-tuple-element.53.refs_0_, bf16[2,256,128]{2,1,0:T(8,128)(2,1)S(1)} %collective-permute-done.12.refs_1_, ...), custom_call_target="tpu_custom_call" | custom-call | flops 2147483648 | bytes 8388608 | tf_op jit(solution)/shard_map/inverse/pallas_call | solution.py:323
  70.6 4.9 %inverse.3 = bf16[256,256,128]{2,1,0:T(8,128)(2,1)} custom-call(s32[2]{0:T(128)S(1)} %pad_add_fusion.me_ref.place_ref, bf16[2,4096,128]{2,1,0:T(8,128)(2,1)S(1)} %copy-done, bf16[2,256,128]{2,1,0:T(8,128)(2,1)S(1)} %get-tuple-element.53.refs_0_, bf16[2,256,128]{2,1,0:T(8,128)(2,1)S(1)} %collective-permute-done.12.refs_1_, ...), custom_call_target="tpu_custom_call", output_to_operand_aliasing={{}: (10, {})} | custom-call | flops 2147483648 | bytes 8388608 | tf_op jit(solution)/shard_map/inverse/pallas_call | solution.py:323
  (31 shorter events, 0.2 us)
Async XLA Ops:
  0.1 1.2 %copy-start.1 = (bf16[33,128,128]{2,1,0:T(8,128)(2,1)S(1)}, bf16[33,128,128]{2,1,0:T(8,128)(2,1)}, u32[]{:S(2)}) copy-start(bf16[33,128,128]{2,1,0:T(8,128)(2,1)} %constant.12.clone.table_hbm) | copy-start | bytes 3244036
  1.3 4.8 %copy-start.2 = (bf16[1,40,2,128,128]{4,3,2,1,0:T(8,128)(2,1)S(1)}, bf16[1,40,2,128,128]{4,3,2,1,0:T(8,128)(2,1)}, u32[]{:S(2)}) copy-start(bf16[1,40,2,128,128]{4,3,2,1,0:T(8,128)(2,1)} %param.9) | copy-start | bytes 7864324
  6.1 13.9 %collective-permute-start = (bf16[40,2,128,128]{3,2,1,0:T(8,128)(2,1)S(1)}, bf16[40,2,128,128]{3,2,1,0:T(8,128)(2,1)S(1)}, u32[]{:S(2)}, u32[]{:S(2)}) collective-permute-start(bf16[40,2,128,128]{3,2,1,0:T(8,128)(2,1)S(1)} %bitcast.3), channel_id=1, source_target_pairs={{0,1},{1,0},{2,3},{3,2},{4,5},{5,4},{6,7},{7,6},{8,9},{9,8},{10,11... | collective-permute-start | bytes 7864328 | tf_op jit(solution)/shard_map/ppermute | solution.py:375
  6.6 14.5 %collective-permute-start.4 = (bf16[2,128,128]{2,1,0:T(8,128)(2,1)S(1)}, bf16[2,128,128]{2,1,0:T(8,128)(2,1)S(1)}, u32[]{:S(2)}, u32[]{:S(2)}) collective-permute-start(bf16[2,128,128]{2,1,0:T(8,128)(2,1)S(1)} %get-tuple-element.45), channel_id=1, source_target_pairs={{0,8},{2,10},{4,12},{6,14},{8,0},{10,2},{12,4},{14,6},{1,9},{3,11}... | collective-permute-start | bytes 196616 | tf_op jit(solution)/shard_map/ppermute | solution.py:349
  10.3 14.0 %collective-permute-start.5 = (bf16[2,128,128]{2,1,0:T(8,128)(2,1)S(1)}, bf16[2,128,128]{2,1,0:T(8,128)(2,1)S(1)}, u32[]{:S(2)}, u32[]{:S(2)}) collective-permute-start(bf16[2,128,128]{2,1,0:T(8,128)(2,1)S(1)} %get-tuple-element.46), channel_id=1, source_target_pairs={{0,10},{2,8},{4,14},{6,12},{8,2},{10,0},{12,6},{14,4},{1,11},{3,9}... | collective-permute-start | bytes 196616 | tf_op jit(solution)/shard_map/ppermute | solution.py:349
  11.6 13.1 %collective-permute-start.6 = (bf16[2,128,128]{2,1,0:T(8,128)(2,1)S(1)}, bf16[2,128,128]{2,1,0:T(8,128)(2,1)S(1)}, u32[]{:S(2)}, u32[]{:S(2)}) collective-permute-start(bf16[2,128,128]{2,1,0:T(8,128)(2,1)S(1)} %get-tuple-element.47), channel_id=1, source_target_pairs={{0,12},{2,14},{4,8},{6,10},{8,4},{10,6},{12,0},{14,2},{1,13},{3,15... | collective-permute-start | bytes 196616 | tf_op jit(solution)/shard_map/ppermute | solution.py:349
  15.2 23.2 %copy-start.3 = (s32[1,16]{1,0:T(1,128)S(1)}, s32[1,16]{1,0:T(1,128)}, u32[]{:S(2)}) copy-start(s32[1,16]{1,0:T(1,128)} %count_ref.1) | copy-start | bytes 196
  15.2 23.2 %copy-start.4 = (s32[1,80]{1,0:T(1,128)S(1)}, s32[1,80]{1,0:T(1,128)}, u32[]{:S(2)}) copy-start(s32[1,80]{1,0:T(1,128)} %column_ref.1) | copy-start | bytes 964
  15.2 11.0 %collective-permute-start.7 = (bf16[2,128,128]{2,1,0:T(8,128)(2,1)S(1)}, bf16[2,128,128]{2,1,0:T(8,128)(2,1)S(1)}, u32[]{:S(2)}, u32[]{:S(2)}) collective-permute-start(bf16[2,128,128]{2,1,0:T(8,128)(2,1)S(1)} %get-tuple-element.48), channel_id=1, source_target_pairs={{0,14},{2,12},{4,10},{6,8},{8,6},{10,4},{12,2},{14,0},{1,15},{3,13... | collective-permute-start | bytes 196616 | tf_op jit(solution)/shard_map/ppermute | solution.py:349
  20.1 7.7 %collective-permute-start.8 = (bf16[2,128,128]{2,1,0:T(8,128)(2,1)S(1)}, bf16[2,128,128]{2,1,0:T(8,128)(2,1)S(1)}, u32[]{:S(2)}, u32[]{:S(2)}) collective-permute-start(bf16[2,128,128]{2,1,0:T(8,128)(2,1)S(1)} %get-tuple-element.49), channel_id=1, source_target_pairs={{0,8},{2,10},{4,12},{6,14},{8,0},{10,2},{12,4},{14,6},{1,9},{3,11}... | collective-permute-start | bytes 196616 | tf_op jit(solution)/shard_map/ppermute | solution.py:349
  21.2 10.3 %collective-permute-start.9 = (bf16[2,128,128]{2,1,0:T(8,128)(2,1)S(1)}, bf16[2,128,128]{2,1,0:T(8,128)(2,1)S(1)}, u32[]{:S(2)}, u32[]{:S(2)}) collective-permute-start(bf16[2,128,128]{2,1,0:T(8,128)(2,1)S(1)} %get-tuple-element.50), channel_id=1, source_target_pairs={{0,10},{2,8},{4,14},{6,12},{8,2},{10,0},{12,6},{14,4},{1,11},{3,9}... | collective-permute-start | bytes 196616 | tf_op jit(solution)/shard_map/ppermute | solution.py:349
  24.3 14.1 %collective-permute-start.1 = (bf16[2,256,128]{2,1,0:T(8,128)(2,1)S(1)}, bf16[2,256,128]{2,1,0:T(8,128)(2,1)S(1)}, u32[]{:S(2)}, u32[]{:S(2)}) collective-permute-start(bf16[2,256,128]{2,1,0:T(8,128)(2,1)S(1)} %get-tuple-element.42), channel_id=1, source_target_pairs={{0,2},{2,0},{4,6},{6,4},{8,10},{10,8},{12,14},{14,12},{1,3},{3,1},... | collective-permute-start | bytes 393224 | tf_op jit(solution)/shard_map/ppermute | solution.py:349
  24.6 13.7 %collective-permute-start.2 = (bf16[2,256,128]{2,1,0:T(8,128)(2,1)S(1)}, bf16[2,256,128]{2,1,0:T(8,128)(2,1)S(1)}, u32[]{:S(2)}, u32[]{:S(2)}) collective-permute-start(bf16[2,256,128]{2,1,0:T(8,128)(2,1)S(1)} %get-tuple-element.43), channel_id=1, source_target_pairs={{0,4},{2,6},{4,0},{6,2},{8,12},{10,14},{12,8},{14,10},{1,5},{3,7},... | collective-permute-start | bytes 393224 | tf_op jit(solution)/shard_map/ppermute | solution.py:349
  26.2 12.2 %collective-permute-start.3 = (bf16[2,256,128]{2,1,0:T(8,128)(2,1)S(1)}, bf16[2,256,128]{2,1,0:T(8,128)(2,1)S(1)}, u32[]{:S(2)}, u32[]{:S(2)}) collective-permute-start(bf16[2,256,128]{2,1,0:T(8,128)(2,1)S(1)} %get-tuple-element.44), channel_id=1, source_target_pairs={{0,6},{2,4},{4,2},{6,0},{8,14},{10,12},{12,10},{14,8},{1,7},{3,5},... | collective-permute-start | bytes 393224 | tf_op jit(solution)/shard_map/ppermute | solution.py:349
  27.8 8.4 %collective-permute-start.10 = (bf16[2,128,128]{2,1,0:T(8,128)(2,1)S(1)}, bf16[2,128,128]{2,1,0:T(8,128)(2,1)S(1)}, u32[]{:S(2)}, u32[]{:S(2)}) collective-permute-start(bf16[2,128,128]{2,1,0:T(8,128)(2,1)S(1)} %get-tuple-element.51), channel_id=1, source_target_pairs={{0,12},{2,14},{4,8},{6,10},{8,4},{10,6},{12,0},{14,2},{1,13},{3,15... | collective-permute-start | bytes 196616 | tf_op jit(solution)/shard_map/ppermute | solution.py:349
  31.4 7.0 %collective-permute-start.11 = (bf16[2,128,128]{2,1,0:T(8,128)(2,1)S(1)}, bf16[2,128,128]{2,1,0:T(8,128)(2,1)S(1)}, u32[]{:S(2)}, u32[]{:S(2)}) collective-permute-start(bf16[2,128,128]{2,1,0:T(8,128)(2,1)S(1)} %get-tuple-element.52), channel_id=1, source_target_pairs={{0,14},{2,12},{4,10},{6,8},{8,6},{10,4},{12,2},{14,0},{1,15},{3,13... | collective-permute-start | bytes 196616 | tf_op jit(solution)/shard_map/ppermute | solution.py:349
  38.4 27.3 %copy-start = (bf16[2,4096,128]{2,1,0:T(8,128)(2,1)S(1)}, bf16[2,4096,128]{2,1,0:T(8,128)(2,1)}, u32[]{:S(2)}) copy-start(bf16[2,4096,128]{2,1,0:T(8,128)(2,1)} %constant.13.clone.table_ref) | copy-start | bytes 6291460
  42.9 8.1 %collective-permute-start.19 = (bf16[2,128,128]{2,1,0:T(8,128)(2,1)S(1)}, bf16[2,128,128]{2,1,0:T(8,128)(2,1)S(1)}, u32[]{:S(2)}, u32[]{:S(2)}) collective-permute-start(bf16[2,128,128]{2,1,0:T(8,128)(2,1)S(1)} %get-tuple-element.61), channel_id=1, source_target_pairs={{0,8},{2,10},{4,12},{6,14},{8,0},{10,2},{12,4},{14,6},{1,9},{3,11}... | collective-permute-start | bytes 196616 | tf_op jit(solution)/shard_map/ppermute | solution.py:349
  42.9 9.2 %collective-permute-start.20 = (bf16[2,128,128]{2,1,0:T(8,128)(2,1)S(1)}, bf16[2,128,128]{2,1,0:T(8,128)(2,1)S(1)}, u32[]{:S(2)}, u32[]{:S(2)}) collective-permute-start(bf16[2,128,128]{2,1,0:T(8,128)(2,1)S(1)} %get-tuple-element.62), channel_id=1, source_target_pairs={{0,10},{2,8},{4,14},{6,12},{8,2},{10,0},{12,6},{14,4},{1,11},{3,9}... | collective-permute-start | bytes 196616 | tf_op jit(solution)/shard_map/ppermute | solution.py:349
  46.1 16.4 %collective-permute-start.12 = (bf16[2,256,128]{2,1,0:T(8,128)(2,1)S(1)}, bf16[2,256,128]{2,1,0:T(8,128)(2,1)S(1)}, u32[]{:S(2)}, u32[]{:S(2)}) collective-permute-start(bf16[2,256,128]{2,1,0:T(8,128)(2,1)S(1)} %get-tuple-element.54), channel_id=1, source_target_pairs={{0,2},{2,0},{4,6},{6,4},{8,10},{10,8},{12,14},{14,12},{1,3},{3,1},... | collective-permute-start | bytes 393224 | tf_op jit(solution)/shard_map/ppermute | solution.py:349
  47.3 15.8 %collective-permute-start.13 = (bf16[2,256,128]{2,1,0:T(8,128)(2,1)S(1)}, bf16[2,256,128]{2,1,0:T(8,128)(2,1)S(1)}, u32[]{:S(2)}, u32[]{:S(2)}) collective-permute-start(bf16[2,256,128]{2,1,0:T(8,128)(2,1)S(1)} %get-tuple-element.55), channel_id=1, source_target_pairs={{0,4},{2,6},{4,0},{6,2},{8,12},{10,14},{12,8},{14,10},{1,5},{3,7},... | collective-permute-start | bytes 393224 | tf_op jit(solution)/shard_map/ppermute | solution.py:349
  48.1 17.6 %collective-permute-start.14 = (bf16[2,256,128]{2,1,0:T(8,128)(2,1)S(1)}, bf16[2,256,128]{2,1,0:T(8,128)(2,1)S(1)}, u32[]{:S(2)}, u32[]{:S(2)}) collective-permute-start(bf16[2,256,128]{2,1,0:T(8,128)(2,1)S(1)} %get-tuple-element.56), channel_id=1, source_target_pairs={{0,6},{2,4},{4,2},{6,0},{8,14},{10,12},{12,10},{14,8},{1,7},{3,5},... | collective-permute-start | bytes 393224 | tf_op jit(solution)/shard_map/ppermute | solution.py:349
  51.0 7.0 %collective-permute-start.21 = (bf16[2,128,128]{2,1,0:T(8,128)(2,1)S(1)}, bf16[2,128,128]{2,1,0:T(8,128)(2,1)S(1)}, u32[]{:S(2)}, u32[]{:S(2)}) collective-permute-start(bf16[2,128,128]{2,1,0:T(8,128)(2,1)S(1)} %get-tuple-element.63), channel_id=1, source_target_pairs={{0,12},{2,14},{4,8},{6,10},{8,4},{10,6},{12,0},{14,2},{1,13},{3,15... | collective-permute-start | bytes 196616 | tf_op jit(solution)/shard_map/ppermute | solution.py:349
  52.2 8.4 %collective-permute-start.22 = (bf16[2,128,128]{2,1,0:T(8,128)(2,1)S(1)}, bf16[2,128,128]{2,1,0:T(8,128)(2,1)S(1)}, u32[]{:S(2)}, u32[]{:S(2)}) collective-permute-start(bf16[2,128,128]{2,1,0:T(8,128)(2,1)S(1)} %get-tuple-element.64), channel_id=1, source_target_pairs={{0,14},{2,12},{4,10},{6,8},{8,6},{10,4},{12,2},{14,0},{1,15},{3,13... | collective-permute-start | bytes 196616 | tf_op jit(solution)/shard_map/ppermute | solution.py:349
  58.0 12.5 %collective-permute-start.15 = (bf16[2,128,128]{2,1,0:T(8,128)(2,1)S(1)}, bf16[2,128,128]{2,1,0:T(8,128)(2,1)S(1)}, u32[]{:S(2)}, u32[]{:S(2)}) collective-permute-start(bf16[2,128,128]{2,1,0:T(8,128)(2,1)S(1)} %get-tuple-element.57), channel_id=1, source_target_pairs={{0,8},{2,10},{4,12},{6,14},{8,0},{10,2},{12,4},{14,6},{1,9},{3,11}... | collective-permute-start | bytes 196616 | tf_op jit(solution)/shard_map/ppermute | solution.py:349
  60.6 10.0 %collective-permute-start.16 = (bf16[2,128,128]{2,1,0:T(8,128)(2,1)S(1)}, bf16[2,128,128]{2,1,0:T(8,128)(2,1)S(1)}, u32[]{:S(2)}, u32[]{:S(2)}) collective-permute-start(bf16[2,128,128]{2,1,0:T(8,128)(2,1)S(1)} %get-tuple-element.58), channel_id=1, source_target_pairs={{0,10},{2,8},{4,14},{6,12},{8,2},{10,0},{12,6},{14,4},{1,11},{3,9}... | collective-permute-start | bytes 196616 | tf_op jit(solution)/shard_map/ppermute | solution.py:349
  62.5 8.1 %collective-permute-start.17 = (bf16[2,128,128]{2,1,0:T(8,128)(2,1)S(1)}, bf16[2,128,128]{2,1,0:T(8,128)(2,1)S(1)}, u32[]{:S(2)}, u32[]{:S(2)}) collective-permute-start(bf16[2,128,128]{2,1,0:T(8,128)(2,1)S(1)} %get-tuple-element.59), channel_id=1, source_target_pairs={{0,12},{2,14},{4,8},{6,10},{8,4},{10,6},{12,0},{14,2},{1,13},{3,15... | collective-permute-start | bytes 196616 | tf_op jit(solution)/shard_map/ppermute | solution.py:349
  63.2 7.4 %collective-permute-start.18 = (bf16[2,128,128]{2,1,0:T(8,128)(2,1)S(1)}, bf16[2,128,128]{2,1,0:T(8,128)(2,1)S(1)}, u32[]{:S(2)}, u32[]{:S(2)}) collective-permute-start(bf16[2,128,128]{2,1,0:T(8,128)(2,1)S(1)} %get-tuple-element.60), channel_id=1, source_target_pairs={{0,14},{2,12},{4,10},{6,8},{8,6},{10,4},{12,2},{14,0},{1,15},{3,13... | collective-permute-start | bytes 196616 | tf_op jit(solution)/shard_map/ppermute | solution.py:349

commit v7 on v5

--- a/solution.py
+++ b/solution.py
@@ -234,7 +234,7 @@
     _, rows, width = nears[0].shape
     far = len(fars) // len(chunks)
     total = (len(nears) + far) * rows
-    block = math.gcd(20, halves)
+    block = math.gcd(40, halves)
     shapes = [nears[0].shape] * len(nears) + [(2, chunks[0][1], width)] * far
     shapes += [(far, 2, part, width) for _, part in chunks[1:]]
     return pl.pallas_call(

time: 75.4 us -> 75.3 us (level)
  no operation moved by 1% of the time
where the time goes in v7:
time: 75.3 us; the launch traced here: 75.1 us
  starting transfers between devices  37.2 us (49%)
  Pallas kernels  23.8 us (32%)
  waiting for transfers between devices  12.7 us (17%)
  local copies, waits for them, and re-layouts  1.25 us (2%)
    ppermute x22, starting transfers between devices, send(): lax.ppermute(block, 'wide', [(i, i ^ k) for i in range(parties)])  36.7 us
    ppermute x22, waiting for transfers between devices, send(): lax.ppermute(block, 'wide', [(i, i ^ k) for i in range(parties)])  12.7 us
    pallas_call x2, Pallas kernels, forward(): pl.pallas_call(functools.partial(forward_kernel, first, step), in_specs=[...  9.79 us
    pallas_call x2, Pallas kernels, inverse(): pl.pallas_call(functools.partial(inverse_kernel, first, step, parties, le...  9.71 us
    pallas_call x1, Pallas kernels, apply_tiles(): pl.pallas_call(functools.partial(tiles_kernel, len(nears), chunks, block)...  4.23 us
  transfers between devices with their start and end apart: 23, of which 5 were waited for; matrix products, arithmetic and copies ran while one was open for 0% of the time, Pallas kernels for 20%

profile of v7, /device:TPU:0, one launch (start us, length us, event | category | flops | bytes accessed | tf_op | source)
XLA Modules:
  0.0 75.1 jit_solution(2550167738393550689)
XLA Ops:
  0.0 0.5 collective-permute-start
  0.5 0.1 pad_add_fusion.me_ref.place_ref
  0.5 1.2 %copy-done.1 = bf16[33,128,128]{2,1,0:T(8,128)(2,1)S(1)} copy-done((bf16[33,128,128]{2,1,0:T(8,128)(2,1)S(1)}, bf16[33,128,128]{2,1,0:T(8,128)(2,1)}, u32[]{:S(2)}) %copy-start.1) | copy-done | bytes 1081368
  1.8 4.7 %forward.2 = (bf16[4,2,128,128]{3,2,1,0:T(8,128)(2,1)S(1)}, bf16[2,128,128]{2,1,0:T(8,128)(2,1)S(1)}, bf16[2,128,128]{2,1,0:T(8,128)(2,1)S(1)}, bf16[2,128,128]{2,1,0:T(8,128)(2,1)S(1)}, bf16[2,128,128]{2,1,0:T(8,128)(2,1)S(1)}) custom-call(s32[2]{0:T(128)S(1)} %pad_add_fusion.me_ref.place_ref, bf16[33,128,128]{2,1,0:T(8,128)(2,1)S(1)} %copy-done.1, ...), custom_call_target="tpu_custom_call" | custom-call | flops 2147483648 | bytes 8388608 | tf_op jit(solution)/shard_map/forward/pallas_call | solution.py:135
  6.4 3.7 %collective-permute-start.4 = (bf16[2,128,128]{2,1,0:T(8,128)(2,1)S(1)}, bf16[2,128,128]{2,1,0:T(8,128)(2,1)S(1)}, u32[]{:S(2)}, u32[]{:S(2)}) collective-permute-start(bf16[2,128,128]{2,1,0:T(8,128)(2,1)S(1)} %get-tuple-element.42), channel_id=1, source_target_pairs={{0,8},{2,10},{4,12},{6,14},{8,0},{10,2},{12,4},{14,6},{1,9},{3,11}... | collective-permute-start | bytes 196616 | tf_op jit(solution)/shard_map/ppermute | solution.py:351
  10.1 1.3 %collective-permute-start.5 = (bf16[2,128,128]{2,1,0:T(8,128)(2,1)S(1)}, bf16[2,128,128]{2,1,0:T(8,128)(2,1)S(1)}, u32[]{:S(2)}, u32[]{:S(2)}) collective-permute-start(bf16[2,128,128]{2,1,0:T(8,128)(2,1)S(1)} %get-tuple-element.43), channel_id=1, source_target_pairs={{0,10},{2,8},{4,14},{6,12},{8,2},{10,0},{12,6},{14,4},{1,11},{3,9}... | collective-permute-start | bytes 196616 | tf_op jit(solution)/shard_map/ppermute | solution.py:351
  11.4 3.6 %collective-permute-start.6 = (bf16[2,128,128]{2,1,0:T(8,128)(2,1)S(1)}, bf16[2,128,128]{2,1,0:T(8,128)(2,1)S(1)}, u32[]{:S(2)}, u32[]{:S(2)}) collective-permute-start(bf16[2,128,128]{2,1,0:T(8,128)(2,1)S(1)} %get-tuple-element.44), channel_id=1, source_target_pairs={{0,12},{2,14},{4,8},{6,10},{8,4},{10,6},{12,0},{14,2},{1,13},{3,15... | collective-permute-start | bytes 196616 | tf_op jit(solution)/shard_map/ppermute | solution.py:351
  15.0 5.1 %forward.3 = (bf16[4,2,256,128]{3,2,1,0:T(8,128)(2,1)S(1)}, bf16[2,128,128]{2,1,0:T(8,128)(2,1)S(1)}, bf16[2,128,128]{2,1,0:T(8,128)(2,1)S(1)}, bf16[2,128,128]{2,1,0:T(8,128)(2,1)S(1)}, bf16[2,128,128]{2,1,0:T(8,128)(2,1)S(1)}) custom-call(s32[2]{0:T(128)S(1)} %pad_add_fusion.me_ref.place_ref, bf16[33,128,128]{2,1,0:T(8,128)(2,1)} %constant.12.clone.table_hbm, ...), custom_call_target="tpu_custom_call" | custom-call | flops 2147483648 | bytes 8388608 | tf_op jit(solution)/shard_map/forward/pallas_call | solution.py:135
  20.1 1.0 %collective-permute-start.8 = (bf16[2,128,128]{2,1,0:T(8,128)(2,1)S(1)}, bf16[2,128,128]{2,1,0:T(8,128)(2,1)S(1)}, u32[]{:S(2)}, u32[]{:S(2)}) collective-permute-start(bf16[2,128,128]{2,1,0:T(8,128)(2,1)S(1)} %get-tuple-element.46), channel_id=1, source_target_pairs={{0,8},{2,10},{4,12},{6,14},{8,0},{10,2},{12,4},{14,6},{1,9},{3,11}... | collective-permute-start | bytes 196616 | tf_op jit(solution)/shard_map/ppermute | solution.py:351
  21.2 3.1 %collective-permute-start.9 = (bf16[2,128,128]{2,1,0:T(8,128)(2,1)S(1)}, bf16[2,128,128]{2,1,0:T(8,128)(2,1)S(1)}, u32[]{:S(2)}, u32[]{:S(2)}) collective-permute-start(bf16[2,128,128]{2,1,0:T(8,128)(2,1)S(1)} %get-tuple-element.47), channel_id=1, source_target_pairs={{0,10},{2,8},{4,14},{6,12},{8,2},{10,0},{12,6},{14,4},{1,11},{3,9}... | collective-permute-start | bytes 196616 | tf_op jit(solution)/shard_map/ppermute | solution.py:351
  24.4 0.3 collective-permute-start.1
  24.7 1.6 %collective-permute-start.2 = (bf16[2,256,128]{2,1,0:T(8,128)(2,1)S(1)}, bf16[2,256,128]{2,1,0:T(8,128)(2,1)S(1)}, u32[]{:S(2)}, u32[]{:S(2)}) collective-permute-start(bf16[2,256,128]{2,1,0:T(8,128)(2,1)S(1)} %get-tuple-element.40), channel_id=1, source_target_pairs={{0,4},{2,6},{4,0},{6,2},{8,12},{10,14},{12,8},{14,10},{1,5},{3,7},... | collective-permute-start | bytes 393224 | tf_op jit(solution)/shard_map/ppermute | solution.py:351
  26.3 1.6 %collective-permute-start.3 = (bf16[2,256,128]{2,1,0:T(8,128)(2,1)S(1)}, bf16[2,256,128]{2,1,0:T(8,128)(2,1)S(1)}, u32[]{:S(2)}, u32[]{:S(2)}) collective-permute-start(bf16[2,256,128]{2,1,0:T(8,128)(2,1)S(1)} %get-tuple-element.41), channel_id=1, source_target_pairs={{0,6},{2,4},{4,2},{6,0},{8,14},{10,12},{12,10},{14,8},{1,7},{3,5},... | collective-permute-start | bytes 393224 | tf_op jit(solution)/shard_map/ppermute | solution.py:351
  27.9 3.6 %collective-permute-start.10 = (bf16[2,128,128]{2,1,0:T(8,128)(2,1)S(1)}, bf16[2,128,128]{2,1,0:T(8,128)(2,1)S(1)}, u32[]{:S(2)}, u32[]{:S(2)}) collective-permute-start(bf16[2,128,128]{2,1,0:T(8,128)(2,1)S(1)} %get-tuple-element.48), channel_id=1, source_target_pairs={{0,12},{2,14},{4,8},{6,10},{8,4},{10,6},{12,0},{14,2},{1,13},{3,15... | collective-permute-start | bytes 196616 | tf_op jit(solution)/shard_map/ppermute | solution.py:351
  31.5 1.4 %collective-permute-start.11 = (bf16[2,128,128]{2,1,0:T(8,128)(2,1)S(1)}, bf16[2,128,128]{2,1,0:T(8,128)(2,1)S(1)}, u32[]{:S(2)}, u32[]{:S(2)}) collective-permute-start(bf16[2,128,128]{2,1,0:T(8,128)(2,1)S(1)} %get-tuple-element.49), channel_id=1, source_target_pairs={{0,14},{2,12},{4,10},{6,8},{8,6},{10,4},{12,2},{14,0},{1,15},{3,13... | collective-permute-start | bytes 196616 | tf_op jit(solution)/shard_map/ppermute | solution.py:351
  32.9 3.8 %collective-permute-done.10.refs_10_ = bf16[2,128,128]{2,1,0:T(8,128)(2,1)S(1)} collective-permute-done((bf16[2,128,128]{2,1,0:T(8,128)(2,1)S(1)}, bf16[2,128,128]{2,1,0:T(8,128)(2,1)S(1)}, u32[]{:S(2)}, u32[]{:S(2)}) %collective-permute-start.10) | collective-permute-done | bytes 65568 | tf_op jit(solution)/shard_map/ppermute | solution.py:351
  36.7 1.7 %collective-permute-done.11.refs_11_ = bf16[2,128,128]{2,1,0:T(8,128)(2,1)S(1)} collective-permute-done((bf16[2,128,128]{2,1,0:T(8,128)(2,1)S(1)}, bf16[2,128,128]{2,1,0:T(8,128)(2,1)S(1)}, u32[]{:S(2)}, u32[]{:S(2)}) %collective-permute-start.11) | collective-permute-done | bytes 65568 | tf_op jit(solution)/shard_map/ppermute | solution.py:351
  38.5 4.2 %tiles.1 = (bf16[2,256,128]{2,1,0:T(8,128)(2,1)S(1)}, bf16[2,256,128]{2,1,0:T(8,128)(2,1)S(1)}, bf16[2,256,128]{2,1,0:T(8,128)(2,1)S(1)}, bf16[2,256,128]{2,1,0:...) custom-call(s32[1,16]{1,0:T(1,128)S(1)} %copy-done.3, ...), custom_call_target="tpu_custom_call" | custom-call | flops 1342177280 | bytes 5242880 | tf_op jit(solution)/shard_map/tiles/pallas_call | solution.py:240
  42.8 3.1 %collective-permute-start.20 = (bf16[2,128,128]{2,1,0:T(8,128)(2,1)S(1)}, bf16[2,128,128]{2,1,0:T(8,128)(2,1)S(1)}, u32[]{:S(2)}, u32[]{:S(2)}) collective-permute-start(bf16[2,128,128]{2,1,0:T(8,128)(2,1)S(1)} %get-tuple-element.60), channel_id=1, source_target_pairs={{0,10},{2,8},{4,14},{6,12},{8,2},{10,0},{12,6},{14,4},{1,11},{3,9}... | collective-permute-start | bytes 196616 | tf_op jit(solution)/shard_map/ppermute | solution.py:351
  45.9 1.3 %collective-permute-start.12 = (bf16[2,256,128]{2,1,0:T(8,128)(2,1)S(1)}, bf16[2,256,128]{2,1,0:T(8,128)(2,1)S(1)}, u32[]{:S(2)}, u32[]{:S(2)}) collective-permute-start(bf16[2,256,128]{2,1,0:T(8,128)(2,1)S(1)} %get-tuple-element.51), channel_id=1, source_target_pairs={{0,2},{2,0},{4,6},{6,4},{8,10},{10,8},{12,14},{14,12},{1,3},{3,1},... | collective-permute-start | bytes 393224 | tf_op jit(solution)/shard_map/ppermute | solution.py:351
  47.2 0.6 collective-permute-start.13
  47.7 1.7 %collective-permute-start.14 = (bf16[2,256,128]{2,1,0:T(8,128)(2,1)S(1)}, bf16[2,256,128]{2,1,0:T(8,128)(2,1)S(1)}, u32[]{:S(2)}, u32[]{:S(2)}) collective-permute-start(bf16[2,256,128]{2,1,0:T(8,128)(2,1)S(1)} %get-tuple-element.53), channel_id=1, source_target_pairs={{0,6},{2,4},{4,2},{6,0},{8,14},{10,12},{12,10},{14,8},{1,7},{3,5},... | collective-permute-start | bytes 393224 | tf_op jit(solution)/shard_map/ppermute | solution.py:351
  49.4 1.3 %collective-permute-done.19.refs_4_ = bf16[2,128,128]{2,1,0:T(8,128)(2,1)S(1)} collective-permute-done((bf16[2,128,128]{2,1,0:T(8,128)(2,1)S(1)}, bf16[2,128,128]{2,1,0:T(8,128)(2,1)S(1)}, u32[]{:S(2)}, u32[]{:S(2)}) %collective-permute-start.19) | collective-permute-done | bytes 65568 | tf_op jit(solution)/shard_map/ppermute | solution.py:351
  50.6 1.1 %collective-permute-start.21 = (bf16[2,128,128]{2,1,0:T(8,128)(2,1)S(1)}, bf16[2,128,128]{2,1,0:T(8,128)(2,1)S(1)}, u32[]{:S(2)}, u32[]{:S(2)}) collective-permute-start(bf16[2,128,128]{2,1,0:T(8,128)(2,1)S(1)} %get-tuple-element.61), channel_id=1, source_target_pairs={{0,12},{2,14},{4,8},{6,10},{8,4},{10,6},{12,0},{14,2},{1,13},{3,15... | collective-permute-start | bytes 196616 | tf_op jit(solution)/shard_map/ppermute | solution.py:351
  51.8 2.6 %collective-permute-start.22 = (bf16[2,128,128]{2,1,0:T(8,128)(2,1)S(1)}, bf16[2,128,128]{2,1,0:T(8,128)(2,1)S(1)}, u32[]{:S(2)}, u32[]{:S(2)}) collective-permute-start(bf16[2,128,128]{2,1,0:T(8,128)(2,1)S(1)} %get-tuple-element.62), channel_id=1, source_target_pairs={{0,14},{2,12},{4,10},{6,8},{8,6},{10,4},{12,2},{14,0},{1,15},{3,13... | collective-permute-start | bytes 196616 | tf_op jit(solution)/shard_map/ppermute | solution.py:351
  54.4 3.3 %collective-permute-done.21.refs_6_ = bf16[2,128,128]{2,1,0:T(8,128)(2,1)S(1)} collective-permute-done((bf16[2,128,128]{2,1,0:T(8,128)(2,1)S(1)}, bf16[2,128,128]{2,1,0:T(8,128)(2,1)S(1)}, u32[]{:S(2)}, u32[]{:S(2)}) %collective-permute-start.21) | collective-permute-done | bytes 65568 | tf_op jit(solution)/shard_map/ppermute | solution.py:351
  57.7 2.5 %collective-permute-done.22.refs_7_ = bf16[2,128,128]{2,1,0:T(8,128)(2,1)S(1)} collective-permute-done((bf16[2,128,128]{2,1,0:T(8,128)(2,1)S(1)}, bf16[2,128,128]{2,1,0:T(8,128)(2,1)S(1)}, u32[]{:S(2)}, u32[]{:S(2)}) %collective-permute-start.22) | collective-permute-done | bytes 65568 | tf_op jit(solution)/shard_map/ppermute | solution.py:351
  60.2 2.2 %collective-permute-start.16 = (bf16[2,128,128]{2,1,0:T(8,128)(2,1)S(1)}, bf16[2,128,128]{2,1,0:T(8,128)(2,1)S(1)}, u32[]{:S(2)}, u32[]{:S(2)}) collective-permute-start(bf16[2,128,128]{2,1,0:T(8,128)(2,1)S(1)} %get-tuple-element.56), channel_id=1, source_target_pairs={{0,10},{2,8},{4,14},{6,12},{8,2},{10,0},{12,6},{14,4},{1,11},{3,9}... | collective-permute-start | bytes 196616 | tf_op jit(solution)/shard_map/ppermute | solution.py:351
  62.4 0.4 collective-permute-start.17
  62.8 2.6 %collective-permute-start.18 = (bf16[2,128,128]{2,1,0:T(8,128)(2,1)S(1)}, bf16[2,128,128]{2,1,0:T(8,128)(2,1)S(1)}, u32[]{:S(2)}, u32[]{:S(2)}) collective-permute-start(bf16[2,128,128]{2,1,0:T(8,128)(2,1)S(1)} %get-tuple-element.58), channel_id=1, source_target_pairs={{0,14},{2,12},{4,10},{6,8},{8,6},{10,4},{12,2},{14,0},{1,15},{3,13... | collective-permute-start | bytes 196616 | tf_op jit(solution)/shard_map/ppermute | solution.py:351
  65.4 4.9 %inverse.2.refs_8_ = bf16[256,256,128]{2,1,0:T(8,128)(2,1)} custom-call(s32[2]{0:T(128)S(1)} %pad_add_fusion.me_ref.place_ref, bf16[2,4096,128]{2,1,0:T(8,128)(2,1)S(1)} %copy-done, bf16[2,256,128]{2,1,0:T(8,128)(2,1)S(1)} %get-tuple-element.50.refs_0_, bf16[2,256,128]{2,1,0:T(8,128)(2,1)S(1)} %collective-permute-done.12.refs_1_, ...), custom_call_target="tpu_custom_call" | custom-call | flops 2147483648 | bytes 8388608 | tf_op jit(solution)/shard_map/inverse/pallas_call | solution.py:325
  70.3 4.9 %inverse.3 = bf16[256,256,128]{2,1,0:T(8,128)(2,1)} custom-call(s32[2]{0:T(128)S(1)} %pad_add_fusion.me_ref.place_ref, bf16[2,4096,128]{2,1,0:T(8,128)(2,1)S(1)} %copy-done, bf16[2,256,128]{2,1,0:T(8,128)(2,1)S(1)} %get-tuple-element.50.refs_0_, bf16[2,256,128]{2,1,0:T(8,128)(2,1)S(1)} %collective-permute-done.12.refs_1_, ...), custom_call_target="tpu_custom_call", output_to_operand_aliasing={{}: (10, {})} | custom-call | flops 2147483648 | bytes 8388608 | tf_op jit(solution)/shard_map/inverse/pallas_call | solution.py:325
  (32 shorter events, 0.2 us)
Async XLA Ops:
  0.0 20.1 %collective-permute-start = (bf16[40,2,128,128]{3,2,1,0:T(8,128)(2,1)}, bf16[40,2,128,128]{3,2,1,0:T(8,128)(2,1)S(1)}, u32[]{:S(2)}, u32[]{:S(2)}) collective-permute-start(bf16[40,2,128,128]{3,2,1,0:T(8,128)(2,1)} %bitcast.3), channel_id=1, source_target_pairs={{0,1},{1,0},{2,3},{3,2},{4,5},{5,4},{6,7},{7,6},{8,9},{9,8},{10,11... | collective-permute-start | bytes 7864328 | tf_op jit(solution)/shard_map/ppermute | solution.py:375
  0.5 1.2 %copy-start.1 = (bf16[33,128,128]{2,1,0:T(8,128)(2,1)S(1)}, bf16[33,128,128]{2,1,0:T(8,128)(2,1)}, u32[]{:S(2)}) copy-start(bf16[33,128,128]{2,1,0:T(8,128)(2,1)} %constant.12.clone.table_hbm) | copy-start | bytes 3244036
  6.4 14.8 %collective-permute-start.4 = (bf16[2,128,128]{2,1,0:T(8,128)(2,1)S(1)}, bf16[2,128,128]{2,1,0:T(8,128)(2,1)S(1)}, u32[]{:S(2)}, u32[]{:S(2)}) collective-permute-start(bf16[2,128,128]{2,1,0:T(8,128)(2,1)S(1)} %get-tuple-element.42), channel_id=1, source_target_pairs={{0,8},{2,10},{4,12},{6,14},{8,0},{10,2},{12,4},{14,6},{1,9},{3,11}... | collective-permute-start | bytes 196616 | tf_op jit(solution)/shard_map/ppermute | solution.py:351
  10.1 14.3 %collective-permute-start.5 = (bf16[2,128,128]{2,1,0:T(8,128)(2,1)S(1)}, bf16[2,128,128]{2,1,0:T(8,128)(2,1)S(1)}, u32[]{:S(2)}, u32[]{:S(2)}) collective-permute-start(bf16[2,128,128]{2,1,0:T(8,128)(2,1)S(1)} %get-tuple-element.43), channel_id=1, source_target_pairs={{0,10},{2,8},{4,14},{6,12},{8,2},{10,0},{12,6},{14,4},{1,11},{3,9}... | collective-permute-start | bytes 196616 | tf_op jit(solution)/shard_map/ppermute | solution.py:351
  11.4 13.3 %collective-permute-start.6 = (bf16[2,128,128]{2,1,0:T(8,128)(2,1)S(1)}, bf16[2,128,128]{2,1,0:T(8,128)(2,1)S(1)}, u32[]{:S(2)}, u32[]{:S(2)}) collective-permute-start(bf16[2,128,128]{2,1,0:T(8,128)(2,1)S(1)} %get-tuple-element.44), channel_id=1, source_target_pairs={{0,12},{2,14},{4,8},{6,10},{8,4},{10,6},{12,0},{14,2},{1,13},{3,15... | collective-permute-start | bytes 196616 | tf_op jit(solution)/shard_map/ppermute | solution.py:351
  15.0 11.3 %collective-permute-start.7 = (bf16[2,128,128]{2,1,0:T(8,128)(2,1)S(1)}, bf16[2,128,128]{2,1,0:T(8,128)(2,1)S(1)}, u32[]{:S(2)}, u32[]{:S(2)}) collective-permute-start(bf16[2,128,128]{2,1,0:T(8,128)(2,1)S(1)} %get-tuple-element.45), channel_id=1, source_target_pairs={{0,14},{2,12},{4,10},{6,8},{8,6},{10,4},{12,2},{14,0},{1,15},{3,13... | collective-permute-start | bytes 196616 | tf_op jit(solution)/shard_map/ppermute | solution.py:351
  15.0 23.5 %copy-start.2 = (bf16[1,40,2,128,128]{4,3,2,1,0:T(8,128)(2,1)S(1)}, bf16[1,40,2,128,128]{4,3,2,1,0:T(8,128)(2,1)}, u32[]{:S(2)}) copy-start(bf16[1,40,2,128,128]{4,3,2,1,0:T(8,128)(2,1)} %param.9) | copy-start | bytes 7864324
  15.0 23.5 %copy-start.3 = (s32[1,16]{1,0:T(1,128)S(1)}, s32[1,16]{1,0:T(1,128)}, u32[]{:S(2)}) copy-start(s32[1,16]{1,0:T(1,128)} %count_ref.1) | copy-start | bytes 196
  15.0 23.5 %copy-start.4 = (s32[1,80]{1,0:T(1,128)S(1)}, s32[1,80]{1,0:T(1,128)}, u32[]{:S(2)}) copy-start(s32[1,80]{1,0:T(1,128)} %column_ref.1) | copy-start | bytes 964
  20.1 7.7 %collective-permute-start.8 = (bf16[2,128,128]{2,1,0:T(8,128)(2,1)S(1)}, bf16[2,128,128]{2,1,0:T(8,128)(2,1)S(1)}, u32[]{:S(2)}, u32[]{:S(2)}) collective-permute-start(bf16[2,128,128]{2,1,0:T(8,128)(2,1)S(1)} %get-tuple-element.46), channel_id=1, source_target_pairs={{0,8},{2,10},{4,12},{6,14},{8,0},{10,2},{12,4},{14,6},{1,9},{3,11}... | collective-permute-start | bytes 196616 | tf_op jit(solution)/shard_map/ppermute | solution.py:351
  21.2 10.2 %collective-permute-start.9 = (bf16[2,128,128]{2,1,0:T(8,128)(2,1)S(1)}, bf16[2,128,128]{2,1,0:T(8,128)(2,1)S(1)}, u32[]{:S(2)}, u32[]{:S(2)}) collective-permute-start(bf16[2,128,128]{2,1,0:T(8,128)(2,1)S(1)} %get-tuple-element.47), channel_id=1, source_target_pairs={{0,10},{2,8},{4,14},{6,12},{8,2},{10,0},{12,6},{14,4},{1,11},{3,9}... | collective-permute-start | bytes 196616 | tf_op jit(solution)/shard_map/ppermute | solution.py:351
  24.4 14.1 %collective-permute-start.1 = (bf16[2,256,128]{2,1,0:T(8,128)(2,1)S(1)}, bf16[2,256,128]{2,1,0:T(8,128)(2,1)S(1)}, u32[]{:S(2)}, u32[]{:S(2)}) collective-permute-start(bf16[2,256,128]{2,1,0:T(8,128)(2,1)S(1)} %get-tuple-element.39), channel_id=1, source_target_pairs={{0,2},{2,0},{4,6},{6,4},{8,10},{10,8},{12,14},{14,12},{1,3},{3,1},... | collective-permute-start | bytes 393224 | tf_op jit(solution)/shard_map/ppermute | solution.py:351
  24.7 13.7 %collective-permute-start.2 = (bf16[2,256,128]{2,1,0:T(8,128)(2,1)S(1)}, bf16[2,256,128]{2,1,0:T(8,128)(2,1)S(1)}, u32[]{:S(2)}, u32[]{:S(2)}) collective-permute-start(bf16[2,256,128]{2,1,0:T(8,128)(2,1)S(1)} %get-tuple-element.40), channel_id=1, source_target_pairs={{0,4},{2,6},{4,0},{6,2},{8,12},{10,14},{12,8},{14,10},{1,5},{3,7},... | collective-permute-start | bytes 393224 | tf_op jit(solution)/shard_map/ppermute | solution.py:351
  26.3 12.2 %collective-permute-start.3 = (bf16[2,256,128]{2,1,0:T(8,128)(2,1)S(1)}, bf16[2,256,128]{2,1,0:T(8,128)(2,1)S(1)}, u32[]{:S(2)}, u32[]{:S(2)}) collective-permute-start(bf16[2,256,128]{2,1,0:T(8,128)(2,1)S(1)} %get-tuple-element.41), channel_id=1, source_target_pairs={{0,6},{2,4},{4,2},{6,0},{8,14},{10,12},{12,10},{14,8},{1,7},{3,5},... | collective-permute-start | bytes 393224 | tf_op jit(solution)/shard_map/ppermute | solution.py:351
  27.9 8.8 %collective-permute-start.10 = (bf16[2,128,128]{2,1,0:T(8,128)(2,1)S(1)}, bf16[2,128,128]{2,1,0:T(8,128)(2,1)S(1)}, u32[]{:S(2)}, u32[]{:S(2)}) collective-permute-start(bf16[2,128,128]{2,1,0:T(8,128)(2,1)S(1)} %get-tuple-element.48), channel_id=1, source_target_pairs={{0,12},{2,14},{4,8},{6,10},{8,4},{10,6},{12,0},{14,2},{1,13},{3,15... | collective-permute-start | bytes 196616 | tf_op jit(solution)/shard_map/ppermute | solution.py:351
  31.5 7.0 %collective-permute-start.11 = (bf16[2,128,128]{2,1,0:T(8,128)(2,1)S(1)}, bf16[2,128,128]{2,1,0:T(8,128)(2,1)S(1)}, u32[]{:S(2)}, u32[]{:S(2)}) collective-permute-start(bf16[2,128,128]{2,1,0:T(8,128)(2,1)S(1)} %get-tuple-element.49), channel_id=1, source_target_pairs={{0,14},{2,12},{4,10},{6,8},{8,6},{10,4},{12,2},{14,0},{1,15},{3,13... | collective-permute-start | bytes 196616 | tf_op jit(solution)/shard_map/ppermute | solution.py:351
  38.5 26.9 %copy-start = (bf16[2,4096,128]{2,1,0:T(8,128)(2,1)S(1)}, bf16[2,4096,128]{2,1,0:T(8,128)(2,1)}, u32[]{:S(2)}) copy-start(bf16[2,4096,128]{2,1,0:T(8,128)(2,1)} %constant.13.clone.table_ref) | copy-start | bytes 6291460
  42.7 7.9 %collective-permute-start.19 = (bf16[2,128,128]{2,1,0:T(8,128)(2,1)S(1)}, bf16[2,128,128]{2,1,0:T(8,128)(2,1)S(1)}, u32[]{:S(2)}, u32[]{:S(2)}) collective-permute-start(bf16[2,128,128]{2,1,0:T(8,128)(2,1)S(1)} %get-tuple-element.59), channel_id=1, source_target_pairs={{0,8},{2,10},{4,12},{6,14},{8,0},{10,2},{12,4},{14,6},{1,9},{3,11}... | collective-permute-start | bytes 196616 | tf_op jit(solution)/shard_map/ppermute | solution.py:351
  42.8 9.0 %collective-permute-start.20 = (bf16[2,128,128]{2,1,0:T(8,128)(2,1)S(1)}, bf16[2,128,128]{2,1,0:T(8,128)(2,1)S(1)}, u32[]{:S(2)}, u32[]{:S(2)}) collective-permute-start(bf16[2,128,128]{2,1,0:T(8,128)(2,1)S(1)} %get-tuple-element.60), channel_id=1, source_target_pairs={{0,10},{2,8},{4,14},{6,12},{8,2},{10,0},{12,6},{14,4},{1,11},{3,9}... | collective-permute-start | bytes 196616 | tf_op jit(solution)/shard_map/ppermute | solution.py:351
  45.9 16.5 %collective-permute-start.12 = (bf16[2,256,128]{2,1,0:T(8,128)(2,1)S(1)}, bf16[2,256,128]{2,1,0:T(8,128)(2,1)S(1)}, u32[]{:S(2)}, u32[]{:S(2)}) collective-permute-start(bf16[2,256,128]{2,1,0:T(8,128)(2,1)S(1)} %get-tuple-element.51), channel_id=1, source_target_pairs={{0,2},{2,0},{4,6},{6,4},{8,10},{10,8},{12,14},{14,12},{1,3},{3,1},... | collective-permute-start | bytes 393224 | tf_op jit(solution)/shard_map/ppermute | solution.py:351
  47.2 15.6 %collective-permute-start.13 = (bf16[2,256,128]{2,1,0:T(8,128)(2,1)S(1)}, bf16[2,256,128]{2,1,0:T(8,128)(2,1)S(1)}, u32[]{:S(2)}, u32[]{:S(2)}) collective-permute-start(bf16[2,256,128]{2,1,0:T(8,128)(2,1)S(1)} %get-tuple-element.52), channel_id=1, source_target_pairs={{0,4},{2,6},{4,0},{6,2},{8,12},{10,14},{12,8},{14,10},{1,5},{3,7},... | collective-permute-start | bytes 393224 | tf_op jit(solution)/shard_map/ppermute | solution.py:351
  47.7 17.6 %collective-permute-start.14 = (bf16[2,256,128]{2,1,0:T(8,128)(2,1)S(1)}, bf16[2,256,128]{2,1,0:T(8,128)(2,1)S(1)}, u32[]{:S(2)}, u32[]{:S(2)}) collective-permute-start(bf16[2,256,128]{2,1,0:T(8,128)(2,1)S(1)} %get-tuple-element.53), channel_id=1, source_target_pairs={{0,6},{2,4},{4,2},{6,0},{8,14},{10,12},{12,10},{14,8},{1,7},{3,5},... | collective-permute-start | bytes 393224 | tf_op jit(solution)/shard_map/ppermute | solution.py:351
  50.6 7.1 %collective-permute-start.21 = (bf16[2,128,128]{2,1,0:T(8,128)(2,1)S(1)}, bf16[2,128,128]{2,1,0:T(8,128)(2,1)S(1)}, u32[]{:S(2)}, u32[]{:S(2)}) collective-permute-start(bf16[2,128,128]{2,1,0:T(8,128)(2,1)S(1)} %get-tuple-element.61), channel_id=1, source_target_pairs={{0,12},{2,14},{4,8},{6,10},{8,4},{10,6},{12,0},{14,2},{1,13},{3,15... | collective-permute-start | bytes 196616 | tf_op jit(solution)/shard_map/ppermute | solution.py:351
  51.8 8.4 %collective-permute-start.22 = (bf16[2,128,128]{2,1,0:T(8,128)(2,1)S(1)}, bf16[2,128,128]{2,1,0:T(8,128)(2,1)S(1)}, u32[]{:S(2)}, u32[]{:S(2)}) collective-permute-start(bf16[2,128,128]{2,1,0:T(8,128)(2,1)S(1)} %get-tuple-element.62), channel_id=1, source_target_pairs={{0,14},{2,12},{4,10},{6,8},{8,6},{10,4},{12,2},{14,0},{1,15},{3,13... | collective-permute-start | bytes 196616 | tf_op jit(solution)/shard_map/ppermute | solution.py:351
  57.7 12.5 %collective-permute-start.15 = (bf16[2,128,128]{2,1,0:T(8,128)(2,1)S(1)}, bf16[2,128,128]{2,1,0:T(8,128)(2,1)S(1)}, u32[]{:S(2)}, u32[]{:S(2)}) collective-permute-start(bf16[2,128,128]{2,1,0:T(8,128)(2,1)S(1)} %get-tuple-element.55), channel_id=1, source_target_pairs={{0,8},{2,10},{4,12},{6,14},{8,0},{10,2},{12,4},{14,6},{1,9},{3,11}... | collective-permute-start | bytes 196616 | tf_op jit(solution)/shard_map/ppermute | solution.py:351
  60.2 10.0 %collective-permute-start.16 = (bf16[2,128,128]{2,1,0:T(8,128)(2,1)S(1)}, bf16[2,128,128]{2,1,0:T(8,128)(2,1)S(1)}, u32[]{:S(2)}, u32[]{:S(2)}) collective-permute-start(bf16[2,128,128]{2,1,0:T(8,128)(2,1)S(1)} %get-tuple-element.56), channel_id=1, source_target_pairs={{0,10},{2,8},{4,14},{6,12},{8,2},{10,0},{12,6},{14,4},{1,11},{3,9}... | collective-permute-start | bytes 196616 | tf_op jit(solution)/shard_map/ppermute | solution.py:351
  62.4 7.8 %collective-permute-start.17 = (bf16[2,128,128]{2,1,0:T(8,128)(2,1)S(1)}, bf16[2,128,128]{2,1,0:T(8,128)(2,1)S(1)}, u32[]{:S(2)}, u32[]{:S(2)}) collective-permute-start(bf16[2,128,128]{2,1,0:T(8,128)(2,1)S(1)} %get-tuple-element.57), channel_id=1, source_target_pairs={{0,12},{2,14},{4,8},{6,10},{8,4},{10,6},{12,0},{14,2},{1,13},{3,15... | collective-permute-start | bytes 196616 | tf_op jit(solution)/shard_map/ppermute | solution.py:351
  62.8 7.5 %collective-permute-start.18 = (bf16[2,128,128]{2,1,0:T(8,128)(2,1)S(1)}, bf16[2,128,128]{2,1,0:T(8,128)(2,1)S(1)}, u32[]{:S(2)}, u32[]{:S(2)}) collective-permute-start(bf16[2,128,128]{2,1,0:T(8,128)(2,1)S(1)} %get-tuple-element.58), channel_id=1, source_target_pairs={{0,14},{2,12},{4,10},{6,8},{8,6},{10,4},{12,2},{14,0},{1,15},{3,13... | collective-permute-start | bytes 196616 | tf_op jit(solution)/shard_map/ppermute | solution.py:351
